TPU v7x, 32 devices: a whole 2x2x4 slice. The times are simulated.
32 devices in a mesh: section: 2 (over y), shard: 4 (over z), rep: 4 (over x, core).
Axes of the slice: x: 2, y: 2, z: 4, core: 2. Of those that a mesh axis runs over, the one named last changes fastest.
Arguments:
- boundary: bfloat16 [2, 4096, 2048], P('section', ('shard', 'rep')), may hold values from -6 to 6
- lengths: int32 [32, 4], P(('shard', 'rep')), may hold values from 1 to 64, 128 in all within a row
- deal_order: int32 [32], P(('shard', 'rep')), may hold values from 0 to 31, as said below
- w_query: bfloat16 [2, 2048, 2048], P('section', 'shard'), may hold values from -0.125 to 0.125
- w_forget: bfloat16 [2, 2048, 2048], P('section', 'shard'), may hold values from -0.125 to 0.125
- w_input: bfloat16 [2, 2048, 2048], P('section', 'shard'), may hold values from -0.125 to 0.125
- w_out: bfloat16 [2, 2048, 2048], P('section', 'shard'), may hold values from -0.125 to 0.125
- w_gate: bfloat16 [2, 2048, 5632], P('section', 'shard'), may hold values from -0.125 to 0.125
- w_up: bfloat16 [2, 2048, 5632], P('section', 'shard'), may hold values from -0.125 to 0.125
- w_down: bfloat16 [2, 5632, 2048], P('section', 'shard'), may hold values from -0.078125 to 0.078125
- norm_mix: bfloat16 [2, 2048], P('section', 'shard'), may hold values from 0.5 to 1.5
- norm_head: bfloat16 [2, 2048], P('section', 'shard'), may hold values from 0.5 to 1.5
- norm_ffn: bfloat16 [2, 2048], P('section', 'shard'), may hold values from 0.5 to 1.5
- gate_gap: bfloat16 [2, 2048], P('section', 'shard'), may hold values from 0.0099487305 to 0.29882812
Outputs:
- boundary_out: bfloat16 [2, 4096, 2048], P('section', ('shard', 'rep'))
- grad_query: float32 [2, 2048, 2048], P('section', 'shard')
- grad_forget: float32 [2, 2048, 2048], P('section', 'shard')
- grad_input: float32 [2, 2048, 2048], P('section', 'shard')
- grad_out: float32 [2, 2048, 2048], P('section', 'shard')
- grad_gate: float32 [2, 2048, 5632], P('section', 'shard')
- grad_up: float32 [2, 2048, 5632], P('section', 'shard')
- grad_down: float32 [2, 5632, 2048], P('section', 'shard')
- mixer_norm_gradient: float32 [2, 2048], P('section', 'shard')
- grad_norm_head: float32 [2, 2048], P('section', 'shard')
- grad_norm_ffn: float32 [2, 2048], P('section', 'shard')
- grad_gate_gap: float32 [2, 2048], P('section', 'shard')
Inputs may be any that keep to these rules, and one draw needn't show every extreme that they name: `lengths`: each row's entries sum to 128; the last entry is the padding at the row's end; in each row some entry equals 64. `deal_order`: each aligned block of 8 entries is a permutation of that block's own row numbers.
All inputs are finite; a program needn't handle non-finite values.
Results may differ from a plain program's by a relative error of at most 0.024.
Values may be sent and summed in bfloat16 or wider, within the bound.
No kernel may reach another device: no remote copies, remote signals or barrier semaphores. Data moves between devices by JAX's collectives and lax.ppermute only.
A program may use at most 576 MiB of HBM per device.

v0:
```python
import math

import jax
import jax.numpy as jnp
from jax import lax
from jax.sharding import PartitionSpec as P

HEADS = 16


EPS = 1e-06
HEAD_EPS = 0.1
TOP_PRECISION = lax.Precision.HIGHEST


def from_behind(block, axis, distance):
    devices = range(lax.axis_size(axis))
    route = [(i - distance, i) for i in devices if i - distance in devices]
    return lax.ppermute(block, axis, route)


def rms_norm(value, gain):
    return value * lax.rsqrt(jnp.mean(value * value, axis=-1, keepdims=True) + EPS) * gain


def head_norm(value, gain):
    return value * lax.rsqrt(jnp.mean(value * value, axis=-1, keepdims=True) + HEAD_EPS) * gain


def product(left, right):
    return jnp.dot(left, right, preferred_element_type=jnp.float32)


def product_t(left, right):
    return lax.dot_general(
        left, right, (((left.ndim - 1,), (1,)), ((), ())), preferred_element_type=jnp.float32
    )


def segment_info(lens_row, length):
    seg_ends = jnp.cumsum(lens_row)
    position = jnp.arange(length)
    segment_ids = jnp.sum((position[:, None] >= seg_ends[None, :]).astype(jnp.int32), axis=1)
    valid_mask = (position < length - lens_row[-1]).astype(jnp.float32)
    return (segment_ids, valid_mask)


def block_recur(query_vector, k, g, v, segment_ids):
    row_count, length, model_width = query_vector.shape
    head_size = model_width // HEADS
    block = math.gcd(length, 64)
    block_count = length // block

    def to_blocks(value):
        return jnp.moveaxis(value.reshape(row_count, block_count, block, HEADS, head_size), 1, 0)

    query_blocks, key_blocks, gate_blocks, value_blocks = (
        to_blocks(query_vector),
        to_blocks(k),
        to_blocks(g),
        to_blocks(v),
    )
    segment_rows = segment_ids.reshape(row_count, block_count, block)
    segment_blocks = jnp.moveaxis(segment_rows, 1, 0)
    prior_segment = jnp.concatenate(
        [jnp.full((row_count, 1), -1, jnp.int32), segment_rows[:, :-1, -1]], axis=1
    )
    prior_segment = jnp.moveaxis(prior_segment, 1, 0)
    causal = jnp.tril(jnp.ones((block, block), jnp.float32))

    def advance(relayed_state, block_items):
        query_blk, key_blk, gate_blk, value_blk, segment_blk, prior_blk = block_items
        decay = jnp.cumsum(jnp.log(gate_blk), axis=1)
        query_decayed = query_blk * jnp.exp(decay)
        key_decayed = key_blk * jnp.exp(-decay)
        same_segment = (segment_blk[:, :, None] == segment_blk[:, None, :]).astype(
            jnp.float32
        ) * causal
        scores = (
            jnp.einsum("rthk,rshk->rhts", query_decayed, key_decayed, precision=TOP_PRECISION)
            * same_segment[:, None]
        )
        within = jnp.einsum("rhts,rshv->rthv", scores, value_blk, precision=TOP_PRECISION)
        carried = (segment_blk == prior_blk[:, None]).astype(jnp.float32)
        within = within + carried[:, :, None, None] * jnp.einsum(
            "rthk,rhkv->rthv", query_decayed, relayed_state, precision=TOP_PRECISION
        )
        end_decay = decay[:, -1]
        tail_mask = (segment_blk == segment_blk[:, -1:]).astype(jnp.float32)
        keys_end = key_blk * jnp.exp(end_decay[:, None] - decay) * tail_mask[:, :, None, None]
        added_state = jnp.einsum("rshk,rshv->rhkv", keys_end, value_blk, precision=TOP_PRECISION)
        continues = carried[:, -1]
        relayed_state = (
            continues[:, None, None, None] * jnp.exp(end_decay)[..., None] * relayed_state
            + added_state
        )
        return (relayed_state, within)

    start_state = jnp.zeros((row_count, HEADS, head_size, head_size), jnp.float32)
    _, outputs = lax.scan(
        advance,
        start_state,
        (query_blocks, key_blocks, gate_blocks, value_blocks, segment_blocks, prior_segment),
    )
    return jnp.moveaxis(outputs, 0, 1).reshape(row_count, length, model_width)


def mixer(query_vector, f, v, gap, gain_head, valid_mask, segment_ids):
    closed = jax.nn.sigmoid(-f) * gap
    k = closed * valid_mask[..., None]
    o = block_recur(query_vector, k, 1.0 - closed, v, segment_ids)
    row_count, length, model_width = o.shape
    head_view = o.reshape(row_count, length, HEADS, model_width // HEADS)
    return head_norm(head_view, gain_head.reshape(HEADS, model_width // HEADS)).reshape(
        row_count, length, model_width
    )


def forward_layer(x, gathered, valid_mask, segment_ids):
    (
        weight_query,
        weight_forget,
        weight_input,
        weight_out,
        weight_gate,
        weight_up,
        weight_down,
        gain_mix,
        gain_head,
        gain_ffn,
        gap,
    ) = gathered
    norm_value, pull_in = jax.vjp(rms_norm, x, gain_mix.astype(jnp.float32))
    normed_in = norm_value.astype(jnp.bfloat16)
    query_vector = product(normed_in, weight_query)
    f = product(normed_in, weight_forget)
    v = product(normed_in, weight_input)
    mixed_norm, pull_mix = jax.vjp(
        lambda a, b, c, d, e: mixer(a, b, c, d, e, valid_mask, segment_ids),
        query_vector,
        f,
        v,
        gap.astype(jnp.float32),
        gain_head.astype(jnp.float32),
    )
    mixed = mixed_norm.astype(jnp.bfloat16)
    resid_mid = x + product(mixed, weight_out)
    mid_value, pull_mid = jax.vjp(rms_norm, resid_mid, gain_ffn.astype(jnp.float32))
    normed_mid = mid_value.astype(jnp.bfloat16)
    gate_value = product(normed_mid, weight_gate)
    up_value = product(normed_mid, weight_up)
    hidden_value, pull_act = jax.vjp(lambda a, b: jax.nn.silu(a) * b, gate_value, up_value)
    hidden = hidden_value.astype(jnp.bfloat16)
    result = (resid_mid + product(hidden, weight_down)) * valid_mask[..., None]
    return (result, (normed_in, mixed, normed_mid, hidden, pull_in, pull_mix, pull_mid, pull_act))


def backward_layer(grad_out, gathered, valid_mask, kept_state):
    weight_query, weight_forget, weight_input, weight_out, weight_gate, weight_up, weight_down = (
        gathered[:7]
    )
    normed_in, mixed, normed_mid, hidden, pull_in, pull_mix, pull_mid, pull_act = kept_state
    grad_mid = grad_out * valid_mask[..., None]
    grad_down = grad_mid.astype(jnp.bfloat16)
    grad_hidden = product_t(grad_down, weight_down)
    grad_gate_value, grad_up_value = pull_act(grad_hidden)
    grad_gate = grad_gate_value.astype(jnp.bfloat16)
    grad_up = grad_up_value.astype(jnp.bfloat16)
    grad_normed_mid = product_t(grad_gate, weight_gate) + product_t(grad_up, weight_up)
    more_mid, grad_gain_ffn = pull_mid(grad_normed_mid)
    grad_mid = grad_mid + more_mid
    grad_attn = grad_mid.astype(jnp.bfloat16)
    grad_mixed = product_t(grad_attn, weight_out)
    grad_q_value, grad_f_value, grad_v_value, grad_gap, grad_gain_head = pull_mix(grad_mixed)
    grad_q = grad_q_value.astype(jnp.bfloat16)
    grad_f = grad_f_value.astype(jnp.bfloat16)
    grad_v = grad_v_value.astype(jnp.bfloat16)
    grad_normed_in = (
        product_t(grad_q, weight_query)
        + product_t(grad_f, weight_forget)
        + product_t(grad_v, weight_input)
    )
    more_in, grad_gain_mix = pull_in(grad_normed_in)
    grad_in = grad_mid + more_in
    weight_pairs = (
        (normed_in, grad_q),
        (normed_in, grad_f),
        (normed_in, grad_v),
        (mixed, grad_attn),
        (normed_mid, grad_gate),
        (normed_mid, grad_up),
        (hidden, grad_down),
    )
    return (grad_in, weight_pairs, (grad_gain_mix, grad_gain_head, grad_gain_ffn, grad_gap))


def weight_term(act_rows, grad_rows):
    return lax.dot_general(
        act_rows, grad_rows, (((0,), (0,)), ((), ())), preferred_element_type=jnp.float32
    )


def joint_owner(act_rows, grad_rows):
    return lax.psum_scatter(
        weight_term(act_rows, grad_rows), ("shard", "rep"), scatter_dimension=0, tiled=True
    )


def local(
    boundary,
    lengths,
    deal_order,
    w_query,
    w_forget,
    w_input,
    w_out,
    w_gate,
    w_up,
    w_down,
    norm_mix,
    norm_head,
    norm_ffn,
    gate_gap,
):
    micro_count = deal_order.shape[0]
    model_width = boundary.shape[2]
    length = boundary.shape[1] // micro_count
    block_rows = micro_count * lax.axis_size("rep")
    on_first = lax.axis_index("section") == 0
    block_order, block_lengths = (
        lax.all_gather(deal_order, "rep", axis=0, tiled=True),
        lax.all_gather(lengths, "rep", axis=0, tiled=True),
    )
    block_local = block_order % block_rows
    local_order = deal_order % block_rows
    dealt_lengths = block_lengths[local_order]
    segment_ids, valid_mask = jax.vmap(lambda lens_row: segment_info(lens_row, length))(
        dealt_lengths
    )
    arrival = boundary[0].reshape(micro_count, length, model_width)
    block_arrival = lax.all_gather(arrival, "rep", axis=0, tiled=True)
    dealt = block_arrival[local_order]
    cotangent = boundary[1].reshape(micro_count, length, model_width)
    gathered = (
        lax.all_gather(w_query[0], "shard", axis=0, tiled=True),
        lax.all_gather(w_forget[0], "shard", axis=0, tiled=True),
        lax.all_gather(w_input[0], "shard", axis=0, tiled=True),
        lax.all_gather(w_out[0], "shard", axis=0, tiled=True),
        lax.all_gather(w_gate[0], "shard", axis=0, tiled=True),
        lax.all_gather(w_up[0], "shard", axis=0, tiled=True),
        lax.all_gather(w_down[0], "shard", axis=0, tiled=True),
        lax.all_gather(norm_mix[0], "shard", axis=0, tiled=True),
        lax.all_gather(norm_head[0], "shard", axis=0, tiled=True),
        lax.all_gather(norm_ffn[0], "shard", axis=0, tiled=True),
        lax.all_gather(gate_gap[0], "shard", axis=0, tiled=True),
    )
    blank_rows = jnp.zeros((1, length, model_width), jnp.bfloat16)
    incoming = blank_rows
    retained_steps = []
    sent_rows = []
    for tick_index in range(micro_count + 1):
        own_rows = dealt[tick_index : tick_index + 1] if tick_index < micro_count else blank_rows
        layer_in = jnp.where(on_first, own_rows, incoming)
        batch_index = jnp.where(
            on_first, min(tick_index, micro_count - 1), max(tick_index - 1, 0)
        ).astype(jnp.int32)
        row_mask = lax.dynamic_slice_in_dim(valid_mask, batch_index, 1, 0)
        row_segments = lax.dynamic_slice_in_dim(segment_ids, batch_index, 1, 0)
        result, kept_state = forward_layer(
            layer_in.astype(jnp.float32), gathered, row_mask, row_segments
        )
        retained_steps.append((kept_state, row_mask))
        rounded = result.astype(jnp.bfloat16)
        sent_rows.append(rounded)
        if tick_index < micro_count:
            incoming = from_behind(rounded, "section", 1)
    incoming_grad = blank_rows
    tick_terms = []
    small_sums = (jnp.zeros((model_width,), jnp.float32),) * 4
    input_grads = []
    for back_index in range(micro_count + 1):
        kept_state, row_mask = retained_steps[micro_count - back_index]
        own_rows = (
            cotangent[micro_count - 1 - back_index : micro_count - back_index]
            if back_index < micro_count
            else blank_rows
        )
        grad_out = jnp.where(on_first, incoming_grad, own_rows).astype(jnp.float32)
        grad_in, weight_pairs, small_terms = backward_layer(
            grad_out, gathered, row_mask, kept_state
        )
        tick_terms.append(weight_pairs)
        small_sums = tuple(
            (running + extra_summand for running, extra_summand in zip(small_sums, small_terms))
        )
        rounded_grad = grad_in.astype(jnp.bfloat16)
        input_grads.append(rounded_grad)
        if back_index < micro_count:
            incoming_grad = from_behind(rounded_grad, "section", -1)
    first_rows = jnp.concatenate([input_grads[micro_count - j] for j in range(micro_count)], axis=0)
    block_grads = lax.all_gather(first_rows, "rep", axis=0, tiled=True)
    inverse_order = jnp.argsort(block_local)
    own_inverse = lax.dynamic_slice_in_dim(
        inverse_order, lax.axis_index("rep") * micro_count, micro_count, 0
    )
    result_values = block_grads[own_inverse]
    second_rows = jnp.concatenate(sent_rows[1:], axis=0)
    boundary_out = jnp.where(on_first, result_values, second_rows).reshape(
        1, micro_count * length, model_width
    )
    pair_rows = []
    for pair_index in range(7):
        sides = []
        for side_index in range(2):
            picked = [
                jnp.where(
                    on_first,
                    tick_terms[micro_count - j][pair_index][side_index],
                    tick_terms[micro_count - 1 - j][pair_index][side_index],
                )
                for j in range(micro_count)
            ]
            stacked = jnp.concatenate(picked, axis=0)
            sides.append(stacked.reshape(-1, stacked.shape[-1]))
        pair_rows.append(sides)
    owned_grads = [joint_owner(act_rows, grad_rows) for act_rows, grad_rows in pair_rows]
    small_owned = (
        lax.psum_scatter(small_sums[0], ("shard", "rep"), scatter_dimension=0, tiled=True),
        lax.psum_scatter(small_sums[1], ("shard", "rep"), scatter_dimension=0, tiled=True),
        lax.psum_scatter(small_sums[2], ("shard", "rep"), scatter_dimension=0, tiled=True),
        lax.psum_scatter(small_sums[3], ("shard", "rep"), scatter_dimension=0, tiled=True),
    )
    totals = (
        lax.all_gather(owned_grads[0].astype(jnp.bfloat16), "rep", axis=0, tiled=True).astype(
            jnp.float32
        ),
        lax.all_gather(owned_grads[1].astype(jnp.bfloat16), "rep", axis=0, tiled=True).astype(
            jnp.float32
        ),
        lax.all_gather(owned_grads[2].astype(jnp.bfloat16), "rep", axis=0, tiled=True).astype(
            jnp.float32
        ),
        lax.all_gather(owned_grads[3].astype(jnp.bfloat16), "rep", axis=0, tiled=True).astype(
            jnp.float32
        ),
        lax.all_gather(owned_grads[4].astype(jnp.bfloat16), "rep", axis=0, tiled=True).astype(
            jnp.float32
        ),
        lax.all_gather(owned_grads[5].astype(jnp.bfloat16), "rep", axis=0, tiled=True).astype(
            jnp.float32
        ),
        lax.all_gather(owned_grads[6].astype(jnp.bfloat16), "rep", axis=0, tiled=True).astype(
            jnp.float32
        ),
        lax.all_gather(small_owned[0].astype(jnp.bfloat16), "rep", axis=0, tiled=True).astype(
            jnp.float32
        ),
        lax.all_gather(small_owned[1].astype(jnp.bfloat16), "rep", axis=0, tiled=True).astype(
            jnp.float32
        ),
        lax.all_gather(small_owned[2].astype(jnp.bfloat16), "rep", axis=0, tiled=True).astype(
            jnp.float32
        ),
        lax.all_gather(small_owned[3].astype(jnp.bfloat16), "rep", axis=0, tiled=True).astype(
            jnp.float32
        ),
    )
    return (
        boundary_out,
        totals[0][None],
        totals[1][None],
        totals[2][None],
        totals[3][None],
        totals[4][None],
        totals[5][None],
        totals[6][None],
        totals[7][None],
        totals[8][None],
        totals[9][None],
        totals[10][None],
    )


def solution(mesh):
    placed = (
        P("section", ("shard", "rep"), None),
        P(("shard", "rep"), None),
        P(("shard", "rep")),
        P("section", "shard", None),
        P("section", "shard", None),
        P("section", "shard", None),
        P("section", "shard", None),
        P("section", "shard", None),
        P("section", "shard", None),
        P("section", "shard", None),
        P("section", "shard"),
        P("section", "shard"),
        P("section", "shard"),
        P("section", "shard"),
    )
    return jax.shard_map(
        local,
        mesh=mesh,
        in_specs=placed,
        out_specs=(
            P("section", ("shard", "rep"), None),
            P("section", "shard", None),
            P("section", "shard", None),
            P("section", "shard", None),
            P("section", "shard", None),
            P("section", "shard", None),
            P("section", "shard", None),
            P("section", "shard", None),
            P("section", "shard"),
            P("section", "shard"),
            P("section", "shard"),
            P("section", "shard"),
        ),
        check_vma=False,
    )
```

profile of v0, /device:TPU:0, one launch (start us, length us, event | category | flops | bytes accessed | tf_op | source)
XLA Modules:
  0.0 4804.7 jit_solution(14554825224256532740)
XLA Ops:
  56.8 15.6 all-gather.8
  77.3 120.8 %all-gather.53.cloned.1.call-done = bf16[1,2048,2048]{2,1,0:T(8,128)(2,1)} async-done(((bf16[1,512,2048]{2,1,0:T(8,128)(2,1)}), bf16[1,2048,2048]{2,1,0:T(8,128)(2,1)}) %all-gather.53.cloned.1.call-update) | async-done | bytes 8388624 | tf_op jit(solution)/shard_map/all_gather | solution.py:246
  204.4 143.1 %all-gather.55.cloned.1.call-done = bf16[1,2048,2048]{2,1,0:T(8,128)(2,1)} async-done(((bf16[1,512,2048]{2,1,0:T(8,128)(2,1)}), bf16[1,2048,2048]{2,1,0:T(8,128)(2,1)}) %all-gather.55.cloned.1.call-update) | async-done | bytes 8388624 | tf_op jit(solution)/shard_map/all_gather | solution.py:247
  360.1 136.7 %all-gather.57.cloned.1.call-done = bf16[1,2048,2048]{2,1,0:T(8,128)(2,1)} async-done(((bf16[1,512,2048]{2,1,0:T(8,128)(2,1)}), bf16[1,2048,2048]{2,1,0:T(8,128)(2,1)}) %all-gather.57.cloned.1.call-update) | async-done | bytes 8388624 | tf_op jit(solution)/shard_map/all_gather | solution.py:245
  530.1 34.9 while.198
  570.9 75.3 %all-gather.59.cloned.1.call-done = bf16[1,2048,2048]{2,1,0:T(8,128)(2,1)} async-done(((bf16[1,512,2048]{2,1,0:T(8,128)(2,1)}), bf16[1,2048,2048]{2,1,0:T(8,128)(2,1)}) %all-gather.59.cloned.1.call-update) | async-done | bytes 8388624 | tf_op jit(solution)/shard_map/all_gather | solution.py:248
  653.1 383.9 %all-gather.61.cloned.1.call-done = bf16[1,2048,5632]{2,1,0:T(8,128)(2,1)} async-done(((bf16[1,512,5632]{2,1,0:T(8,128)(2,1)}), bf16[1,2048,5632]{2,1,0:T(8,128)(2,1)}) %all-gather.61.cloned.1.call-update) | async-done | bytes 23068688 | tf_op jit(solution)/shard_map/all_gather | solution.py:249
  1050.3 377.7 %all-gather.63.cloned.1.call-done = bf16[1,2048,5632]{2,1,0:T(8,128)(2,1)} async-done(((bf16[1,512,5632]{2,1,0:T(8,128)(2,1)}), bf16[1,2048,5632]{2,1,0:T(8,128)(2,1)}) %all-gather.63.cloned.1.call-update) | async-done | bytes 23068688 | tf_op jit(solution)/shard_map/all_gather | solution.py:250
  1443.2 375.8 %all-gather.51.cloned.1.call-done = bf16[1,5632,2048]{2,1,0:T(8,128)(2,1)} async-done(((bf16[1,1408,2048]{2,1,0:T(8,128)(2,1)}), bf16[1,5632,2048]{2,1,0:T(8,128)(2,1)}) %all-gather.51.cloned.1.call-update) | async-done | bytes 23068688 | tf_op jit(solution)/shard_map/all_gather | solution.py:251
  1878.3 34.9 while.199
  2008.1 34.8 while.200
  2118.1 56.0 %while.195 = (s32[]{:T(128)}, f32[1,16,128,128]{2,3,1,0:T(8,128)S(1)}, bf16[2,1,64,16,128]{4,2,3,1,0:T(8,128)(2,1)}, f32[2,1,64,16,128]{4,3,2,0,1:T(8,128)}, f32...) while((s32[]{:T(128)}, ...), condition=%wide.region_26.27_spmd.clone, body=%wide.region_22.26_spmd.clone.sunk | while | flops 1221527552 | bytes 99523912 | solution.py:100
  2214.1 15.9 select_bitcast_fusion.10
  2271.1 55.9 %while.196 = (s32[]{:T(128)}, f32[1,16,128,128]{2,3,1,0:T(8,128)S(1)}, bf16[2,1,64,16,128]{4,2,3,1,0:T(8,128)(2,1)}, f32[2,1,64,16,128]{4,3,2,0,1:T(8,128)}, f32...) while((s32[]{:T(128)}, ...), condition=%wide.region_34.35_spmd.clone, body=%wide.region_30.34_spmd.clone.sunk | while | flops 1221527552 | bytes 99523912 | solution.py:100
  2363.8 15.7 select_bitcast_fusion.11
  2420.8 56.0 %while.197 = (s32[]{:T(128)}, f32[1,16,128,128]{2,3,1,0:T(8,128)S(1)}, bf16[2,1,64,16,128]{4,2,3,1,0:T(8,128)(2,1)}, f32[2,1,64,16,128]{4,3,2,0,1:T(8,128)}, f32...) while((s32[]{:T(128)}, ...), condition=%wide.region_42.43_spmd.clone, body=%wide.region_38.42_spmd.clone.sunk | while | flops 1221527552 | bytes 99523912 | solution.py:100
  2536.2 19.9 convolution_bitcast_fusion.23
  2557.5 19.4 convolution_bitcast_fusion.22
  2583.1 20.3 convolution_bitcast_fusion.21
  2623.5 41.5 reduce-scatter.8.cloned.1.call-done
  2667.2 179.4 %reduce-scatter.10.cloned.1.call-done = f32[128,2048]{1,0:T(8,128)} async-done(((f32[2048,2048]{1,0:T(8,128)}), f32[128,2048]{1,0:T(8,128)}) %reduce-scatter.10.cloned.1.call-update) | async-done | bytes 1048592 | tf_op jit(solution)/shard_map/reduce_scatter | solution.py:204
  2848.9 179.4 %reduce-scatter.12.cloned.1.call-done = f32[128,2048]{1,0:T(8,128)} async-done(((f32[2048,2048]{1,0:T(8,128)}), f32[128,2048]{1,0:T(8,128)}) %reduce-scatter.12.cloned.1.call-update) | async-done | bytes 1048592 | tf_op jit(solution)/shard_map/reduce_scatter | solution.py:204
  3030.5 179.4 %reduce-scatter.14.cloned.1.call-done = f32[128,2048]{1,0:T(8,128)} async-done(((f32[2048,2048]{1,0:T(8,128)}), f32[128,2048]{1,0:T(8,128)}) %reduce-scatter.14.cloned.1.call-update) | async-done | bytes 1048592 | tf_op jit(solution)/shard_map/reduce_scatter | solution.py:204
  3212.0 434.3 %reduce-scatter.16.cloned.1.call-done = f32[128,5632]{1,0:T(8,128)} async-done(((f32[2048,5632]{1,0:T(8,128)}), f32[128,5632]{1,0:T(8,128)}) %reduce-scatter.16.cloned.1.call-update) | async-done | bytes 2883600 | tf_op jit(solution)/shard_map/reduce_scatter | solution.py:204
  3649.5 433.2 %reduce-scatter.18.cloned.1.call-done = f32[128,5632]{1,0:T(8,128)} async-done(((f32[2048,5632]{1,0:T(8,128)}), f32[128,5632]{1,0:T(8,128)}) %reduce-scatter.18.cloned.1.call-update) | async-done | bytes 2883600 | tf_op jit(solution)/shard_map/reduce_scatter | solution.py:204
  4094.5 17.0 fusion.462
  4111.6 407.5 %reduce-scatter.20.cloned.1.call-done = f32[352,2048]{1,0:T(8,128)} async-done(((f32[5632,2048]{1,0:T(8,128)}), f32[352,2048]{1,0:T(8,128)}) %reduce-scatter.20.cloned.1.call-update) | async-done | bytes 2883600 | tf_op jit(solution)/shard_map/reduce_scatter | solution.py:204
  4526.2 60.5 %all-reduce.8 = (bf16[2048]{0:T(1024)(128)(2,1)S(1)}, bf16[2048]{0:T(1024)(128)(2,1)S(1)}, bf16[2048]{0:T(1024)(128)(2,1)S(1)}, bf16[2048]{0:T(1024)(128)(2,1)S(1)}) all-reduce(f32[2048]{0:T(1024)S(1)} %add_add_fusion.12, f32[2048]{0:T(1024)S(1)} %get-tuple-element.3625, ...), channel_id=20, replica_groups=mesh['section'=2,'shard'=4,'rep'=4] {'shard','rep'}, use_global_device_ids=true, to_apply=%region_55.56.clone | all-reduce | flops 8192 | bytes 49152
  4633.2 19.9 all-gather.43.cloned.1.call-done
  4657.2 41.5 all-gather.45.cloned.1.call-done
  4707.2 37.0 all-gather.47.cloned.1.call-done
  4752.8 36.4 all-gather.49.cloned.1.call-done
  (1436 shorter events, 989.1 us)
Async XLA Ops:
  7.2 66.8 %all-gather.33.cloned.1.call-start = ((), (), s32[]{:S(2)}) async-start(), calls=%async_computation.7 | async-start | bytes 5242880 | tf_op jit(solution)/shard_map/all_gather | solution.py:241
  7.9 190.2 %all-gather.53.cloned.1.call-start = ((), (), s32[]{:S(2)}) async-start(), calls=%async_computation.24 | async-start | bytes 10485760 | tf_op jit(solution)/shard_map/all_gather | solution.py:246
  8.7 338.9 %all-gather.55.cloned.1.call-start = ((), (), s32[]{:S(2)}) async-start(), calls=%async_computation.25 | async-start | bytes 10485760 | tf_op jit(solution)/shard_map/all_gather | solution.py:247
  9.4 487.5 %all-gather.57.cloned.1.call-start = ((), (), s32[]{:S(2)}) async-start(), calls=%async_computation.26 | async-start | bytes 10485760 | tf_op jit(solution)/shard_map/all_gather | solution.py:245
  10.0 636.2 %all-gather.59.cloned.1.call-start = ((), (), s32[]{:S(2)}) async-start(), calls=%async_computation.27 | async-start | bytes 10485760 | tf_op jit(solution)/shard_map/all_gather | solution.py:248
  10.6 1026.4 %all-gather.61.cloned.1.call-start = ((), (), s32[]{:S(2)}) async-start(), calls=%async_computation.28 | async-start | bytes 28835840 | tf_op jit(solution)/shard_map/all_gather | solution.py:249
  11.1 1416.9 %all-gather.63.cloned.1.call-start = ((), (), s32[]{:S(2)}) async-start(), calls=%async_computation.29 | async-start | bytes 28835840 | tf_op jit(solution)/shard_map/all_gather | solution.py:250
  11.9 1807.1 %all-gather.51.cloned.1.call-start = ((), (), s32[]{:S(2)}) async-start(), calls=%async_computation.23 | async-start | bytes 28835840 | tf_op jit(solution)/shard_map/all_gather | solution.py:251
  12.7 2652.4 %reduce-scatter.8.cloned.1.call-start = ((), (), s32[]{:S(2)}) async-start(), calls=%async_computation.9 | async-start | bytes 17825792 | tf_op jit(solution)/shard_map/reduce_scatter | solution.py:204
  44.0 1934.9 %copy-start.206 = (f32[1,2048]{1,0:T(1,128)}, f32[1,2048]{1,0:T(1,128)S(1)}, u32[]{:S(2)}) copy-start(f32[1,2048]{1,0:T(1,128)S(1)} %convert_element_type.596) | copy-start | bytes 24580
  74.0 1745.0 %copy-start.242 = (f32[128]{0:T(128)}, f32[128]{0:T(128)S(1)}, u32[]{:S(2)}) copy-start(f32[128]{0:T(128)S(1)} %get-tuple-element.3595) | copy-start | bytes 1540
  77.1 1770.0 %copy-start.246 = (f32[128]{0:T(128)}, f32[128]{0:T(128)S(1)}, u32[]{:S(2)}) copy-start(f32[128]{0:T(128)S(1)} %fusion.588) | copy-start | bytes 1540
  653.1 1165.9 %copy-start.23 = (f32[1,128,2048]{2,1,0:T(8,128)}, f32[1,128,2048]{2,1,0:T(8,128)S(1)}, u32[]{:S(2)}) copy-start(f32[1,128,2048]{2,1,0:T(8,128)S(1)} %get-tuple-element.3600) | copy-start | bytes 3145732
  653.1 1270.4 %copy-start.244 = (f32[128]{0:T(128)}, f32[128]{0:T(128)S(1)}, u32[]{:S(2)}) copy-start(f32[128]{0:T(128)S(1)} %fusion.589) | copy-start | bytes 1540
  1830.7 15.0 collective-permute-start
  1960.7 18.0 collective-permute-start.1
  2197.0 14.8 collective-permute-start.2
  2350.0 13.8 collective-permute-start.3
  2489.0 357.6 %reduce-scatter.10.cloned.1.call-start = ((), (), s32[]{:S(2)}) async-start(), calls=%async_computation.11 | async-start | bytes 17825792 | tf_op jit(solution)/shard_map/reduce_scatter | solution.py:204
  2504.2 524.1 %reduce-scatter.12.cloned.1.call-start = ((), (), s32[]{:S(2)}) async-start(), calls=%async_computation.13 | async-start | bytes 17825792 | tf_op jit(solution)/shard_map/reduce_scatter | solution.py:204
  2516.1 693.8 %reduce-scatter.14.cloned.1.call-start = ((), (), s32[]{:S(2)}) async-start(), calls=%async_computation.15 | async-start | bytes 17825792 | tf_op jit(solution)/shard_map/reduce_scatter | solution.py:204
  2534.5 1111.8 %reduce-scatter.16.cloned.1.call-start = ((), (), s32[]{:S(2)}) async-start(), calls=%async_computation.17 | async-start | bytes 49020928 | tf_op jit(solution)/shard_map/reduce_scatter | solution.py:204
  2556.1 1526.6 %reduce-scatter.18.cloned.1.call-start = ((), (), s32[]{:S(2)}) async-start(), calls=%async_computation.19 | async-start | bytes 49020928 | tf_op jit(solution)/shard_map/reduce_scatter | solution.py:204
  2576.9 1942.1 %reduce-scatter.20.cloned.1.call-start = ((), (), s32[]{:S(2)}) async-start(), calls=%async_computation.21 | async-start | bytes 49020928 | tf_op jit(solution)/shard_map/reduce_scatter | solution.py:204
  2603.5 2005.9 %all-gather.35.cloned.1.call-start = ((), (), s32[]{:S(2)}) async-start(), calls=%async_computation.8 | async-start | bytes 5242880 | tf_op jit(solution)/shard_map/all_gather | solution.py:301
  2623.5 1991.1 %all-gather.37.cloned.1.call-start = ((), (), s32[]{:S(2)}) async-start(), calls=%async_computation.10 | async-start | bytes 2621440 | tf_op jit(solution)/shard_map/all_gather | solution.py:334
  2667.2 1951.5 %all-gather.39.cloned.1.call-start = ((), (), s32[]{:S(2)}) async-start(), calls=%async_computation.12 | async-start | bytes 2621440 | tf_op jit(solution)/shard_map/all_gather | solution.py:337
  2848.7 1780.3 %all-gather.41.cloned.1.call-start = ((), (), s32[]{:S(2)}) async-start(), calls=%async_computation.14 | async-start | bytes 2621440 | tf_op jit(solution)/shard_map/all_gather | solution.py:340
  3030.4 1622.6 %all-gather.43.cloned.1.call-start = ((), (), s32[]{:S(2)}) async-start(), calls=%async_computation.16 | async-start | bytes 2621440 | tf_op jit(solution)/shard_map/all_gather | solution.py:343
  3212.0 1486.7 %all-gather.45.cloned.1.call-start = ((), (), s32[]{:S(2)}) async-start(), calls=%async_computation.18 | async-start | bytes 7208960 | tf_op jit(solution)/shard_map/all_gather | solution.py:346
  3649.4 1094.8 %all-gather.47.cloned.1.call-start = ((), (), s32[]{:S(2)}) async-start(), calls=%async_computation.20 | async-start | bytes 7208960 | tf_op jit(solution)/shard_map/all_gather | solution.py:349
  4085.7 703.5 %all-gather.49.cloned.1.call-start = ((), (), s32[]{:S(2)}) async-start(), calls=%async_computation.22 | async-start | bytes 7208960 | tf_op jit(solution)/shard_map/all_gather | solution.py:352
  (408 other events, 7019.1 us)
Sparse Core Ops, SparseCore 0:
  9.6 37.1 all-gather.32
  48.3 149.6 all-gather.52
  199.7 147.8 all-gather.54
  349.0 147.8 all-gather.56
  498.3 147.8 all-gather.58
  647.6 389.3 all-gather.60
  1038.6 389.3 all-gather.62
  1429.6 389.3 all-gather.50
  2489.1 175.9 reduce-scatter.7
  2669.0 177.5 reduce-scatter.9
  2850.7 177.5 reduce-scatter.11
  3032.3 177.5 reduce-scatter.13
  3214.1 432.1 reduce-scatter.15
  3650.4 432.2 reduce-scatter.17
  4086.7 432.2 reduce-scatter.19
  4521.0 34.2 all-gather.34
  4557.2 22.8 all-gather.36
  4582.1 22.6 all-gather.38
  4606.4 22.5 all-gather.40
  4630.4 22.5 all-gather.42
  4655.2 43.3 all-gather.44
  4700.8 43.3 all-gather.46
  4745.8 43.3 all-gather.48
where the time goes:
time: 4810 us; the launch traced here: 4800 us
  waiting for transfers between devices  3640 us (76%)
  matrix products  587 us (12%)
  local copies, waits for them, and re-layouts  197 us (4%)
  other arithmetic  193 us (4%)
  blocking collectives  143 us (3%)
    reduce_scatter x7, waiting for transfers between devices, joint_owner(): lax.psum_scatter(weight_term(act_rows, grad_rows), ('shard', 'rep'), scat...  1850 us
    all_gather x1, waiting for transfers between devices, local(): lax.all_gather(w_gate[0], 'shard', axis=0, tiled=True)  384 us
    all_gather x1, waiting for transfers between devices, local(): lax.all_gather(w_up[0], 'shard', axis=0, tiled=True)  378 us
    all_gather x1, waiting for transfers between devices, local(): lax.all_gather(w_down[0], 'shard', axis=0, tiled=True)  376 us
    dot_general x21, matrix products, product_t(): lax.dot_general(left, right, (((left.ndim - 1,), (1,)), ((), ())), prefer...  197 us
    dot_general x21, matrix products, product(): return jnp.dot(left, right, preferred_element_type=jnp.float32)  176 us
    all_gather x1, waiting for transfers between devices, local(): lax.all_gather(w_input[0], 'shard', axis=0, tiled=True)  143 us
    all_gather x1, waiting for transfers between devices, local(): lax.all_gather(w_query[0], 'shard', axis=0, tiled=True)  137 us
  transfers between devices with their start and end apart: 27, of which 22 were waited for; matrix products, arithmetic and copies ran while one was open for 7% of the time, Pallas kernels for 0%

commit v1 on v0

v1 whole, which is shorter than its diff:
```python
import jax
import jax.numpy as jnp
from jax import lax
from jax.sharding import PartitionSpec as P

HEADS = 16
EPS = 1e-06
HEAD_EPS = 0.1
TOP_PRECISION = lax.Precision.HIGHEST
BF16 = jnp.bfloat16
F32 = jnp.float32


def swap(block, stage):
    axis, distance = stage
    return lax.ppermute(block, axis, [(i, i ^ distance) for i in range(lax.axis_size(axis))])


def one_way(block, source):
    return lax.ppermute(block, "section", [(source, 1 - source)])


def spread(block, stages):
    for stage in stages:
        block = jnp.concatenate([block, swap(block, stage)], axis=0)
    return block


def collapse(send, keep, stages):
    for stage in stages[::-1]:
        total = keep + swap(send.astype(BF16), stage).astype(F32)
        half = total.shape[0] // 2
        keep, send = total[:half], total[half:]
    return total


def reduced_product(left, right, stages):
    half = left.shape[0] // 2
    return collapse(product(left[half:], right), product(left[:half], right), stages)


def product(left, right):
    return jnp.dot(left, right, preferred_element_type=F32)


def product_t(left, right):
    return lax.dot_general(left, right, (((1,), (1,)), ((), ())), preferred_element_type=F32)


def weight_term(act_rows, grad_rows):
    return lax.dot_general(
        act_rows, grad_rows, (((0,), (0,)), ((), ())), preferred_element_type=F32
    ).astype(BF16)


def rms_norm(value, gain):
    return value * lax.rsqrt(jnp.mean(value * value, axis=-1, keepdims=True) + EPS) * gain


def head_norm(value, gain):
    return value * lax.rsqrt(jnp.mean(value * value, axis=-1, keepdims=True) + HEAD_EPS) * gain


def segment_info(lens_row, length):
    seg_ends = jnp.cumsum(lens_row)
    position = jnp.arange(length)
    segment_ids = jnp.sum((position[:, None] >= seg_ends[None, :]).astype(jnp.int32), axis=1)
    valid_mask = (position < length - lens_row[-1]).astype(F32)
    return (segment_ids, valid_mask)


def mixer(q, f, v, gap, gain_head, valid_mask, same):
    closed = jax.nn.sigmoid(-f) * gap
    k = closed * valid_mask[:, :, None, None]
    decay = jnp.cumsum(jnp.log(1.0 - closed), axis=1)
    query_decayed = q * jnp.exp(decay)
    key_decayed = k * jnp.exp(-decay)
    scores = (
        jnp.einsum("rthk,rshk->rhts", query_decayed, key_decayed, precision=TOP_PRECISION)
        * same[:, None]
    )
    o = jnp.einsum("rhts,rshv->rthv", scores, v, precision=TOP_PRECISION)
    return head_norm(o, gain_head)


def split_weights(
    w_query, w_forget, w_input, w_out, w_gate, w_up, w_down, ident, shards, group, sharing
):
    model_width = w_query.shape[1]
    head = model_width // HEADS
    per_device = HEADS // group
    per_shard = HEADS // shards
    cluster, member = ident // sharing, ident % sharing
    each = sharing * per_device // shards

    def head_columns(weight):
        parts = []
        for t in range(per_device):
            at = member * per_device + t
            number = per_shard * (at // each) + cluster * each + at % each
            parts.append(lax.dynamic_slice_in_dim(weight, number * head, head, 1))
        return parts

    qfv = jnp.concatenate(
        head_columns(w_query) + head_columns(w_forget) + head_columns(w_input), axis=1
    )
    width = model_width // sharing
    out = lax.dynamic_slice(
        w_out, (cluster * each * head, member * width), (each * head, width)
    )
    local_ff = w_down.shape[0]
    own_ff = local_ff // group

    def ff_columns(weight):
        return [
            lax.dynamic_slice_in_dim(weight, local_ff * s + own_ff * ident, own_ff, 1)
            for s in range(shards)
        ]

    gate_up = jnp.concatenate(ff_columns(w_gate) + ff_columns(w_up), axis=1)
    down = lax.dynamic_slice_in_dim(w_down, own_ff * ident, own_ff, 0)
    return (qfv, out, gate_up, down)


def local(
    boundary,
    lengths,
    deal_order,
    w_query,
    w_forget,
    w_input,
    w_out,
    w_gate,
    w_up,
    w_down,
    norm_mix,
    norm_head,
    norm_ffn,
    gate_gap,
):
    micro = deal_order.shape[0]
    reps = lax.axis_size("rep")
    shards = lax.axis_size("shard")
    group = 2 * reps
    model_width = boundary.shape[2]
    length = boundary.shape[1] // micro
    head = model_width // HEADS
    per_device = HEADS // group
    per_shard = HEADS // shards
    sharing = shards * group // HEADS
    each = sharing * per_device // shards
    section = lax.axis_index("section")
    rep = lax.axis_index("rep")
    shard = lax.axis_index("shard")
    on_first = section == 0
    ident = section * reps + rep

    rep_stages = []
    distance = reps // 2
    while distance:
        rep_stages.append(("rep", distance))
        distance //= 2
    stages = [("section", 1)] + rep_stages
    share_stages = [stage for stage in rep_stages if stage[1] < sharing]

    def codes(some):
        order = [0]
        for axis, distance in some:
            bit = reps if axis == "section" else distance
            order = order + [o ^ bit for o in order]
        return order

    def places(some):
        order = codes(some)
        slot = [0] * len(order)
        for at, code in enumerate(order):
            slot[code] = at
        return jnp.array(slot, jnp.int32)

    plane_order = jnp.array(codes(stages), jnp.int32)
    plane_place = places(stages)
    rep_place = places(rep_stages)

    block_rows = micro * reps
    numbers = lax.all_gather(
        jnp.concatenate([deal_order[:, None], lengths], axis=1), "rep", axis=0, tiled=True
    )
    block_order = numbers[:, 0] % block_rows
    block_lengths = numbers[:, 1:]
    gains = jnp.stack([norm_mix[0], norm_ffn[0], norm_head[0], gate_gap[0]])
    gains = lax.all_gather(gains, ("section", "shard"), axis=0, tiled=False)
    gains = gains.reshape(2, shards, 4, -1).transpose(0, 2, 1, 3).reshape(2, 4, model_width)
    gains = gains.astype(F32)

    local_weights = (w_query[0], w_forget[0], w_input[0], w_out[0], w_gate[0], w_up[0], w_down[0])
    kept = split_weights(*local_weights, ident, shards, group, sharing)
    sent = split_weights(
        *local_weights, (1 - section) * reps + rep, shards, group, sharing
    )
    received = [swap(piece, ("section", 1)) for piece in sent]
    layer_pieces = (
        [jnp.where(on_first, a, b) for a, b in zip(kept, received)],
        [jnp.where(on_first, b, a) for a, b in zip(kept, received)],
    )
    layer_weights = []
    member = ident % sharing
    for layer in range(2):
        qfv, out, gate_up, down = [
            lax.all_gather(piece, "shard", axis=0, tiled=True) for piece in layer_pieces[layer]
        ]
        wide = spread(out[None], share_stages)
        wide = wide[places(share_stages)[jnp.arange(sharing) ^ member]]
        wide = jnp.swapaxes(wide, 0, 1).reshape(shards * each * head, model_width)
        out = lax.dynamic_slice_in_dim(wide, member * per_device * head, per_device * head, 0)
        layer_weights.append((qfv, out, gate_up, down))

    cluster = ident // sharing
    own_heads = []
    for t in range(per_device):
        at = member * per_device + t
        own_heads.append(per_shard * (at // each) + cluster * each + at % each)

    def own_channels(vector):
        return jnp.stack(
            [lax.dynamic_slice_in_dim(vector, number * head, head, 0) for number in own_heads]
        )

    holder = plane_order ^ ident
    dealt_row = (holder % reps) * micro + holder // reps
    arrival_row = block_order[dealt_row]
    segment_ids, valid_mask = jax.vmap(lambda lens_row: segment_info(lens_row, length))(
        block_lengths[arrival_row]
    )
    causal = jnp.tril(jnp.ones((length, length), F32))
    same = (segment_ids[:, :, None] == segment_ids[:, None, :]).astype(F32) * causal
    valid_own = valid_mask[0][:, None]

    rows = boundary[0].reshape(micro, length, model_width)
    first_rows = jnp.where(on_first, rows, one_way(rows, 0))
    arrivals = spread(first_rows, rep_stages)
    slot = rep_place[(arrival_row // micro) ^ rep] * micro + arrival_row % micro
    dealt = arrivals[slot]
    own_cotangent = jnp.where(on_first, one_way(rows[0], 1), rows[1]).astype(F32)

    def forward(x_own, normed_all, weights, gain):
        qfv_weight, out_weight, gate_up_weight, down_weight = weights
        qfv = product(normed_all, qfv_weight).reshape(group, length, 3, per_device, head)
        mixed, pull_mix = jax.vjp(
            lambda a, b, c, d, e: mixer(a, b, c, d, e, valid_mask, same),
            qfv[:, :, 0],
            qfv[:, :, 1],
            qfv[:, :, 2],
            own_channels(gain[3]),
            own_channels(gain[2]),
        )
        mixed = mixed.reshape(group * length, per_device * head).astype(BF16)
        resid_mid = x_own + reduced_product(mixed, out_weight, stages)
        mid_value, pull_mid = jax.vjp(rms_norm, resid_mid, gain[1])
        normed_mid = spread(mid_value.astype(BF16), stages)
        gate_up = product(normed_mid, gate_up_weight)
        half = gate_up.shape[1] // 2
        hidden, pull_act = jax.vjp(
            lambda a, b: jax.nn.silu(a) * b, gate_up[:, :half], gate_up[:, half:]
        )
        hidden = hidden.astype(BF16)
        result = (resid_mid + reduced_product(hidden, down_weight, stages)) * valid_own
        return result.astype(BF16), (normed_all, mixed, normed_mid, hidden, pull_mix, pull_mid, pull_act)

    def transposed_sum(left, right, stages):
        half = left.shape[0] // 2
        return collapse(product_t(left[half:], right), product_t(left[:half], right), stages)

    def backward(grad_out, weights, kept_state, pull_in):
        qfv_weight, out_weight, gate_up_weight, down_weight = weights
        normed_all, mixed, normed_mid, hidden, pull_mix, pull_mid, pull_act = kept_state
        d_out = grad_out * valid_own
        d_down = spread(d_out.astype(BF16), stages)
        d_hidden = product_t(d_down, down_weight)
        d_gate_up = jnp.concatenate(pull_act(d_hidden), axis=1).astype(BF16)
        term_down = weight_term(hidden, d_down)
        term_gate_up = weight_term(normed_mid, d_gate_up)
        more, grad_ffn = pull_mid(transposed_sum(d_gate_up, gate_up_weight, stages))
        d_resid = d_out + more
        d_attn = spread(d_resid.astype(BF16), stages)
        d_mixed = product_t(d_attn, out_weight).reshape(group, length, per_device, head)
        d_q, d_f, d_v, grad_gap, grad_head = pull_mix(d_mixed)
        d_qfv = jnp.stack([d_q, d_f, d_v], axis=2).astype(BF16)
        d_qfv = d_qfv.reshape(group * length, 3 * per_device * head)
        term_out = weight_term(mixed, d_attn)
        term_qfv = weight_term(normed_all, d_qfv)
        more, grad_mix = pull_in(transposed_sum(d_qfv, qfv_weight, stages))
        d_x = d_resid + more
        wide = spread(term_out[None], share_stages)
        wide = wide[places(share_stages)[jnp.arange(sharing) ^ member]]
        wide = wide.reshape(sharing * per_device * head, model_width)
        term_out = lax.dynamic_slice_in_dim(
            wide, member * (model_width // sharing), model_width // sharing, 1
        )
        small = jnp.zeros((4, model_width), F32).at[0].set(grad_mix).at[1].set(grad_ffn)
        for t in range(per_device):
            column = own_heads[t] * head
            small = lax.dynamic_update_slice(small, grad_head[t][None], (2, column))
            small = lax.dynamic_update_slice(small, grad_gap[t][None], (3, column))
        return d_x, (term_qfv, term_out, term_gate_up, term_down), small

    dealt_f32 = dealt.astype(F32)
    normed_first = rms_norm(dealt_f32, gains[0, 0]).astype(BF16)
    _, pull_in_first = jax.vjp(rms_norm, dealt_f32[0], gains[0, 0])
    first, kept_first = forward(
        dealt_f32[0],
        normed_first.reshape(group * length, model_width),
        layer_weights[0],
        gains[0],
    )
    first_f32 = first.astype(F32)
    normed_second, pull_in_second = jax.vjp(rms_norm, first_f32, gains[1, 0])
    second, kept_second = forward(
        first_f32, spread(normed_second.astype(BF16), stages), layer_weights[1], gains[1]
    )
    d_first, terms_second, small_second = backward(
        own_cotangent, layer_weights[1], kept_second, pull_in_second
    )
    d_dealt, terms_first, small_first = backward(
        d_first.astype(BF16).astype(F32), layer_weights[0], kept_first, pull_in_first
    )

    all_grads = spread(d_dealt.astype(BF16)[None], stages)
    inverse = jnp.argsort(block_order)
    own_dealt = lax.dynamic_slice_in_dim(inverse, rep * micro, micro, 0)
    own_holder = (own_dealt % micro) * reps + own_dealt // micro
    back_rows = all_grads[plane_place[own_holder ^ ident]]
    second_rows = jnp.stack([one_way(second, 0), second])
    boundary_out = jnp.where(on_first, back_rows, second_rows).reshape(
        1, micro * length, model_width
    )

    absolute = plane_place[jnp.arange(group) ^ ident]
    pieces = []
    for number in range(4):
        summed = [
            lax.psum_scatter(terms[number], "shard", scatter_dimension=0, tiled=True)
            for terms in (terms_first, terms_second)
        ]
        keep = jnp.where(on_first, summed[0], summed[1])[None]
        send = jnp.where(on_first, summed[1], summed[0])[None]
        pair = jnp.concatenate([keep, swap(send, ("section", 1))], axis=0)
        pieces.append(spread(pair, rep_stages)[absolute].astype(F32))
    qfv, out, gate_up, down = pieces
    local_rows = qfv.shape[1]
    clusters = group // sharing
    qfv = qfv.reshape(clusters, sharing, local_rows, 3, per_device, head)
    qfv = qfv.transpose(3, 2, 1, 4, 0, 5).reshape(
        3, local_rows, shards, each, clusters, head
    )
    qfv = qfv.transpose(0, 1, 2, 4, 3, 5).reshape(3, local_rows, model_width)
    out = out.reshape(clusters, sharing, each * head, model_width // sharing)
    out = out.transpose(0, 2, 1, 3).reshape(local_rows, model_width)
    own_ff = w_down.shape[1] // group
    gate_up = gate_up.reshape(group, local_rows, 2, shards, own_ff)
    gate_up = gate_up.transpose(2, 1, 3, 0, 4).reshape(2, local_rows, -1)
    down = down.reshape(-1, model_width)

    small = jnp.stack([small_first, small_second])
    for stage in stages:
        small = small + swap(small, stage)
    small = jnp.where(on_first, small[0], small[1])
    small = jnp.sum(lax.all_gather(small, "shard", axis=0, tiled=False), axis=0)
    small = lax.dynamic_slice_in_dim(small, shard * local_rows, local_rows, 1)

    return (
        boundary_out,
        qfv[0][None],
        qfv[1][None],
        qfv[2][None],
        out[None],
        gate_up[0][None],
        gate_up[1][None],
        down[None],
        small[0][None],
        small[2][None],
        small[1][None],
        small[3][None],
    )


def solution(mesh):
    row_blocks = P("section", ("shard", "rep"), None)
    weight = P("section", "shard", None)
    vector = P("section", "shard")
    return jax.shard_map(
        local,
        mesh=mesh,
        in_specs=(row_blocks, P(("shard", "rep"), None), P(("shard", "rep")))
        + (weight,) * 7
        + (vector,) * 4,
        out_specs=(row_blocks,) + (weight,) * 7 + (vector,) * 4,
        check_vma=False,
    )
```

time: 4810 us -> 1670 us (0.35)
  waiting for transfers between devices: 3640 us -> 844 us
  matrix products: 587 us -> 199 us
  local copies, waits for them, and re-layouts: 197 us -> 301 us
  blocking collectives: 143 us -> 50.2 us
  starting transfers between devices: 12.6 us -> 93.3 us
    all_gather x16 -> x8, waiting for transfers between devices: 1750 us -> 56.9 us  [local(): lax.all_gather(piece, 'shard', axis=0, tiled=True)]
    reduce_scatter x7 -> x8, waiting for transfers between devices: 1850 us -> 202 us  [local(): lax.psum_scatter(terms[number], 'shard', scatter_dimension=0, tiled=True)]
    ppermute x4 -> x76, waiting for transfers between devices: 28.6 us -> 585 us  [the longest x73 585 us: swap(): lax.ppermute(block, axis, [(i, i ^ distance) for i in range(lax.axis_size...]
    dot_general x114 -> x36, matrix products: 490 us -> 147 us  [the longest x12 64.2 us: product_t(): lax.dot_general(left, right, (((1,), (1,)), ((), ())), preferred_element_...]
    slice x15 -> x47, local copies, waits for them, and re-layouts: 8.74 us -> 107 us  [the longest x2 26.5 us: local(): gate_up[1][None]]
    concatenate x1 -> x35, other arithmetic: 1.06 us -> 72.6 us  [the longest x31 67.3 us: spread(): block = jnp.concatenate([block, swap(block, stage)], axis=0)]
    ppermute x4 -> x76, starting transfers between devices: 10.9 us -> 80.4 us  [the longest x73 72.9 us: swap(): lax.ppermute(block, axis, [(i, i ^ distance) for i in range(lax.axis_size...]
    unnamed x2 -> x0, blocking collectives: 65.4 us -> none
  transfers between devices with their start and end apart: 27 -> 92, of which waited for: 22 -> 51; matrix products, arithmetic and copies ran while one was open for 7% -> 29% of each run, Pallas kernels for 0% -> 0%
where the time goes in v1:
time: 1670 us; the launch traced here: 1660 us
  waiting for transfers between devices  844 us (51%)
  local copies, waits for them, and re-layouts  301 us (18%)
  matrix products  199 us (12%)
  other arithmetic  152 us (9%)
  starting transfers between devices  93.3 us (6%)
  blocking collectives  50.2 us (3%)
  between operations  17.1 us (1%)
    ppermute x73, waiting for transfers between devices, swap(): lax.ppermute(block, axis, [(i, i ^ distance) for i in range(lax.axis_size...  585 us
    reduce_scatter x8, waiting for transfers between devices, local(): lax.psum_scatter(terms[number], 'shard', scatter_dimension=0, tiled=True)  202 us
    ppermute x73, starting transfers between devices, swap(): lax.ppermute(block, axis, [(i, i ^ distance) for i in range(lax.axis_size...  72.9 us
    concatenate x31, other arithmetic, spread(): block = jnp.concatenate([block, swap(block, stage)], axis=0)  67.3 us
    dot_general x12, matrix products, product_t(): lax.dot_general(left, right, (((1,), (1,)), ((), ())), preferred_element_...  64.2 us
    unnamed x344, local copies, waits for them, and re-layouts  58 us
    all_gather x8, waiting for transfers between devices, local(): lax.all_gather(piece, 'shard', axis=0, tiled=True)  56.9 us
    dot_general x12, matrix products, product(): return jnp.dot(left, right, preferred_element_type=F32)  55.6 us
  transfers between devices with their start and end apart: 92, of which 51 were waited for; matrix products, arithmetic and copies ran while one was open for 29% of the time, Pallas kernels for 0%

profile of v1, /device:TPU:0, one launch (start us, length us, event | category | flops | bytes accessed | tf_op | source)
XLA Modules:
  0.0 1656.1 jit_solution(977885797840418396)
XLA Ops:
  39.7 31.3 %all-gather.2 = bf16[8,4,512]{2,1,0:T(4,128)(2,1)S(1)} all-gather(bf16[1,4,512]{2,1,0:T(4,128)(2,1)S(1)} %maximum_bitcast_fusion), channel_id=2, replica_groups=mesh['section'=2,'shard'=4,'rep'=4] {'section','shard'}, dimensions={0}, use_global_device_ids=true | all-gather | bytes 36864 | tf_op jit(solution)/shard_map/all_gather | solution.py:191
  83.5 23.2 %collective-permute-done.6 = bf16[2,128,2048]{2,1,0:T(8,128)(2,1)S(1)} collective-permute-done((bf16[2,128,2048]{2,1,0:T(8,128)(2,1)S(1)}, bf16[2,128,2048]{2,1,0:T(8,128)(2,1)S(1)}, u32[]{:S(2)}, u32[]{:S(2)}) %collective-permute-start.6) | collective-permute-done | bytes 1048608 | tf_op jit(solution)/shard_map/ppermute | solution.py:16
  173.3 23.7 %collective-permute-done.12 = bf16[256,2048]{1,0:T(8,128)(2,1)S(1)} collective-permute-done((bf16[256,2048]{1,0:T(8,128)(2,1)S(1)}, bf16[256,2048]{1,0:T(8,128)(2,1)S(1)}, u32[]{:S(2)}, u32[]{:S(2)}) %collective-permute-start.12) | collective-permute-done | bytes 1048608 | tf_op jit(solution)/shard_map/ppermute | solution.py:16
  229.4 18.0 %collective-permute-done.15 = bf16[256,2048]{1,0:T(8,128)(2,1)} collective-permute-done((bf16[256,2048]{1,0:T(8,128)(2,1)S(1)}, bf16[256,2048]{1,0:T(8,128)(2,1)}, u32[]{:S(2)}, u32[]{:S(2)}) %collective-permute-start.15) | collective-permute-done | bytes 1048608 | tf_op jit(solution)/shard_map/ppermute | solution.py:16
  268.3 42.8 %all-gather.20.cloned.1.call-done = bf16[704,2048]{1,0:T(8,128)(2,1)} async-done(((bf16[176,2048]{1,0:T(8,128)(2,1)}), bf16[704,2048]{1,0:T(8,128)(2,1)}) %all-gather.20.cloned.1.call-update) | async-done | bytes 2883600 | tf_op jit(solution)/shard_map/all_gather | solution.py:209
  327.0 22.6 %collective-permute-done.19 = bf16[256,2048]{1,0:T(8,128)(2,1)} collective-permute-done((bf16[256,2048]{1,0:T(8,128)(2,1)}, bf16[256,2048]{1,0:T(8,128)(2,1)}, u32[]{:S(2)}, u32[]{:S(2)}) %collective-permute-start.19) | collective-permute-done | bytes 1048608 | tf_op jit(solution)/shard_map/ppermute | solution.py:16
  385.0 21.1 %collective-permute-done.22 = bf16[256,2048]{1,0:T(8,128)(2,1)S(1)} collective-permute-done((bf16[256,2048]{1,0:T(8,128)(2,1)S(1)}, bf16[256,2048]{1,0:T(8,128)(2,1)S(1)}, u32[]{:S(2)}, u32[]{:S(2)}) %collective-permute-start.22) | collective-permute-done | bytes 1048608 | tf_op jit(solution)/shard_map/ppermute | solution.py:16
  453.2 23.8 %collective-permute-done.26 = bf16[256,2048]{1,0:T(8,128)(2,1)S(1)} collective-permute-done((bf16[256,2048]{1,0:T(8,128)(2,1)S(1)}, bf16[256,2048]{1,0:T(8,128)(2,1)S(1)}, u32[]{:S(2)}, u32[]{:S(2)}) %collective-permute-start.26) | collective-permute-done | bytes 1048608 | tf_op jit(solution)/shard_map/ppermute | solution.py:16
  508.3 19.8 %collective-permute-done.29 = bf16[256,2048]{1,0:T(8,128)(2,1)} collective-permute-done((bf16[256,2048]{1,0:T(8,128)(2,1)}, bf16[256,2048]{1,0:T(8,128)(2,1)}, u32[]{:S(2)}, u32[]{:S(2)}) %collective-permute-start.29) | collective-permute-done | bytes 1048608 | tf_op jit(solution)/shard_map/ppermute | solution.py:16
  532.7 24.2 %collective-permute-done.2 = bf16[256,2048]{1,0:T(8,128)(2,1)S(1)} collective-permute-done((bf16[256,2048]{1,0:T(8,128)(2,1)S(1)}, bf16[256,2048]{1,0:T(8,128)(2,1)S(1)}, u32[]{:S(2)}, u32[]{:S(2)}) %collective-permute-start.2) | collective-permute-done | bytes 1048608 | tf_op jit(solution)/shard_map/ppermute | solution.py:16
  558.6 12.7 fusion.91
  612.2 21.8 %collective-permute-done.32 = bf16[256,2048]{1,0:T(8,128)(2,1)S(1)} collective-permute-done((bf16[256,2048]{1,0:T(8,128)(2,1)S(1)}, bf16[256,2048]{1,0:T(8,128)(2,1)S(1)}, u32[]{:S(2)}, u32[]{:S(2)}) %collective-permute-start.32) | collective-permute-done | bytes 1048608 | tf_op jit(solution)/shard_map/ppermute | solution.py:16
  635.9 19.8 %collective-permute-done.56 = bf16[256,2048]{1,0:T(8,128)(2,1)S(1)} collective-permute-done((bf16[256,2048]{1,0:T(8,128)(2,1)S(1)}, bf16[256,2048]{1,0:T(8,128)(2,1)S(1)}, u32[]{:S(2)}, u32[]{:S(2)}) %collective-permute-start.56) | collective-permute-done | bytes 1048608 | tf_op jit(solution)/shard_map/ppermute | solution.py:16
  685.1 21.1 %collective-permute-done.35 = bf16[256,2048]{1,0:T(8,128)(2,1)S(1)} collective-permute-done((bf16[256,2048]{1,0:T(8,128)(2,1)S(1)}, bf16[256,2048]{1,0:T(8,128)(2,1)S(1)}, u32[]{:S(2)}, u32[]{:S(2)}) %collective-permute-start.35) | collective-permute-done | bytes 1048608 | tf_op jit(solution)/shard_map/ppermute | solution.py:16
  746.5 23.7 %collective-permute-done.38 = bf16[256,2048]{1,0:T(8,128)(2,1)S(1)} collective-permute-done((bf16[256,2048]{1,0:T(8,128)(2,1)S(1)}, bf16[256,2048]{1,0:T(8,128)(2,1)S(1)}, u32[]{:S(2)}, u32[]{:S(2)}) %collective-permute-start.38) | collective-permute-done | bytes 1048608 | tf_op jit(solution)/shard_map/ppermute | solution.py:16
  799.5 21.1 %collective-permute-done.41 = bf16[256,2048]{1,0:T(8,128)(2,1)S(1)} collective-permute-done((bf16[256,2048]{1,0:T(8,128)(2,1)S(1)}, bf16[256,2048]{1,0:T(8,128)(2,1)S(1)}, u32[]{:S(2)}, u32[]{:S(2)}) %collective-permute-start.41) | collective-permute-done | bytes 1048608 | tf_op jit(solution)/shard_map/ppermute | solution.py:16
  867.2 17.8 %collective-permute-done.44 = bf16[256,2048]{1,0:T(8,128)(2,1)} collective-permute-done((bf16[256,2048]{1,0:T(8,128)(2,1)}, bf16[256,2048]{1,0:T(8,128)(2,1)}, u32[]{:S(2)}, u32[]{:S(2)}) %collective-permute-start.44) | collective-permute-done | bytes 1048608 | tf_op jit(solution)/shard_map/ppermute | solution.py:16
  888.7 11.9 collective-permute-done.45
  917.1 21.2 %collective-permute-done.47 = bf16[256,2048]{1,0:T(8,128)(2,1)S(1)} collective-permute-done((bf16[256,2048]{1,0:T(8,128)(2,1)S(1)}, bf16[256,2048]{1,0:T(8,128)(2,1)S(1)}, u32[]{:S(2)}, u32[]{:S(2)}) %collective-permute-start.47) | collective-permute-done | bytes 1048608 | tf_op jit(solution)/shard_map/ppermute | solution.py:16
  1008.3 15.7 collective-permute-done.70
  1084.3 26.7 %reduce-scatter.19.cloned.1.call-done = bf16[512,1408]{1,0:T(8,128)(2,1)} async-done(((bf16[2048,1408]{1,0:T(8,128)(2,1)}), bf16[512,1408]{1,0:T(8,128)(2,1)}) %reduce-scatter.19.cloned.1.call-update) | async-done | bytes 1441808 | tf_op jit(solution)/shard_map/reduce_scatter | solution.py:341
  1110.9 105.5 %reduce-scatter.17.cloned.1.call-done = bf16[512,1408]{1,0:T(8,128)(2,1)} async-done(((bf16[2048,1408]{1,0:T(8,128)(2,1)}), bf16[512,1408]{1,0:T(8,128)(2,1)}) %reduce-scatter.17.cloned.1.call-update) | async-done | bytes 1441808 | tf_op jit(solution)/shard_map/reduce_scatter | solution.py:341
  1239.5 25.2 %collective-permute-done.51 = bf16[128,2048]{1,0:T(8,128)(2,1)} collective-permute-done((bf16[128,2048]{1,0:T(8,128)(2,1)}, bf16[128,2048]{1,0:T(8,128)(2,1)}, u32[]{:S(2)}, u32[]{:S(2)}) %collective-permute-start.51) | collective-permute-done | bytes 524320 | tf_op jit(solution)/shard_map/ppermute | solution.py:16
  1280.0 63.0 %reduce-scatter.9.cloned.1.call-done = bf16[512,768]{1,0:T(8,128)(2,1)} async-done(((bf16[2048,768]{1,0:T(8,128)(2,1)}), bf16[512,768]{1,0:T(8,128)(2,1)}) %reduce-scatter.9.cloned.1.call-update) | async-done | bytes 786448 | tf_op jit(solution)/shard_map/reduce_scatter | solution.py:341
  1350.3 15.0 collective-permute-done.59
  1384.7 36.9 %collective-permute-done.53 = bf16[2,128,2048]{2,1,0:T(8,128)(2,1)S(1)} collective-permute-done((bf16[2,128,2048]{2,1,0:T(8,128)(2,1)S(1)}, bf16[2,128,2048]{2,1,0:T(8,128)(2,1)S(1)}, u32[]{:S(2)}, u32[]{:S(2)}) %collective-permute-start.53) | collective-permute-done | bytes 1048608 | tf_op jit(solution)/shard_map/ppermute | solution.py:16
  1436.2 13.9 all_gather.48
  1494.7 13.7 reshape.824
  1571.3 16.9 %copy.432 = f32[8,512,1408]{1,2,0:T(8,128)} copy(bf16[8,512,1408]{2,1,0:T(8,128)(2,1)} %gather_fusion.14) | data formatting | bytes 34603008 | tf_op jit(solution)/shard_map/transpose | solution.py:360
  1588.2 15.7 fusion.186
  1614.7 11.9 copy.438
  1637.4 11.9 copy.437
  (813 shorter events, 845.4 us)
Async XLA Ops:
  7.2 103.1 %all-gather.16.cloned.1.call-start = ((), (), s32[]{:S(2)}) async-start(), calls=%async_computation.10 | async-start | bytes 1310720 | tf_op jit(solution)/shard_map/all_gather | solution.py:209
  11.3 69.8 %collective-permute-start.5 = (bf16[2,128,2048]{2,1,0:T(8,128)(2,1)}, bf16[2,128,2048]{2,1,0:T(8,128)(2,1)S(1)}, u32[]{:S(2)}, u32[]{:S(2)}) collective-permute-start(bf16[2,128,2048]{2,1,0:T(8,128)(2,1)} %bitcast.512), channel_id=1, source_target_pairs={{0,16},{1,17},{2,18},{3,19},{4,20},{5,21},{6,22},{7,23},{8,24},{9,... | collective-permute-start | bytes 3145736 | tf_op jit(solution)/shard_map/ppermute | solution.py:20
  19.9 123.4 %all-gather.14.cloned.1.call-start = ((), (), s32[]{:S(2)}) async-start(), calls=%async_computation.9 | async-start | bytes 3932160 | tf_op jit(solution)/shard_map/all_gather | solution.py:209
  26.5 49.7 %collective-permute-start.8 = (bf16[512,768]{1,0:T(8,128)(2,1)}, bf16[512,768]{1,0:T(8,128)(2,1)}, u32[]{:S(2)}, u32[]{:S(2)}) collective-permute-start(bf16[512,768]{1,0:T(8,128)(2,1)} %get-tuple-element.201), channel_id=1, source_target_pairs={{0,16},{16,0},{1,17},{17,1},{2,18},{18,2},{3,19},{19,3},{4,20},{20... | collective-permute-start | bytes 2359304 | tf_op jit(solution)/shard_map/ppermute | solution.py:16
  39.5 75.3 %collective-permute-start.17 = (bf16[512,1408]{1,0:T(8,128)(2,1)}, bf16[512,1408]{1,0:T(8,128)(2,1)}, u32[]{:S(2)}, u32[]{:S(2)}) collective-permute-start(bf16[512,1408]{1,0:T(8,128)(2,1)} %concatenate.195), channel_id=1, source_target_pairs={{0,16},{16,0},{1,17},{17,1},{2,18},{18,2},{3,19},{19,3},{4,20},{20... | collective-permute-start | bytes 4325384 | tf_op jit(solution)/shard_map/ppermute | solution.py:16
  78.6 174.7 %all-gather.18.cloned.1.call-start = ((), (), s32[]{:S(2)}) async-start(), calls=%async_computation.11 | async-start | bytes 7208960 | tf_op jit(solution)/shard_map/all_gather | solution.py:209
  118.0 193.0 %all-gather.20.cloned.1.call-start = ((), (), s32[]{:S(2)}) async-start(), calls=%async_computation.12 | async-start | bytes 3604480 | tf_op jit(solution)/shard_map/all_gather | solution.py:209
  252.9 155.7 %all-gather.24.cloned.1.call-start = ((), (), s32[]{:S(2)}) async-start(), calls=%async_computation.14 | async-start | bytes 1310720 | tf_op jit(solution)/shard_map/all_gather | solution.py:209
  325.6 96.9 %all-gather.22.cloned.1.call-start = ((), (), s32[]{:S(2)}) async-start(), calls=%async_computation.13 | async-start | bytes 3932160 | tf_op jit(solution)/shard_map/all_gather | solution.py:209
  355.4 203.2 %all-gather.26.cloned.1.call-start = ((), (), s32[]{:S(2)}) async-start(), calls=%async_computation.15 | async-start | bytes 7208960 | tf_op jit(solution)/shard_map/all_gather | solution.py:209
  409.9 173.0 %all-gather.12.cloned.1.call-start = ((), (), s32[]{:S(2)}) async-start(), calls=%async_computation.8 | async-start | bytes 3604480 | tf_op jit(solution)/shard_map/all_gather | solution.py:209
  506.3 496.8 %reduce-scatter.23.cloned.1.call-start = ((), (), s32[]{:S(2)}) async-start(), calls=%async_computation.23 | async-start | bytes 3604480 | tf_op jit(solution)/shard_map/reduce_scatter | solution.py:341
  829.5 173.7 %reduce-scatter.21.cloned.1.call-start = ((), (), s32[]{:S(2)}) async-start(), calls=%async_computation.22 | async-start | bytes 3604480 | tf_op jit(solution)/shard_map/reduce_scatter | solution.py:341
  867.1 213.9 %reduce-scatter.15.cloned.1.call-start = ((), (), s32[]{:S(2)}) async-start(), calls=%async_computation.19 | async-start | bytes 1310720 | tf_op jit(solution)/shard_map/reduce_scatter | solution.py:341
  953.2 127.8 %reduce-scatter.13.cloned.1.call-start = ((), (), s32[]{:S(2)}) async-start(), calls=%async_computation.18 | async-start | bytes 1310720 | tf_op jit(solution)/shard_map/reduce_scatter | solution.py:341
  967.6 143.4 %reduce-scatter.19.cloned.1.call-start = ((), (), s32[]{:S(2)}) async-start(), calls=%async_computation.21 | async-start | bytes 7208960 | tf_op jit(solution)/shard_map/reduce_scatter | solution.py:341
  978.5 237.9 %reduce-scatter.17.cloned.1.call-start = ((), (), s32[]{:S(2)}) async-start(), calls=%async_computation.20 | async-start | bytes 7208960 | tf_op jit(solution)/shard_map/reduce_scatter | solution.py:341
  990.6 289.4 %reduce-scatter.11.cloned.1.call-start = ((), (), s32[]{:S(2)}) async-start(), calls=%async_computation.17 | async-start | bytes 3932160 | tf_op jit(solution)/shard_map/reduce_scatter | solution.py:341
  1002.9 340.2 %reduce-scatter.9.cloned.1.call-start = ((), (), s32[]{:S(2)}) async-start(), calls=%async_computation.16 | async-start | bytes 3932160 | tf_op jit(solution)/shard_map/reduce_scatter | solution.py:341
  1067.9 160.1 %collective-permute-start.72 = (bf16[4,176,2048]{2,1,0:T(8,128)(2,1)}, bf16[4,176,2048]{2,1,0:T(8,128)(2,1)}, u32[]{:S(2)}, u32[]{:S(2)}) collective-permute-start(bf16[4,176,2048]{2,1,0:T(8,128)(2,1)} %pad_maximum_fusion.19), channel_id=1, source_target_pairs={{0,1},{1,0},{2,3},{3,2},{4,5},{5,4},{6,7},{7,6},{8,9},{9,8},{10,11... | collective-permute-start | bytes 8650760 | tf_op jit(solution)/shard_map/ppermute | solution.py:16
  1080.5 140.8 %collective-permute-start.50 = (bf16[256,2048]{1,0:T(8,128)(2,1)}, bf16[256,2048]{1,0:T(8,128)(2,1)}, u32[]{:S(2)}, u32[]{:S(2)}) collective-permute-start(bf16[256,2048]{1,0:T(8,128)(2,1)} %slice.818), channel_id=1, source_target_pairs={{0,2},{1,3},{2,0},{3,1},{4,6},{5,7},{6,4},{7,5},{8,10},{9,11},{10,... | collective-permute-start | bytes 3145736 | tf_op jit(solution)/shard_map/ppermute | solution.py:16
  1082.8 142.7 %collective-permute-start.64 = (bf16[1,128,1024]{2,1,0:T(8,128)(2,1)}, bf16[1,128,1024]{2,1,0:T(8,128)(2,1)S(1)}, u32[]{:S(2)}, u32[]{:S(2)}) collective-permute-start(bf16[1,128,1024]{2,1,0:T(8,128)(2,1)} %get-tuple-element.227), channel_id=1, source_target_pairs={{0,16},{16,0},{1,17},{17,1},{2,18},{18,2},{3,19},{19,3},{4,20},{20... | collective-permute-start | bytes 786440 | tf_op jit(solution)/shard_map/ppermute | solution.py:16
  1226.5 150.4 %collective-permute-start.65 = (bf16[2,128,1024]{2,1,0:T(8,128)(2,1)}, bf16[2,128,1024]{2,1,0:T(8,128)(2,1)}, u32[]{:S(2)}, u32[]{:S(2)}) collective-permute-start(bf16[2,128,1024]{2,1,0:T(8,128)(2,1)} %pad_maximum_fusion.60), channel_id=1, source_target_pairs={{0,2},{1,3},{2,0},{3,1},{4,6},{5,7},{6,4},{7,5},{8,10},{9,11},{10,... | collective-permute-start | bytes 1572872 | tf_op jit(solution)/shard_map/ppermute | solution.py:16
  1268.6 111.0 %collective-permute-start.68 = (bf16[2,512,1408]{2,1,0:T(8,128)(2,1)}, bf16[2,512,1408]{2,1,0:T(8,128)(2,1)}, u32[]{:S(2)}, u32[]{:S(2)}) collective-permute-start(bf16[2,512,1408]{2,1,0:T(8,128)(2,1)} %pad_maximum_fusion.18), channel_id=1, source_target_pairs={{0,2},{1,3},{2,0},{3,1},{4,6},{5,7},{6,4},{7,5},{8,10},{9,11},{10,... | collective-permute-start | bytes 8650760 | tf_op jit(solution)/shard_map/ppermute | solution.py:16
  1271.8 76.9 %collective-permute-start.73 = (f32[2,4,2048]{2,1,0:T(4,128)}, f32[2,4,2048]{2,1,0:T(4,128)S(1)}, u32[]{:S(2)}, u32[]{:S(2)}) collective-permute-start(f32[2,4,2048]{2,1,0:T(4,128)} %pad_maximum_fusion.61), channel_id=1, source_target_pairs={{0,16},{16,0},{1,17},{17,1},{2,18},{18,2},{3,19},{19,3},{4,20},{20... | collective-permute-start | bytes 196616 | tf_op jit(solution)/shard_map/ppermute | solution.py:16
  1365.4 57.9 %collective-permute-start.60 = (bf16[2,512,768]{2,1,0:T(8,128)(2,1)S(1)}, bf16[2,512,768]{2,1,0:T(8,128)(2,1)S(1)}, u32[]{:S(2)}, u32[]{:S(2)}) collective-permute-start(bf16[2,512,768]{2,1,0:T(8,128)(2,1)S(1)} %pad_maximum_fusion.35), channel_id=1, source_target_pairs={{0,2},{1,3},{2,0},{3,1},{4,6},{5,7},{6,4},{7,5},{8,10},{9,11},{10,... | collective-permute-start | bytes 4718600 | tf_op jit(solution)/shard_map/ppermute | solution.py:16
  1376.8 55.2 %collective-permute-start.75 = (f32[2,4,2048]{2,1,0:T(4,128)S(1)}, f32[2,4,2048]{2,1,0:T(4,128)S(1)}, u32[]{:S(2)}, u32[]{:S(2)}) collective-permute-start(f32[2,4,2048]{2,1,0:T(4,128)S(1)} %fusion.228), channel_id=1, source_target_pairs={{0,1},{1,0},{2,3},{3,2},{4,5},{5,4},{6,7},{7,6},{8,9},{9,8},{10,11... | collective-permute-start | bytes 196616 | tf_op jit(solution)/shard_map/ppermute | solution.py:16
  1379.2 73.1 %collective-permute-start.66 = (bf16[4,128,1024]{2,1,0:T(8,128)(2,1)}, bf16[4,128,1024]{2,1,0:T(8,128)(2,1)}, u32[]{:S(2)}, u32[]{:S(2)}) collective-permute-start(bf16[4,128,1024]{2,1,0:T(8,128)(2,1)} %pad_maximum_fusion.45), channel_id=1, source_target_pairs={{0,1},{1,0},{2,3},{3,2},{4,5},{5,4},{6,7},{7,6},{8,9},{9,8},{10,11... | collective-permute-start | bytes 3145736 | tf_op jit(solution)/shard_map/ppermute | solution.py:16
  1384.6 166.9 %collective-permute-start.69 = (bf16[4,512,1408]{2,1,0:T(8,128)(2,1)}, bf16[4,512,1408]{2,1,0:T(8,128)(2,1)}, u32[]{:S(2)}, u32[]{:S(2)}) collective-permute-start(bf16[4,512,1408]{2,1,0:T(8,128)(2,1)} %pad_maximum_fusion.2), channel_id=1, source_target_pairs={{0,1},{1,0},{2,3},{3,2},{4,5},{5,4},{6,7},{7,6},{8,9},{9,8},{10,11... | collective-permute-start | bytes 17301512 | tf_op jit(solution)/shard_map/ppermute | solution.py:16
  1423.3 49.7 %collective-permute-start.54 = (bf16[4,128,2048]{2,1,0:T(8,128)(2,1)}, bf16[4,128,2048]{2,1,0:T(8,128)(2,1)}, u32[]{:S(2)}, u32[]{:S(2)}) collective-permute-start(bf16[4,128,2048]{2,1,0:T(8,128)(2,1)} %pad_maximum_fusion.30), channel_id=1, source_target_pairs={{0,1},{1,0},{2,3},{3,2},{4,5},{5,4},{6,7},{7,6},{8,9},{9,8},{10,11... | collective-permute-start | bytes 6291464 | tf_op jit(solution)/shard_map/ppermute | solution.py:16
  1425.5 57.7 %collective-permute-start.61 = (bf16[4,512,768]{2,1,0:T(8,128)(2,1)}, bf16[4,512,768]{2,1,0:T(8,128)(2,1)}, u32[]{:S(2)}, u32[]{:S(2)}) collective-permute-start(bf16[4,512,768]{2,1,0:T(8,128)(2,1)} %pad_maximum_fusion.15), channel_id=1, source_target_pairs={{0,1},{1,0},{2,3},{3,2},{4,5},{5,4},{6,7},{7,6},{8,9},{9,8},{10,11... | collective-permute-start | bytes 9437192 | tf_op jit(solution)/shard_map/ppermute | solution.py:16
  1432.0 48.4 %collective-permute-start.58 = (bf16[128,2048]{1,0:T(8,128)(2,1)}, bf16[128,2048]{1,0:T(8,128)(2,1)}, u32[]{:S(2)}, u32[]{:S(2)}) collective-permute-start(bf16[128,2048]{1,0:T(8,128)(2,1)} %get-tuple-element.223), channel_id=1, source_target_pairs={{0,16},{1,17},{2,18},{3,19},{4,20},{5,21},{6,22},{7,23},{8,24},{9,... | collective-permute-start | bytes 1572872 | tf_op jit(solution)/shard_map/ppermute | solution.py:20
  (226 other events, 4188.8 us)
Sparse Core Ops, SparseCore 0:
  20.0 30.3 all-gather.15
  78.8 64.4 all-gather.13
  145.4 105.3 all-gather.17
  253.0 58.0 all-gather.19
  325.7 25.7 all-gather.23
  355.5 61.2 all-gather.21
  418.4 105.3 all-gather.25
  525.4 57.4 all-gather.11
  829.6 55.0 reduce-scatter.22
  886.8 56.0 reduce-scatter.20
  953.3 25.6 reduce-scatter.14
  981.3 25.8 reduce-scatter.12
  1010.0 100.8 reduce-scatter.18
  1113.7 102.7 reduce-scatter.16
  1219.2 60.7 reduce-scatter.10
  1282.8 60.2 reduce-scatter.8

commit v2 on v1

--- a/solution.py
+++ b/solution.py
@@ -1,6 +1,10 @@
+import functools
+
 import jax
 import jax.numpy as jnp
 from jax import lax
+from jax.experimental import pallas as pl
+from jax.experimental.pallas import tpu as pltpu
 from jax.sharding import PartitionSpec as P
 
 HEADS = 16
@@ -26,12 +30,77 @@
     return block
 
 
+def orders(stages):
+    outer = stages[:-1]
+    turned = outer[1:] + outer[:1]
+    codes = []
+    for some in (outer, turned):
+        order = [0]
+        for stage in some:
+            order = order + [o ^ (1 << stages.index(stage)) for o in order]
+        codes.append(order)
+    return outer, turned, codes[0], codes[1]
+
+
+def blocks_in_order(value, source, target):
+    size = value.shape[0] // len(source)
+    return jnp.concatenate(
+        [value[size * source.index(c) : size * (source.index(c) + 1)] for c in target], axis=0
+    )
+
+
+def join_kernel(order_ref, left, right, far_left, far_right, whole):
+    half = left.shape[1]
+    whole[0, :, :half] = left[...]
+    whole[0, :, half:] = right[...]
+    whole[1, :, :half] = far_left[...]
+    whole[1, :, half:] = far_right[...]
+
+
+def join_halves(halves, order):
+    rows, half = halves[0].shape
+    tile = rows // len(order)
+    plain = pl.BlockSpec((tile, half), lambda i, order: (i, 0))
+    turned = pl.BlockSpec((tile, half), lambda i, order: (order[i], 0))
+    whole = pl.pallas_call(
+        join_kernel,
+        grid_spec=pltpu.PrefetchScalarGridSpec(
+            num_scalar_prefetch=1,
+            grid=(len(order),),
+            in_specs=[plain, turned, plain, turned],
+            out_specs=pl.BlockSpec((2, tile, 2 * half), lambda i, order: (0, i, 0)),
+        ),
+        out_shape=jax.ShapeDtypeStruct((2, rows, 2 * half), halves[0].dtype),
+        compiler_params=pltpu.CompilerParams(vmem_limit_bytes=32 << 20),
+    )(jnp.array(order, jnp.int32), *halves)
+    return whole.reshape(2 * rows, 2 * half)
+
+
+def spread_rows(block, stages, tie=None):
+    outer, turned, codes, turned_codes = orders(stages)
+    half = block.shape[1] // 2
+    left, right = block[:, :half], block[:, half:]
+    for number, (stage, other) in enumerate(zip(outer, turned)):
+        left = jnp.concatenate([left, swap(left, stage)], axis=0)
+        right = jnp.concatenate([right, swap(right, other)], axis=0)
+        if number == len(outer) - 1 and tie is not None:
+            left, right, tie = lax.optimization_barrier((left, right, tie))
+    halves = (left, right, swap(left, stages[-1]), swap(right, stages[-1]))
+    return join_halves(halves, [turned_codes.index(c) for c in codes]), tie
+
+
 def collapse(send, keep, stages):
-    for stage in stages[::-1]:
-        total = keep + swap(send.astype(BF16), stage).astype(F32)
-        half = total.shape[0] // 2
-        keep, send = total[:half], total[half:]
-    return total
+    outer, turned, codes, turned_codes = orders(stages)
+    total = keep + swap(send.astype(BF16), stages[-1]).astype(F32)
+    half = total.shape[1] // 2
+    left, right = total[:, :half], blocks_in_order(total[:, half:], codes, turned_codes)
+    for stage, other in zip(outer[::-1], turned[::-1]):
+        size = left.shape[0] // 2
+        left_in = swap(left[size:].astype(BF16), stage)
+        right_in = swap(right[size:].astype(BF16), other)
+        left = left[:size] + left_in.astype(F32)
+        right = right[:size] + right_in.astype(F32)
+    return jnp.concatenate([left, right], axis=1)
 
 
 def reduced_product(left, right, stages):
@@ -83,6 +152,96 @@
     return head_norm(o, gain_head)
 
 
+def place_mixer_kernel(wide, columns, corners, *refs):
+    sources, (query_ref, forget_ref, input_ref, out_ref) = refs[:-4], refs[-4:]
+    step = pl.program_id(0)
+    head = wide // (columns.shape[0] // len(sources))
+    for j, source in enumerate(sources):
+        for kind, target in enumerate((query_ref, forget_ref, input_ref)):
+            for t in range(wide // head):
+                at = pl.multiple_of(columns[j * (wide // head) + t], head)
+                low = kind * wide + t * head
+                target[:, pl.ds(at, head)] = source[:, low : low + head].astype(F32)
+        row = pl.multiple_of(corners[2 * j], source.shape[0])
+        column = pl.multiple_of(corners[2 * j + 1] + step * wide, wide)
+        out_ref[pl.ds(row, source.shape[0]), pl.ds(column, wide)] = source[
+            :, 3 * wide : 4 * wide
+        ].astype(F32)
+
+
+def place_mixer(sources, columns, corners, tile, model_width):
+    rows, total = sources[0].shape
+    return pl.pallas_call(
+        functools.partial(place_mixer_kernel, total // 4),
+        grid_spec=pltpu.PrefetchScalarGridSpec(
+            num_scalar_prefetch=2,
+            grid=(rows // tile,),
+            in_specs=[pl.BlockSpec((tile, total), lambda i, *_: (i, 0))] * len(sources),
+            out_specs=[pl.BlockSpec((tile, model_width), lambda i, *_: (i, 0))] * 3
+            + [pl.BlockSpec((rows, model_width), lambda i, *_: (0, 0))],
+        ),
+        out_shape=[jax.ShapeDtypeStruct((rows, model_width), F32)] * 4,
+        compiler_params=pltpu.CompilerParams(vmem_limit_bytes=48 << 20),
+    )(columns, corners, *sources)
+
+
+def place_columns_kernel(shards, ident_ref, *refs):
+    sources, targets = refs[:-2], refs[-2:]
+    values = [source[...] for source in sources]
+    bit = 1
+    while bit < len(values):
+        on = (ident_ref[0] & bit) != 0
+        values = [jnp.where(on, values[j ^ bit], values[j]) for j in range(len(values))]
+        bit *= 2
+    wide = values[0].shape[1] // (2 * shards)
+    for kind, target in enumerate(targets):
+        parts = []
+        for s in range(shards):
+            low = (kind * shards + s) * wide
+            parts += [value[:, low : low + wide] for value in values]
+        target[...] = jnp.concatenate(parts, axis=1).astype(F32)
+
+
+def place_columns(sources, ident, shards):
+    rows, total = sources[0].shape
+    tile = 64
+    width = len(sources) * total // 2
+    return pl.pallas_call(
+        functools.partial(place_columns_kernel, shards),
+        grid_spec=pltpu.PrefetchScalarGridSpec(
+            num_scalar_prefetch=1,
+            grid=(rows // tile,),
+            in_specs=[pl.BlockSpec((tile, total), lambda i, *_: (i, 0))] * len(sources),
+            out_specs=[pl.BlockSpec((tile, width), lambda i, *_: (i, 0))] * 2,
+        ),
+        out_shape=[jax.ShapeDtypeStruct((rows, width), F32)] * 2,
+        compiler_params=pltpu.CompilerParams(vmem_limit_bytes=48 << 20),
+    )(ident[None], *sources)
+
+
+def place_rows_kernel(ident_ref, *refs):
+    sources, target = refs[:-1], refs[-1]
+    for j, source in enumerate(sources):
+        at = pl.multiple_of((ident_ref[0] ^ j) * source.shape[0], 8)
+        target[pl.ds(at, source.shape[0]), :] = source[...].astype(F32)
+
+
+def place_rows(sources, ident):
+    rows, width = sources[0].shape
+    tile = 512
+    return pl.pallas_call(
+        place_rows_kernel,
+        grid_spec=pltpu.PrefetchScalarGridSpec(
+            num_scalar_prefetch=1,
+            grid=(width // tile,),
+            in_specs=[pl.BlockSpec((rows, tile), lambda i, *_: (0, i))] * len(sources),
+            out_specs=pl.BlockSpec((rows * len(sources), tile), lambda i, *_: (0, i)),
+        ),
+        out_shape=jax.ShapeDtypeStruct((rows * len(sources), width), F32),
+        compiler_params=pltpu.CompilerParams(vmem_limit_bytes=48 << 20),
+    )(ident[None], *sources)
+
+
 def split_weights(
     w_query, w_forget, w_input, w_out, w_gate, w_up, w_down, ident, shards, group, sharing
 ):
@@ -101,12 +260,14 @@
             parts.append(lax.dynamic_slice_in_dim(weight, number * head, head, 1))
         return parts
 
-    qfv = jnp.concatenate(
-        head_columns(w_query) + head_columns(w_forget) + head_columns(w_input), axis=1
-    )
     width = model_width // sharing
     out = lax.dynamic_slice(
         w_out, (cluster * each * head, member * width), (each * head, width)
+    )
+    wide = per_device * head
+    out = jnp.concatenate([out[:, b : b + wide] for b in range(0, width, wide)], axis=0)
+    mix = jnp.concatenate(
+        head_columns(w_query) + head_columns(w_forget) + head_columns(w_input) + [out], axis=1
     )
     local_ff = w_down.shape[0]
     own_ff = local_ff // group
@@ -119,7 +280,7 @@
 
     gate_up = jnp.concatenate(ff_columns(w_gate) + ff_columns(w_up), axis=1)
     down = lax.dynamic_slice_in_dim(w_down, own_ff * ident, own_ff, 0)
-    return (qfv, out, gate_up, down)
+    return (mix, gate_up, down)
 
 
 def local(
@@ -181,16 +342,15 @@
     plane_place = places(stages)
     rep_place = places(rep_stages)
 
-    block_rows = micro * reps
-    numbers = lax.all_gather(
-        jnp.concatenate([deal_order[:, None], lengths], axis=1), "rep", axis=0, tiled=True
-    )
-    block_order = numbers[:, 0] % block_rows
-    block_lengths = numbers[:, 1:]
     gains = jnp.stack([norm_mix[0], norm_ffn[0], norm_head[0], gate_gap[0]])
-    gains = lax.all_gather(gains, ("section", "shard"), axis=0, tiled=False)
-    gains = gains.reshape(2, shards, 4, -1).transpose(0, 2, 1, 3).reshape(2, 4, model_width)
-    gains = gains.astype(F32)
+    shard_stages = []
+    distance = shards // 2
+    while distance:
+        shard_stages.append(("shard", distance))
+        distance //= 2
+    gains = spread(gains[None], shard_stages)
+    gains = gains[places(shard_stages)[jnp.arange(shards) ^ shard]]
+    gains = spread(gains[None], [("section", 1)])[jnp.arange(2) ^ section]
 
     local_weights = (w_query[0], w_forget[0], w_input[0], w_out[0], w_gate[0], w_up[0], w_down[0])
     kept = split_weights(*local_weights, ident, shards, group, sharing)
@@ -198,27 +358,47 @@
         *local_weights, (1 - section) * reps + rep, shards, group, sharing
     )
     received = [swap(piece, ("section", 1)) for piece in sent]
-    layer_pieces = (
-        [jnp.where(on_first, a, b) for a, b in zip(kept, received)],
-        [jnp.where(on_first, b, a) for a, b in zip(kept, received)],
-    )
-    layer_weights = []
+    mix_first, gate_up_first, down_first = [
+        jnp.where(on_first, a, b) for a, b in zip(kept, received)
+    ]
+    mix_second, gate_up_second, down_second = [
+        jnp.where(on_first, b, a) for a, b in zip(kept, received)
+    ]
+
+    mix_first, gains = lax.optimization_barrier((mix_first, gains))
+
+    def over_shard(piece):
+        return lax.all_gather(piece, "shard", axis=0, tiled=True)
+
     member = ident % sharing
-    for layer in range(2):
-        qfv, out, gate_up, down = [
-            lax.all_gather(piece, "shard", axis=0, tiled=True) for piece in layer_pieces[layer]
-        ]
-        wide = spread(out[None], share_stages)
-        wide = wide[places(share_stages)[jnp.arange(sharing) ^ member]]
-        wide = jnp.swapaxes(wide, 0, 1).reshape(shards * each * head, model_width)
-        out = lax.dynamic_slice_in_dim(wide, member * per_device * head, per_device * head, 0)
-        layer_weights.append((qfv, out, gate_up, down))
-
     cluster = ident // sharing
-    own_heads = []
-    for t in range(per_device):
-        at = member * per_device + t
-        own_heads.append(per_shard * (at // each) + cluster * each + at % each)
+    wide = per_device * head
+    local_rows = model_width // shards
+
+    def mixer_weights(mix):
+        mix = over_shard(mix)
+        out = mix[:, 3 * wide :].reshape(shards, -1, each * head, wide)
+        out = out.transpose(0, 2, 1, 3).reshape(shards * each * head, model_width // sharing)
+        out = spread(out[None], share_stages)
+        out = out[places(share_stages)[jnp.arange(sharing) ^ member]]
+        out = jnp.swapaxes(out, 0, 1).reshape(shards * each * head, model_width)
+        out = lax.dynamic_slice_in_dim(out, member * wide, wide, 0)
+        return (mix[:, : 3 * wide], out)
+
+    block_rows = micro * reps
+    numbers = jnp.concatenate([deal_order[:, None], lengths], axis=1)
+    numbers = spread(numbers[None], rep_stages)[rep_place[jnp.arange(reps) ^ rep]]
+    numbers = numbers.reshape(block_rows, -1)
+    block_order = numbers[:, 0] % block_rows
+    block_lengths = numbers[:, 1:]
+    gains = gains.reshape(2, shards, 4, -1).transpose(0, 2, 1, 3).reshape(2, 4, model_width)
+    gains = gains.astype(F32)
+
+    def head_number(device, t):
+        at = device % sharing * per_device + t
+        return per_shard * (at // each) + device // sharing * each + at % each
+
+    own_heads = [head_number(ident, t) for t in range(per_device)]
 
     def own_channels(vector):
         return jnp.stack(
@@ -242,8 +422,10 @@
     dealt = arrivals[slot]
     own_cotangent = jnp.where(on_first, one_way(rows[0], 1), rows[1]).astype(F32)
 
-    def forward(x_own, normed_all, weights, gain):
-        qfv_weight, out_weight, gate_up_weight, down_weight = weights
+    d_down_second, _ = spread_rows((own_cotangent * valid_own).astype(BF16), stages)
+
+    def forward(x_own, normed_all, mix, gate_up_piece, gain, down_pieces=None, down_weight=None):
+        qfv_weight, out_weight = mixer_weights(mix)
         qfv = product(normed_all, qfv_weight).reshape(group, length, 3, per_device, head)
         mixed, pull_mix = jax.vjp(
             lambda a, b, c, d, e: mixer(a, b, c, d, e, valid_mask, same),
@@ -254,77 +436,148 @@
             own_channels(gain[2]),
         )
         mixed = mixed.reshape(group * length, per_device * head).astype(BF16)
+        if down_weight is None:
+            mixed, down_pieces = lax.optimization_barrier((mixed, down_pieces))
+            down_weight = over_shard(down_pieces).reshape(shards, 2, -1, model_width)
+            down_weight = [down_weight[:, i].reshape(-1, model_width) for i in range(2)]
+            gate_up_weight, tied = over_shard(gate_up_piece), None
+        else:
+            down_weight = [down_weight]
+            gate_up_weight = tied = over_shard(gate_up_piece)
         resid_mid = x_own + reduced_product(mixed, out_weight, stages)
         mid_value, pull_mid = jax.vjp(rms_norm, resid_mid, gain[1])
-        normed_mid = spread(mid_value.astype(BF16), stages)
+        normed_mid, tied = spread_rows(mid_value.astype(BF16), stages, tied)
+        early = ()
+        if tied is not None:
+            gate_up_weight = tied
+            early = product_t(d_down_second, down_weight[0])
+            normed_mid, early = lax.optimization_barrier((normed_mid, early))
         gate_up = product(normed_mid, gate_up_weight)
         half = gate_up.shape[1] // 2
         hidden, pull_act = jax.vjp(
             lambda a, b: jax.nn.silu(a) * b, gate_up[:, :half], gate_up[:, half:]
         )
         hidden = hidden.astype(BF16)
-        result = (resid_mid + reduced_product(hidden, down_weight, stages)) * valid_own
-        return result.astype(BF16), (normed_all, mixed, normed_mid, hidden, pull_mix, pull_mid, pull_act)
+        if tied is None:
+            hidden, early = lax.optimization_barrier((hidden, d_down_second))
+        result = (resid_mid + reduced_product(hidden, down_weight[0], stages)) * valid_own
+        weights = (qfv_weight, out_weight, gate_up_weight, down_weight[0])
+        kept = (normed_all, mixed, normed_mid, hidden, pull_mix, pull_mid, pull_act)
+        return result.astype(BF16), weights, kept, down_weight[-1], early
 
     def transposed_sum(left, right, stages):
         half = left.shape[0] // 2
         return collapse(product_t(left[half:], right), product_t(left[:half], right), stages)
 
-    def backward(grad_out, weights, kept_state, pull_in):
+    def to_owner(term):
+        return lax.psum_scatter(term, "shard", scatter_dimension=0, tiled=True)
+
+    def backward(grad_out, d_down, d_hidden, weights, kept_state, pull_in, earlier):
         qfv_weight, out_weight, gate_up_weight, down_weight = weights
         normed_all, mixed, normed_mid, hidden, pull_mix, pull_mid, pull_act = kept_state
+        last = d_hidden is None
         d_out = grad_out * valid_own
-        d_down = spread(d_out.astype(BF16), stages)
-        d_hidden = product_t(d_down, down_weight)
+        if last:
+            d_down, _ = spread_rows(d_out.astype(BF16), stages)
+            d_hidden = product_t(d_down, down_weight)
+            term_down = weight_term(hidden, d_down)
+            earlier, term_down = lax.optimization_barrier((earlier, term_down))
+        else:
+            term_down = weight_term(hidden, d_down)
+            d_hidden, term_down = lax.optimization_barrier((d_hidden, term_down))
         d_gate_up = jnp.concatenate(pull_act(d_hidden), axis=1).astype(BF16)
-        term_down = weight_term(hidden, d_down)
         term_gate_up = weight_term(normed_mid, d_gate_up)
+        d_gate_up, term_gate_up, earlier = lax.optimization_barrier(
+            (d_gate_up, term_gate_up, earlier)
+        )
+        summed_down = to_owner(term_down)
+        summed_gate_up = to_owner(term_gate_up)
         more, grad_ffn = pull_mid(transposed_sum(d_gate_up, gate_up_weight, stages))
         d_resid = d_out + more
-        d_attn = spread(d_resid.astype(BF16), stages)
+        d_attn = d_resid.astype(BF16)
+        if not last:
+            d_attn, summed_down = lax.optimization_barrier((d_attn, summed_down))
+        d_attn, _ = spread_rows(d_attn, stages)
         d_mixed = product_t(d_attn, out_weight).reshape(group, length, per_device, head)
         d_q, d_f, d_v, grad_gap, grad_head = pull_mix(d_mixed)
         d_qfv = jnp.stack([d_q, d_f, d_v], axis=2).astype(BF16)
-        d_qfv = d_qfv.reshape(group * length, 3 * per_device * head)
-        term_out = weight_term(mixed, d_attn)
-        term_qfv = weight_term(normed_all, d_qfv)
+        d_qfv = d_qfv.reshape(group * length, 3 * wide)
+        term_out = spread(weight_term(mixed, d_attn)[None], share_stages)
+        term_out = term_out[places(share_stages)[jnp.arange(sharing) ^ member]]
+        part = model_width // sharing
+        term_out = lax.dynamic_slice_in_dim(
+            term_out.reshape(sharing * wide, model_width), member * part, part, 1
+        )
+        term_out = term_out.reshape(shards, each * head, -1, wide).transpose(0, 2, 1, 3)
+        term_mix = jnp.concatenate(
+            [weight_term(normed_all, d_qfv), term_out.reshape(model_width, wide)], axis=1
+        )
+        d_qfv, term_mix, summed_gate_up = lax.optimization_barrier(
+            (d_qfv, term_mix, summed_gate_up)
+        )
+        summed_mix = to_owner(term_mix)
         more, grad_mix = pull_in(transposed_sum(d_qfv, qfv_weight, stages))
         d_x = d_resid + more
-        wide = spread(term_out[None], share_stages)
-        wide = wide[places(share_stages)[jnp.arange(sharing) ^ member]]
-        wide = wide.reshape(sharing * per_device * head, model_width)
-        term_out = lax.dynamic_slice_in_dim(
-            wide, member * (model_width // sharing), model_width // sharing, 1
-        )
         small = jnp.zeros((4, model_width), F32).at[0].set(grad_mix).at[1].set(grad_ffn)
         for t in range(per_device):
             column = own_heads[t] * head
             small = lax.dynamic_update_slice(small, grad_head[t][None], (2, column))
             small = lax.dynamic_update_slice(small, grad_gap[t][None], (3, column))
-        return d_x, (term_qfv, term_out, term_gate_up, term_down), small
+        return d_x, (summed_mix, summed_gate_up, summed_down), small, earlier
 
     dealt_f32 = dealt.astype(F32)
     normed_first = rms_norm(dealt_f32, gains[0, 0]).astype(BF16)
     _, pull_in_first = jax.vjp(rms_norm, dealt_f32[0], gains[0, 0])
-    first, kept_first = forward(
+    first, weights_first, kept_first, down_second, d_down_second = forward(
         dealt_f32[0],
         normed_first.reshape(group * length, model_width),
-        layer_weights[0],
+        mix_first,
+        gate_up_first,
         gains[0],
+        down_pieces=jnp.concatenate([down_first, down_second], axis=0),
     )
     first_f32 = first.astype(F32)
     normed_second, pull_in_second = jax.vjp(rms_norm, first_f32, gains[1, 0])
-    second, kept_second = forward(
-        first_f32, spread(normed_second.astype(BF16), stages), layer_weights[1], gains[1]
-    )
-    d_first, terms_second, small_second = backward(
-        own_cotangent, layer_weights[1], kept_second, pull_in_second
-    )
-    d_dealt, terms_first, small_first = backward(
-        d_first.astype(BF16).astype(F32), layer_weights[0], kept_first, pull_in_first
-    )
+    second, weights_second, kept_second, _, d_hidden_second = forward(
+        first_f32,
+        spread_rows(normed_second.astype(BF16), stages)[0],
+        mix_second,
+        gate_up_second,
+        gains[1],
+        down_weight=down_second,
+    )
+    d_first, (mix_1, gate_up_1, down_1), small_second, _ = backward(
+        own_cotangent,
+        d_down_second,
+        d_hidden_second,
+        weights_second,
+        kept_second,
+        pull_in_second,
+        (),
+    )
+    d_dealt, (mix_0, gate_up_0, down_0), small_first, mix_1 = backward(
+        d_first.astype(BF16).astype(F32), None, None, weights_first, kept_first, pull_in_first, mix_1
+    )
+
+    def begin_collect(of_first, of_second):
+        own = jnp.where(on_first, of_first, of_second)
+        sent = jnp.where(on_first, of_second, of_first)
+        return own, swap(sent, ("section", 1)), swap(own, rep_stages[0])
+
+    def collect(own, other, across):
+        blocks = {0: own, reps: other, rep_stages[0][1]: across}
+        blocks[reps ^ rep_stages[0][1]] = swap(other, rep_stages[0])
+        for stage in rep_stages[1:]:
+            blocks.update({code ^ stage[1]: swap(blocks[code], stage) for code in list(blocks)})
+        return [blocks[code] for code in range(group)]
+
+    begun = begin_collect(gate_up_0, gate_up_1)
+    d_dealt, begun = lax.optimization_barrier((d_dealt, begun))
+    gate, up = place_columns(collect(*begun), ident, shards)
+    down = place_rows(collect(*begin_collect(down_0, down_1)), ident)
 
     all_grads = spread(d_dealt.astype(BF16)[None], stages)
+    mix_0, all_grads, gate, up, down = lax.optimization_barrier((mix_0, all_grads, gate, up, down))
     inverse = jnp.argsort(block_order)
     own_dealt = lax.dynamic_slice_in_dim(inverse, rep * micro, micro, 0)
     own_holder = (own_dealt % micro) * reps + own_dealt // micro
@@ -334,32 +587,6 @@
         1, micro * length, model_width
     )
 
-    absolute = plane_place[jnp.arange(group) ^ ident]
-    pieces = []
-    for number in range(4):
-        summed = [
-            lax.psum_scatter(terms[number], "shard", scatter_dimension=0, tiled=True)
-            for terms in (terms_first, terms_second)
-        ]
-        keep = jnp.where(on_first, summed[0], summed[1])[None]
-        send = jnp.where(on_first, summed[1], summed[0])[None]
-        pair = jnp.concatenate([keep, swap(send, ("section", 1))], axis=0)
-        pieces.append(spread(pair, rep_stages)[absolute].astype(F32))
-    qfv, out, gate_up, down = pieces
-    local_rows = qfv.shape[1]
-    clusters = group // sharing
-    qfv = qfv.reshape(clusters, sharing, local_rows, 3, per_device, head)
-    qfv = qfv.transpose(3, 2, 1, 4, 0, 5).reshape(
-        3, local_rows, shards, each, clusters, head
-    )
-    qfv = qfv.transpose(0, 1, 2, 4, 3, 5).reshape(3, local_rows, model_width)
-    out = out.reshape(clusters, sharing, each * head, model_width // sharing)
-    out = out.transpose(0, 2, 1, 3).reshape(local_rows, model_width)
-    own_ff = w_down.shape[1] // group
-    gate_up = gate_up.reshape(group, local_rows, 2, shards, own_ff)
-    gate_up = gate_up.transpose(2, 1, 3, 0, 4).reshape(2, local_rows, -1)
-    down = down.reshape(-1, model_width)
-
     small = jnp.stack([small_first, small_second])
     for stage in stages:
         small = small + swap(small, stage)
@@ -367,14 +594,25 @@
     small = jnp.sum(lax.all_gather(small, "shard", axis=0, tiled=False), axis=0)
     small = lax.dynamic_slice_in_dim(small, shard * local_rows, local_rows, 1)
 
+    sources = [ident ^ code for code in range(group)]
+    columns = jnp.stack(
+        [head_number(device, t) * head for device in sources for t in range(per_device)]
+    )
+    corners = []
+    for device in sources:
+        corners += [device // sharing * each * head, device % sharing * (model_width // sharing)]
+    query, forget, into, out = place_mixer(
+        collect(*begin_collect(mix_0, mix_1)), columns, jnp.stack(corners), each * head, model_width
+    )
+
     return (
         boundary_out,
-        qfv[0][None],
-        qfv[1][None],
-        qfv[2][None],
+        query[None],
+        forget[None],
+        into[None],
         out[None],
-        gate_up[0][None],
-        gate_up[1][None],
+        gate[None],
+        up[None],
         down[None],
         small[0][None],
         small[2][None],

time: 1670 us -> 1270 us (0.76)
  waiting for transfers between devices: 844 us -> 635 us
  local copies, waits for them, and re-layouts: 301 us -> 144 us
  Pallas kernels: 0 us -> 45.1 us
  other arithmetic: 152 us -> 111 us
  blocking collectives: 50.2 us -> 14 us
  matrix products: 199 us -> 179 us
  starting transfers between devices: 93.3 us -> 111 us
    reduce_scatter x8 -> x6, waiting for transfers between devices: 202 us -> 37 us  [to_owner(): return lax.psum_scatter(term, 'shard', scatter_dimension=0, tiled=True)]
    ppermute x73 -> x123, waiting for transfers between devices: 585 us -> 463 us  [swap(): lax.ppermute(block, axis, [(i, i ^ distance) for i in range(lax.axis_size...]
    slice x37 -> x51, local copies, waits for them, and re-layouts: 103 us -> 12.9 us  [the longest x1 5.27 us: forward(): down_weight = [down_weight[:, i].reshape(-1, model_width) for i in range(2)]]
    all_gather x8 -> x5, waiting for transfers between devices: 56.9 us -> 126 us  [over_shard(): return lax.all_gather(piece, 'shard', axis=0, tiled=True)]
    concatenate x31 -> x14, other arithmetic: 67.3 us -> 22.2 us  [spread(): block = jnp.concatenate([block, swap(block, stage)], axis=0)]
    pallas_call x0 -> x10, Pallas kernels: none -> 45.1 us  [the longest x7 14.6 us: join_halves(): pl.pallas_call(join_kernel, grid_spec=pltpu.PrefetchScalarGridSpec(num_sc...]
    all_gather x2 -> x0, blocking collectives: 36.3 us -> none  [the longest x1 31.3 us: local(): gains = lax.all_gather(gains, ('section', 'shard'), axis=0, tiled=False)]
    transpose x4, local copies, waits for them, and re-layouts: 37.5 us -> 8.29 us  [the longest x2 7.95 us: mixer_weights(): out = jnp.swapaxes(out, 0, 1).reshape(shards * each * head, model_width)]
  transfers between devices with their start and end apart: 92 -> 137, of which waited for: 51 -> 74; matrix products, arithmetic and copies ran while one was open for 29% -> 29% of each run, Pallas kernels for 0% -> 3%
where the time goes in v2:
time: 1270 us; the launch traced here: 1260 us
  waiting for transfers between devices  635 us (50%)
  matrix products  179 us (14%)
  local copies, waits for them, and re-layouts  144 us (11%)
  starting transfers between devices  111 us (9%)
  other arithmetic  111 us (9%)
  Pallas kernels  45.1 us (4%)
  between operations  17.6 us (1%)
  blocking collectives  14 us (1%)
    ppermute x123, waiting for transfers between devices, swap(): lax.ppermute(block, axis, [(i, i ^ distance) for i in range(lax.axis_size...  463 us
    all_gather x5, waiting for transfers between devices, over_shard(): return lax.all_gather(piece, 'shard', axis=0, tiled=True)  126 us
    ppermute x123, starting transfers between devices, swap(): lax.ppermute(block, axis, [(i, i ^ distance) for i in range(lax.axis_size...  101 us
    dot_general x12, matrix products, product_t(): lax.dot_general(left, right, (((1,), (1,)), ((), ())), preferred_element_...  56.2 us
    dot_general x12, matrix products, product(): return jnp.dot(left, right, preferred_element_type=F32)  48.6 us
    dot_general x8, matrix products, weight_term(): lax.dot_general(act_rows, grad_rows, (((0,), (0,)), ((), ())), preferred_...  47.8 us
    reduce_scatter x6, waiting for transfers between devices, to_owner(): return lax.psum_scatter(term, 'shard', scatter_dimension=0, tiled=True)  37 us
    unnamed x269, local copies, waits for them, and re-layouts  36.2 us
  transfers between devices with their start and end apart: 137, of which 74 were waited for; matrix products, arithmetic and copies ran while one was open for 29% of the time, Pallas kernels for 3%

profile of v2, /device:TPU:0, one launch (start us, length us, event | category | flops | bytes accessed | tf_op | source)
XLA Modules:
  0.0 1256.8 jit_solution(194161405659490013)
XLA Ops:
  31.3 14.5 %collective-permute-done.9 = bf16[1,4,4,512]{3,2,1,0:T(4,128)(2,1)S(1)} collective-permute-done((bf16[1,4,4,512]{3,2,1,0:T(4,128)(2,1)S(1)}, bf16[1,4,4,512]{3,2,1,0:T(4,128)(2,1)S(1)}, u32[]{:S(2)}, u32[]{:S(2)}) %collective-permute-start.9) | collective-permute-done | bytes 16416 | tf_op jit(solution)/shard_map/ppermute | solution.py:20
  86.4 18.8 %collective-permute-done.4 = bf16[2,128,2048]{2,1,0:T(8,128)(2,1)S(1)} collective-permute-done((bf16[2,128,2048]{2,1,0:T(8,128)(2,1)S(1)}, bf16[2,128,2048]{2,1,0:T(8,128)(2,1)S(1)}, u32[]{:S(2)}, u32[]{:S(2)}) %collective-permute-start.4) | collective-permute-done | bytes 1048608 | tf_op jit(solution)/shard_map/ppermute | solution.py:20
  109.5 12.1 collective-permute-done.23
  195.5 9.9 collective-permute-done.15
  229.1 13.2 %collective-permute-done.19 = bf16[128,1024]{1,0:T(8,128)(2,1)S(1)} collective-permute-done((bf16[128,1024]{1,0:T(8,128)(2,1)S(1)}, bf16[128,1024]{1,0:T(8,128)(2,1)S(1)}, u32[]{:S(2)}, u32[]{:S(2)}) %collective-permute-start.19) | collective-permute-done | bytes 262176 | tf_op jit(solution)/shard_map/ppermute | solution.py:20
  258.6 10.5 fusion.199
  271.6 73.9 %all-gather.10.cloned.1.call-done = bf16[1408,2048]{1,0:T(8,128)(2,1)} async-done(((bf16[352,2048]{1,0:T(8,128)(2,1)}), bf16[1408,2048]{1,0:T(8,128)(2,1)}) %all-gather.10.cloned.1.call-update) | async-done | bytes 5767184 | tf_op jit(solution)/shard_map/all_gather | solution.py:371
  366.5 10.8 collective-permute-done.33
  398.0 35.3 %all-gather.12.cloned.1.call-done = bf16[2048,1024]{1,0:T(8,128)(2,1)} async-done(((bf16[512,1024]{1,0:T(8,128)(2,1)}), bf16[2048,1024]{1,0:T(8,128)(2,1)}) %all-gather.12.cloned.1.call-update) | async-done | bytes 4194320 | tf_op jit(solution)/shard_map/all_gather | solution.py:371
  487.4 11.1 collective-permute-done.45
  517.7 10.2 collective-permute-done.48
  528.1 16.4 %all-gather.14.cloned.1.call-done = bf16[2048,1408]{1,0:T(8,128)(2,1)} async-done(((bf16[512,1408]{1,0:T(8,128)(2,1)}), bf16[2048,1408]{1,0:T(8,128)(2,1)}) %all-gather.14.cloned.1.call-update) | async-done | bytes 5767184 | tf_op jit(solution)/shard_map/all_gather | solution.py:371
  661.0 10.0 collective-permute-done.59
  718.1 14.9 %reduce-scatter.9.cloned.1.call-done = bf16[512,1408]{1,0:T(8,128)(2,1)} async-done(((bf16[2048,1408]{1,0:T(8,128)(2,1)}), bf16[512,1408]{1,0:T(8,128)(2,1)}) %reduce-scatter.9.cloned.1.call-update) | async-done | bytes 1441808 | tf_op jit(solution)/shard_map/reduce_scatter | solution.py:473
  746.4 10.8 collective-permute-done.68
  779.9 9.6 collective-permute-done.71
  805.6 10.8 convolution_convert_fusion
  816.4 22.0 %reduce-scatter.11.cloned.1.call-done = bf16[512,1024]{1,0:T(8,128)(2,1)} async-done(((bf16[2048,1024]{1,0:T(8,128)(2,1)}), bf16[512,1024]{1,0:T(8,128)(2,1)}) %reduce-scatter.11.cloned.1.call-update) | async-done | bytes 1048592 | tf_op jit(solution)/shard_map/reduce_scatter | solution.py:473
  858.1 10.8 collective-permute-done.79
  889.3 10.1 collective-permute-done.82
  962.9 9.5 collective-permute-done.91
  987.9 25.8 %collective-permute-done.93.refs_4_ = bf16[512,1408]{1,0:T(8,128)(2,1)} collective-permute-done((bf16[512,1408]{1,0:T(8,128)(2,1)S(1)}, bf16[512,1408]{1,0:T(8,128)(2,1)}, u32[]{:S(2)}, u32[]{:S(2)}) %collective-permute-start.93) | collective-permute-done | bytes 1441824 | tf_op jit(solution)/shard_map/ppermute | solution.py:20
  1017.2 11.4 collective-permute-done.95
  1045.3 27.3 %collective-permute-done.104.refs_2_ = bf16[176,2048]{1,0:T(8,128)(2,1)} collective-permute-done((bf16[176,2048]{1,0:T(8,128)(2,1)S(1)}, bf16[176,2048]{1,0:T(8,128)(2,1)}, u32[]{:S(2)}, u32[]{:S(2)}) %collective-permute-start.104) | collective-permute-done | bytes 720928 | tf_op jit(solution)/shard_map/ppermute | solution.py:20
  1072.7 15.4 %collective-permute-done.108.refs_6_ = bf16[176,2048]{1,0:T(8,128)(2,1)} collective-permute-done((bf16[176,2048]{1,0:T(8,128)(2,1)S(1)}, bf16[176,2048]{1,0:T(8,128)(2,1)}, u32[]{:S(2)}, u32[]{:S(2)}) %collective-permute-start.108) | collective-permute-done | bytes 720928 | tf_op jit(solution)/shard_map/ppermute | solution.py:20
  1093.0 19.7 %collective-permute-done.101.refs_6_ = bf16[512,1408]{1,0:T(8,128)(2,1)} collective-permute-done((bf16[512,1408]{1,0:T(8,128)(2,1)}, bf16[512,1408]{1,0:T(8,128)(2,1)}, u32[]{:S(2)}, u32[]{:S(2)}) %collective-permute-start.101) | collective-permute-done | bytes 1441824 | tf_op jit(solution)/shard_map/ppermute | solution.py:20
  1124.1 13.9 %shard_map.371 = (f32[512,5632]{1,0:T(8,128)}, f32[512,5632]{1,0:T(8,128)}) custom-call(s32[1]{0:T(128)} %bitcast.149.ident_ref, bf16[512,1408]{1,0:T(8,128)(2,1)S(1)} %get-tuple-element.130.refs_0_, bf16[512,1408]{1,0:T(8,128)(2,1)} %collective-permute-done.98.refs_1_, bf16[512,1408]{1,0:T(8,128)(2,1)} %collective-permute-done.94.refs_2_, ...), custom_call_target="tpu_custom_call" | custom-call | tf_op jit(solution)/shard_map/pallas_call | solution.py:209
  1147.0 23.7 %collective-permute-done.123 = f32[2,4,2048]{2,1,0:T(4,128)S(1)} collective-permute-done((f32[2,4,2048]{2,1,0:T(4,128)S(1)}, f32[2,4,2048]{2,1,0:T(4,128)S(1)}, u32[]{:S(2)}, u32[]{:S(2)}) %collective-permute-start.123) | collective-permute-done | bytes 65568 | tf_op jit(solution)/shard_map/ppermute | solution.py:20
  1182.2 16.2 %collective-permute-done.117.refs_2_ = bf16[512,1024]{1,0:T(8,128)(2,1)S(1)} collective-permute-done((bf16[512,1024]{1,0:T(8,128)(2,1)S(1)}, bf16[512,1024]{1,0:T(8,128)(2,1)S(1)}, u32[]{:S(2)}, u32[]{:S(2)}) %collective-permute-start.117) | collective-permute-done | bytes 1048608 | tf_op jit(solution)/shard_map/ppermute | solution.py:20
  1198.4 20.7 %collective-permute-done.121.refs_6_ = bf16[512,1024]{1,0:T(8,128)(2,1)} collective-permute-done((bf16[512,1024]{1,0:T(8,128)(2,1)S(1)}, bf16[512,1024]{1,0:T(8,128)(2,1)}, u32[]{:S(2)}, u32[]{:S(2)}) %collective-permute-start.121) | collective-permute-done | bytes 1048608 | tf_op jit(solution)/shard_map/ppermute | solution.py:20
  1219.1 14.0 %all_gather.24 = f32[4,4,2048]{2,1,0:T(4,128)S(1)} all-gather(f32[1,4,2048]{2,1,0:T(4,128)S(1)} %slice_select_fusion), channel_id=1, replica_groups=mesh['section'=2,'shard'=4,'rep'=4] {'shard'}, dimensions={0}, use_global_device_ids=true | all-gather | bytes 163840 | tf_op jit(solution)/shard_map/all_gather | solution.py:594
  1240.3 9.7 shard_map.373
  (904 shorter events, 695.8 us)
Async XLA Ops:
  7.2 136.8 %all-gather.6.cloned.1.call-start = ((), (), s32[]{:S(2)}) async-start(), calls=%async_computation.6 | async-start | bytes 5242880 | tf_op jit(solution)/shard_map/all_gather | solution.py:371
  48.5 210.1 %all-gather.8.cloned.1.call-start = ((), (), s32[]{:S(2)}) async-start(), calls=%async_computation.7 | async-start | bytes 7208960 | tf_op jit(solution)/shard_map/all_gather | solution.py:371
  50.4 29.0 %collective-permute-start.3 = (bf16[2,128,2048]{2,1,0:T(8,128)(2,1)S(1)}, bf16[2,128,2048]{2,1,0:T(8,128)(2,1)}, u32[]{:S(2)}, u32[]{:S(2)}) collective-permute-start(bf16[2,128,2048]{2,1,0:T(8,128)(2,1)S(1)} %bitcast.647), channel_id=1, source_target_pairs={{0,16},{1,17},{2,18},{3,19},{4,20},{5,21},{6,22},{7,23},{8,24},{9,... | collective-permute-start | bytes 3145736 | tf_op jit(solution)/shard_map/ppermute | solution.py:24
  56.9 49.8 %collective-permute-start.10 = (bf16[176,2048]{1,0:T(8,128)(2,1)}, bf16[176,2048]{1,0:T(8,128)(2,1)}, u32[]{:S(2)}, u32[]{:S(2)}) collective-permute-start(bf16[176,2048]{1,0:T(8,128)(2,1)} %dynamic-slice_bitcast_fusion), channel_id=1, source_target_pairs={{0,16},{16,0},{1,17},{17,1},{2,18},{18,2},{3,19},{19,3},{4,20},{20... | collective-permute-start | bytes 2162696 | tf_op jit(solution)/shard_map/ppermute | solution.py:20
  67.5 54.1 %collective-permute-start.23 = (bf16[512,1408]{1,0:T(8,128)(2,1)}, bf16[512,1408]{1,0:T(8,128)(2,1)}, u32[]{:S(2)}, u32[]{:S(2)}) collective-permute-start(bf16[512,1408]{1,0:T(8,128)(2,1)} %concatenate.329), channel_id=1, source_target_pairs={{0,16},{16,0},{1,17},{17,1},{2,18},{18,2},{3,19},{19,3},{4,20},{20... | collective-permute-start | bytes 4325384 | tf_op jit(solution)/shard_map/ppermute | solution.py:20
  124.8 220.7 %all-gather.10.cloned.1.call-start = ((), (), s32[]{:S(2)}) async-start(), calls=%async_computation.8 | async-start | bytes 7208960 | tf_op jit(solution)/shard_map/all_gather | solution.py:371
  179.4 253.9 %all-gather.12.cloned.1.call-start = ((), (), s32[]{:S(2)}) async-start(), calls=%async_computation.9 | async-start | bytes 5242880 | tf_op jit(solution)/shard_map/all_gather | solution.py:371
  354.0 190.5 %all-gather.14.cloned.1.call-start = ((), (), s32[]{:S(2)}) async-start(), calls=%async_computation.10 | async-start | bytes 7208960 | tf_op jit(solution)/shard_map/all_gather | solution.py:371
  394.8 42.2 %collective-permute-start.36 = (bf16[256,1024]{1,0:T(8,128)(2,1)S(1)}, bf16[256,1024]{1,0:T(8,128)(2,1)S(1)}, u32[]{:S(2)}, u32[]{:S(2)}) collective-permute-start(bf16[256,1024]{1,0:T(8,128)(2,1)S(1)} %pad_maximum_fusion.38), channel_id=1, source_target_pairs={{0,2},{1,3},{2,0},{3,1},{4,6},{5,7},{6,4},{7,5},{8,10},{9,11},{10,... | collective-permute-start | bytes 1572872 | tf_op jit(solution)/shard_map/ppermute | solution.py:20
  398.0 39.7 %collective-permute-start.38 = (bf16[256,1024]{1,0:T(8,128)(2,1)}, bf16[256,1024]{1,0:T(8,128)(2,1)}, u32[]{:S(2)}, u32[]{:S(2)}) collective-permute-start(bf16[256,1024]{1,0:T(8,128)(2,1)} %pad_maximum_fusion.39), channel_id=1, source_target_pairs={{0,16},{16,0},{1,17},{17,1},{2,18},{18,2},{3,19},{19,3},{4,20},{20... | collective-permute-start | bytes 1572872 | tf_op jit(solution)/shard_map/ppermute | solution.py:20
  439.0 212.3 %reduce-scatter.7.cloned.1.call-start = ((), (), s32[]{:S(2)}) async-start(), calls=%async_computation.11 | async-start | bytes 3604480 | tf_op jit(solution)/shard_map/reduce_scatter | solution.py:473
  573.4 159.7 %reduce-scatter.9.cloned.1.call-start = ((), (), s32[]{:S(2)}) async-start(), calls=%async_computation.12 | async-start | bytes 7208960 | tf_op jit(solution)/shard_map/reduce_scatter | solution.py:473
  601.8 236.6 %reduce-scatter.11.cloned.1.call-start = ((), (), s32[]{:S(2)}) async-start(), calls=%async_computation.13 | async-start | bytes 5242880 | tf_op jit(solution)/shard_map/reduce_scatter | solution.py:473
  762.4 182.5 %reduce-scatter.13.cloned.1.call-start = ((), (), s32[]{:S(2)}) async-start(), calls=%async_computation.14 | async-start | bytes 7208960 | tf_op jit(solution)/shard_map/reduce_scatter | solution.py:473
  838.4 177.0 %reduce-scatter.17.cloned.1.call-start = ((), (), s32[]{:S(2)}) async-start(), calls=%async_computation.16 | async-start | bytes 3604480 | tf_op jit(solution)/shard_map/reduce_scatter | solution.py:473
  902.5 239.3 %reduce-scatter.15.cloned.1.call-start = ((), (), s32[]{:S(2)}) async-start(), calls=%async_computation.15 | async-start | bytes 5242880 | tf_op jit(solution)/shard_map/reduce_scatter | solution.py:473
  977.2 36.5 %collective-permute-start.93 = (bf16[512,1408]{1,0:T(8,128)(2,1)S(1)}, bf16[512,1408]{1,0:T(8,128)(2,1)}, u32[]{:S(2)}, u32[]{:S(2)}) collective-permute-start(bf16[512,1408]{1,0:T(8,128)(2,1)S(1)} %get-tuple-element.215), channel_id=1, source_target_pairs={{0,16},{16,0},{1,17},{17,1},{2,18},{18,2},{3,19},{19,3},{4,20},{20... | collective-permute-start | bytes 4325384 | tf_op jit(solution)/shard_map/ppermute | solution.py:20
  977.8 36.0 %collective-permute-start.94 = (bf16[512,1408]{1,0:T(8,128)(2,1)S(1)}, bf16[512,1408]{1,0:T(8,128)(2,1)}, u32[]{:S(2)}, u32[]{:S(2)}) collective-permute-start(bf16[512,1408]{1,0:T(8,128)(2,1)S(1)} %get-tuple-element.130.refs_0_), channel_id=1, source_target_pairs={{0,2},{1,3},{2,0},{3,1},{4,6},{5,7},{6,4},{7,5},{8,10},{9,11},{10,... | collective-permute-start | bytes 4325384 | tf_op jit(solution)/shard_map/ppermute | solution.py:20
  1030.8 57.3 %collective-permute-start.96 = (bf16[2,128,2048]{2,1,0:T(8,128)(2,1)}, bf16[2,128,2048]{2,1,0:T(8,128)(2,1)}, u32[]{:S(2)}, u32[]{:S(2)}) collective-permute-start(bf16[2,128,2048]{2,1,0:T(8,128)(2,1)} %pad_maximum_fusion.31), channel_id=1, source_target_pairs={{0,2},{1,3},{2,0},{3,1},{4,6},{5,7},{6,4},{7,5},{8,10},{9,11},{10,... | collective-permute-start | bytes 3145736 | tf_op jit(solution)/shard_map/ppermute | solution.py:20
  1032.3 40.4 %collective-permute-start.104 = (bf16[176,2048]{1,0:T(8,128)(2,1)S(1)}, bf16[176,2048]{1,0:T(8,128)(2,1)}, u32[]{:S(2)}, u32[]{:S(2)}) collective-permute-start(bf16[176,2048]{1,0:T(8,128)(2,1)S(1)} %get-tuple-element.254.refs_0_), channel_id=1, source_target_pairs={{0,2},{1,3},{2,0},{3,1},{4,6},{5,7},{6,4},{7,5},{8,10},{9,11},{10,... | collective-permute-start | bytes 2162696 | tf_op jit(solution)/shard_map/ppermute | solution.py:20
  1041.3 46.8 %collective-permute-start.108 = (bf16[176,2048]{1,0:T(8,128)(2,1)S(1)}, bf16[176,2048]{1,0:T(8,128)(2,1)}, u32[]{:S(2)}, u32[]{:S(2)}) collective-permute-start(bf16[176,2048]{1,0:T(8,128)(2,1)S(1)} %collective-permute-done.106.refs_4_), channel_id=1, source_target_pairs={{0,2},{1,3},{2,0},{3,1},{4,6},{5,7},{6,4},{7,5},{8,10},{9,11},{10,... | collective-permute-start | bytes 2162696 | tf_op jit(solution)/shard_map/ppermute | solution.py:20
  1042.6 70.1 %collective-permute-start.101 = (bf16[512,1408]{1,0:T(8,128)(2,1)}, bf16[512,1408]{1,0:T(8,128)(2,1)}, u32[]{:S(2)}, u32[]{:S(2)}) collective-permute-start(bf16[512,1408]{1,0:T(8,128)(2,1)} %collective-permute-done.93.refs_4_), channel_id=1, source_target_pairs={{0,2},{1,3},{2,0},{3,1},{4,6},{5,7},{6,4},{7,5},{8,10},{9,11},{10,... | collective-permute-start | bytes 4325384 | tf_op jit(solution)/shard_map/ppermute | solution.py:20
  1045.3 47.1 %collective-permute-start.103 = (bf16[176,2048]{1,0:T(8,128)(2,1)S(1)}, bf16[176,2048]{1,0:T(8,128)(2,1)}, u32[]{:S(2)}, u32[]{:S(2)}) collective-permute-start(bf16[176,2048]{1,0:T(8,128)(2,1)S(1)} %get-tuple-element.254.refs_0_), channel_id=1, source_target_pairs={{0,1},{1,0},{2,3},{3,2},{4,5},{5,4},{6,7},{7,6},{8,9},{9,8},{10,11... | collective-permute-start | bytes 2162696 | tf_op jit(solution)/shard_map/ppermute | solution.py:20
  1092.4 31.6 %collective-permute-start.100 = (bf16[512,1408]{1,0:T(8,128)(2,1)}, bf16[512,1408]{1,0:T(8,128)(2,1)}, u32[]{:S(2)}, u32[]{:S(2)}) collective-permute-start(bf16[512,1408]{1,0:T(8,128)(2,1)} %collective-permute-done.93.refs_4_), channel_id=1, source_target_pairs={{0,1},{1,0},{2,3},{3,2},{4,5},{5,4},{6,7},{7,6},{8,9},{9,8},{10,11... | collective-permute-start | bytes 4325384 | tf_op jit(solution)/shard_map/ppermute | solution.py:20
  1092.4 31.6 %collective-permute-start.98 = (bf16[512,1408]{1,0:T(8,128)(2,1)S(1)}, bf16[512,1408]{1,0:T(8,128)(2,1)}, u32[]{:S(2)}, u32[]{:S(2)}) collective-permute-start(bf16[512,1408]{1,0:T(8,128)(2,1)S(1)} %get-tuple-element.130.refs_0_), channel_id=1, source_target_pairs={{0,1},{1,0},{2,3},{3,2},{4,5},{5,4},{6,7},{7,6},{8,9},{9,8},{10,11... | collective-permute-start | bytes 4325384 | tf_op jit(solution)/shard_map/ppermute | solution.py:20
  1092.9 31.1 %collective-permute-start.99 = (bf16[512,1408]{1,0:T(8,128)(2,1)}, bf16[512,1408]{1,0:T(8,128)(2,1)}, u32[]{:S(2)}, u32[]{:S(2)}) collective-permute-start(bf16[512,1408]{1,0:T(8,128)(2,1)} %collective-permute-done.94.refs_2_), channel_id=1, source_target_pairs={{0,1},{1,0},{2,3},{3,2},{4,5},{5,4},{6,7},{7,6},{8,9},{9,8},{10,11... | collective-permute-start | bytes 4325384 | tf_op jit(solution)/shard_map/ppermute | solution.py:20
  1144.1 28.8 %collective-permute-start.119 = (bf16[512,1024]{1,0:T(8,128)(2,1)}, bf16[512,1024]{1,0:T(8,128)(2,1)S(1)}, u32[]{:S(2)}, u32[]{:S(2)}) collective-permute-start(bf16[512,1024]{1,0:T(8,128)(2,1)} %get-tuple-element.219), channel_id=1, source_target_pairs={{0,16},{16,0},{1,17},{17,1},{2,18},{18,2},{3,19},{19,3},{4,20},{20... | collective-permute-start | bytes 3145736 | tf_op jit(solution)/shard_map/ppermute | solution.py:20
  1172.9 46.2 %collective-permute-start.121 = (bf16[512,1024]{1,0:T(8,128)(2,1)S(1)}, bf16[512,1024]{1,0:T(8,128)(2,1)}, u32[]{:S(2)}, u32[]{:S(2)}) collective-permute-start(bf16[512,1024]{1,0:T(8,128)(2,1)S(1)} %collective-permute-done.119.refs_4_), channel_id=1, source_target_pairs={{0,2},{1,3},{2,0},{3,1},{4,6},{5,7},{6,4},{7,5},{8,10},{9,11},{10,... | collective-permute-start | bytes 3145736 | tf_op jit(solution)/shard_map/ppermute | solution.py:20
  1173.9 63.8 %collective-permute-start.115 = (bf16[128,2048]{1,0:T(8,128)(2,1)}, bf16[128,2048]{1,0:T(8,128)(2,1)}, u32[]{:S(2)}, u32[]{:S(2)}) collective-permute-start(bf16[128,2048]{1,0:T(8,128)(2,1)} %get-tuple-element.255), channel_id=1, source_target_pairs={{0,16},{1,17},{2,18},{3,19},{4,20},{5,21},{6,22},{7,23},{8,24},{9,... | collective-permute-start | bytes 1572872 | tf_op jit(solution)/shard_map/ppermute | solution.py:24
  1181.5 58.7 %collective-permute-start.116 = (bf16[512,1024]{1,0:T(8,128)(2,1)S(1)}, bf16[512,1024]{1,0:T(8,128)(2,1)}, u32[]{:S(2)}, u32[]{:S(2)}) collective-permute-start(bf16[512,1024]{1,0:T(8,128)(2,1)S(1)} %get-tuple-element.220.refs_0_), channel_id=1, source_target_pairs={{0,1},{1,0},{2,3},{3,2},{4,5},{5,4},{6,7},{7,6},{8,9},{9,8},{10,11... | collective-permute-start | bytes 3145736 | tf_op jit(solution)/shard_map/ppermute | solution.py:20
  1182.1 58.2 %collective-permute-start.120 = (bf16[512,1024]{1,0:T(8,128)(2,1)S(1)}, bf16[512,1024]{1,0:T(8,128)(2,1)}, u32[]{:S(2)}, u32[]{:S(2)}) collective-permute-start(bf16[512,1024]{1,0:T(8,128)(2,1)S(1)} %collective-permute-done.119.refs_4_), channel_id=1, source_target_pairs={{0,1},{1,0},{2,3},{3,2},{4,5},{5,4},{6,7},{7,6},{8,9},{9,8},{10,11... | collective-permute-start | bytes 3145736 | tf_op jit(solution)/shard_map/ppermute | solution.py:20
  1198.4 41.9 %collective-permute-start.118 = (bf16[512,1024]{1,0:T(8,128)(2,1)S(1)}, bf16[512,1024]{1,0:T(8,128)(2,1)}, u32[]{:S(2)}, u32[]{:S(2)}) collective-permute-start(bf16[512,1024]{1,0:T(8,128)(2,1)S(1)} %collective-permute-done.117.refs_2_), channel_id=1, source_target_pairs={{0,1},{1,0},{2,3},{3,2},{4,5},{5,4},{6,7},{7,6},{8,9},{9,8},{10,11... | collective-permute-start | bytes 3145736 | tf_op jit(solution)/shard_map/ppermute | solution.py:20
  (235 other events, 3155.5 us)
Sparse Core Ops, SparseCore 0:
  48.6 82.2 all-gather.5
  133.0 105.2 all-gather.7
  240.5 104.9 all-gather.9
  354.1 79.1 all-gather.11
  439.1 105.3 all-gather.13
  573.5 54.4 reduce-scatter.6
  630.9 102.1 reduce-scatter.8
  762.5 75.8 reduce-scatter.10
  841.4 102.7 reduce-scatter.12
  947.0 56.6 reduce-scatter.16
  1006.7 76.6 reduce-scatter.14

commit v3 on v2

--- a/solution.py
+++ b/solution.py
@@ -89,7 +89,7 @@
     return join_halves(halves, [turned_codes.index(c) for c in codes]), tie
 
 
-def collapse(send, keep, stages):
+def collapse(send, keep, stages, tie=None):
     outer, turned, codes, turned_codes = orders(stages)
     total = keep + swap(send.astype(BF16), stages[-1]).astype(F32)
     half = total.shape[1] // 2
@@ -100,12 +100,14 @@
         right_in = swap(right[size:].astype(BF16), other)
         left = left[:size] + left_in.astype(F32)
         right = right[:size] + right_in.astype(F32)
-    return jnp.concatenate([left, right], axis=1)
+        if tie is not None:
+            left, right, tie = lax.optimization_barrier((left, right, tie))
+    return jnp.concatenate([left, right], axis=1), tie
 
 
 def reduced_product(left, right, stages):
     half = left.shape[0] // 2
-    return collapse(product(left[half:], right), product(left[:half], right), stages)
+    return collapse(product(left[half:], right), product(left[:half], right), stages)[0]
 
 
 def product(left, right):
@@ -339,7 +341,6 @@
         return jnp.array(slot, jnp.int32)
 
     plane_order = jnp.array(codes(stages), jnp.int32)
-    plane_place = places(stages)
     rep_place = places(rep_stages)
 
     gains = jnp.stack([norm_mix[0], norm_ffn[0], norm_head[0], gate_gap[0]])
@@ -358,14 +359,13 @@
         *local_weights, (1 - section) * reps + rep, shards, group, sharing
     )
     received = [swap(piece, ("section", 1)) for piece in sent]
-    mix_first, gate_up_first, down_first = [
-        jnp.where(on_first, a, b) for a, b in zip(kept, received)
+    kept_mix = kept[0]
+    gate_up_first, down_first = [
+        jnp.where(on_first, a, b) for a, b in zip(kept[1:], received[1:])
     ]
-    mix_second, gate_up_second, down_second = [
-        jnp.where(on_first, b, a) for a, b in zip(kept, received)
+    gate_up_second, down_second = [
+        jnp.where(on_first, b, a) for a, b in zip(kept[1:], received[1:])
     ]
-
-    mix_first, gains = lax.optimization_barrier((mix_first, gains))
 
     def over_shard(piece):
         return lax.all_gather(piece, "shard", axis=0, tiled=True)
@@ -375,8 +375,12 @@
     wide = per_device * head
     local_rows = model_width // shards
 
+    kept_mix = over_shard(kept_mix)
+    received_mix = over_shard(received[0])
+    mix_first = jnp.where(on_first, kept_mix, received_mix)
+    mix_second = jnp.where(on_first, received_mix, kept_mix)
+
     def mixer_weights(mix):
-        mix = over_shard(mix)
         out = mix[:, 3 * wide :].reshape(shards, -1, each * head, wide)
         out = out.transpose(0, 2, 1, 3).reshape(shards * each * head, model_width // sharing)
         out = spread(out[None], share_stages)
@@ -414,6 +418,11 @@
     causal = jnp.tril(jnp.ones((length, length), F32))
     same = (segment_ids[:, :, None] == segment_ids[:, None, :]).astype(F32) * causal
     valid_own = valid_mask[0][:, None]
+
+    inverse = lax.dynamic_slice_in_dim(jnp.argsort(block_order), rep * micro, micro, 0)
+    back_places = places(rep_stages[:1] + stages[:1] + rep_stages[1:])[
+        (inverse % micro * reps + inverse // micro) ^ ident
+    ]
 
     rows = boundary[0].reshape(micro, length, model_width)
     first_rows = jnp.where(on_first, rows, one_way(rows, 0))
@@ -436,41 +445,53 @@
             own_channels(gain[2]),
         )
         mixed = mixed.reshape(group * length, per_device * head).astype(BF16)
+        gate_up_weight, tied = over_shard(gate_up_piece), None
         if down_weight is None:
             mixed, down_pieces = lax.optimization_barrier((mixed, down_pieces))
-            down_weight = over_shard(down_pieces).reshape(shards, 2, -1, model_width)
-            down_weight = [down_weight[:, i].reshape(-1, model_width) for i in range(2)]
-            gate_up_weight, tied = over_shard(gate_up_piece), None
+            down_weight = over_shard(down_pieces[0])
         else:
-            down_weight = [down_weight]
-            gate_up_weight = tied = over_shard(gate_up_piece)
+            tied = product_t(d_down_second, down_weight)
         resid_mid = x_own + reduced_product(mixed, out_weight, stages)
         mid_value, pull_mid = jax.vjp(rms_norm, resid_mid, gain[1])
         normed_mid, tied = spread_rows(mid_value.astype(BF16), stages, tied)
-        early = ()
-        if tied is not None:
-            gate_up_weight = tied
-            early = product_t(d_down_second, down_weight[0])
-            normed_mid, early = lax.optimization_barrier((normed_mid, early))
+        early = tied
         gate_up = product(normed_mid, gate_up_weight)
         half = gate_up.shape[1] // 2
         hidden, pull_act = jax.vjp(
             lambda a, b: jax.nn.silu(a) * b, gate_up[:, :half], gate_up[:, half:]
         )
         hidden = hidden.astype(BF16)
+        later = ()
         if tied is None:
-            hidden, early = lax.optimization_barrier((hidden, d_down_second))
-        result = (resid_mid + reduced_product(hidden, down_weight[0], stages)) * valid_own
-        weights = (qfv_weight, out_weight, gate_up_weight, down_weight[0])
+            hidden, early, later = lax.optimization_barrier(
+                (hidden, d_down_second, down_pieces[1])
+            )
+            later = over_shard(later)
+        result = (resid_mid + reduced_product(hidden, down_weight, stages)) * valid_own
+        weights = (qfv_weight, out_weight, gate_up_weight, down_weight)
         kept = (normed_all, mixed, normed_mid, hidden, pull_mix, pull_mid, pull_act)
-        return result.astype(BF16), weights, kept, down_weight[-1], early
-
-    def transposed_sum(left, right, stages):
+        return result.astype(BF16), weights, kept, later, early
+
+    def transposed_sum(left, right, stages, tie=None):
         half = left.shape[0] // 2
-        return collapse(product_t(left[half:], right), product_t(left[:half], right), stages)
+        return collapse(product_t(left[half:], right), product_t(left[:half], right), stages, tie)
 
     def to_owner(term):
         return lax.psum_scatter(term, "shard", scatter_dimension=0, tiled=True)
+
+    def begin_collect(of_first, of_second):
+        own = jnp.where(on_first, of_first, of_second)
+        sent = jnp.where(on_first, of_second, of_first)
+        return own, swap(sent, ("section", 1)), swap(own, rep_stages[0])
+
+    def collect(own, other, across, diagonal=None):
+        blocks = {0: own, reps: other, rep_stages[0][1]: across}
+        if diagonal is None:
+            diagonal = swap(other, rep_stages[0])
+        blocks[reps ^ rep_stages[0][1]] = diagonal
+        for stage in rep_stages[1:]:
+            blocks.update({code ^ stage[1]: swap(blocks[code], stage) for code in list(blocks)})
+        return [blocks[code] for code in range(group)]
 
     def backward(grad_out, d_down, d_hidden, weights, kept_state, pull_in, earlier):
         qfv_weight, out_weight, gate_up_weight, down_weight = weights
@@ -480,24 +501,24 @@
         if last:
             d_down, _ = spread_rows(d_out.astype(BF16), stages)
             d_hidden = product_t(d_down, down_weight)
-            term_down = weight_term(hidden, d_down)
-            earlier, term_down = lax.optimization_barrier((earlier, term_down))
-        else:
-            term_down = weight_term(hidden, d_down)
-            d_hidden, term_down = lax.optimization_barrier((d_hidden, term_down))
         d_gate_up = jnp.concatenate(pull_act(d_hidden), axis=1).astype(BF16)
         term_gate_up = weight_term(normed_mid, d_gate_up)
-        d_gate_up, term_gate_up, earlier = lax.optimization_barrier(
-            (d_gate_up, term_gate_up, earlier)
+        if last:
+            d_gate_up, term_gate_up, earlier = lax.optimization_barrier(
+                (d_gate_up, term_gate_up, earlier)
+            )
+        else:
+            d_gate_up, term_gate_up = lax.optimization_barrier((d_gate_up, term_gate_up))
+        summed_gate_up = to_owner(term_gate_up)
+        more, grad_ffn = pull_mid(transposed_sum(d_gate_up, gate_up_weight, stages)[0])
+        d_resid = d_out + more
+        d_attn, term_down = lax.optimization_barrier(
+            (d_resid.astype(BF16), weight_term(hidden, d_down))
         )
         summed_down = to_owner(term_down)
-        summed_gate_up = to_owner(term_gate_up)
-        more, grad_ffn = pull_mid(transposed_sum(d_gate_up, gate_up_weight, stages))
-        d_resid = d_out + more
-        d_attn = d_resid.astype(BF16)
+        d_attn, _ = spread_rows(d_attn, stages)
         if not last:
-            d_attn, summed_down = lax.optimization_barrier((d_attn, summed_down))
-        d_attn, _ = spread_rows(d_attn, stages)
+            d_attn, summed_gate_up = lax.optimization_barrier((d_attn, summed_gate_up))
         d_mixed = product_t(d_attn, out_weight).reshape(group, length, per_device, head)
         d_q, d_f, d_v, grad_gap, grad_head = pull_mix(d_mixed)
         d_qfv = jnp.stack([d_q, d_f, d_v], axis=2).astype(BF16)
@@ -512,12 +533,22 @@
         term_mix = jnp.concatenate(
             [weight_term(normed_all, d_qfv), term_out.reshape(model_width, wide)], axis=1
         )
-        d_qfv, term_mix, summed_gate_up = lax.optimization_barrier(
-            (d_qfv, term_mix, summed_gate_up)
-        )
+        if last:
+            d_qfv, term_mix, summed_gate_up = lax.optimization_barrier(
+                (d_qfv, term_mix, summed_gate_up)
+            )
+            begun = begin_collect(summed_gate_up, gate_up_1)
+        else:
+            d_qfv, term_mix, summed_down, earlier = lax.optimization_barrier(
+                (d_qfv, term_mix, summed_down, earlier)
+            )
+            begun = None
         summed_mix = to_owner(term_mix)
-        more, grad_mix = pull_in(transposed_sum(d_qfv, qfv_weight, stages))
+        d_normed, begun = transposed_sum(d_qfv, qfv_weight, stages, begun)
+        more, grad_mix = pull_in(d_normed)
         d_x = d_resid + more
+        if last:
+            summed_gate_up = begun
         small = jnp.zeros((4, model_width), F32).at[0].set(grad_mix).at[1].set(grad_ffn)
         for t in range(per_device):
             column = own_heads[t] * head
@@ -534,66 +565,51 @@
         mix_first,
         gate_up_first,
         gains[0],
-        down_pieces=jnp.concatenate([down_first, down_second], axis=0),
+        down_pieces=(down_first, down_second),
     )
     first_f32 = first.astype(F32)
     normed_second, pull_in_second = jax.vjp(rms_norm, first_f32, gains[1, 0])
+    normed_second, down_second = spread_rows(normed_second.astype(BF16), stages, down_second)
     second, weights_second, kept_second, _, d_hidden_second = forward(
         first_f32,
-        spread_rows(normed_second.astype(BF16), stages)[0],
+        normed_second,
         mix_second,
         gate_up_second,
         gains[1],
         down_weight=down_second,
     )
-    d_first, (mix_1, gate_up_1, down_1), small_second, _ = backward(
+    second_rows = jnp.stack([one_way(second, 0), second])
+    d_first, (mix_1, gate_up_1, down_1), small_second, second_rows = backward(
         own_cotangent,
         d_down_second,
         d_hidden_second,
         weights_second,
         kept_second,
         pull_in_second,
-        (),
-    )
-    d_dealt, (mix_0, gate_up_0, down_0), small_first, mix_1 = backward(
+        second_rows,
+    )
+    d_dealt, (mix_0, gate_up_begun, down_0), small_first, mix_1 = backward(
         d_first.astype(BF16).astype(F32), None, None, weights_first, kept_first, pull_in_first, mix_1
     )
 
-    def begin_collect(of_first, of_second):
-        own = jnp.where(on_first, of_first, of_second)
-        sent = jnp.where(on_first, of_second, of_first)
-        return own, swap(sent, ("section", 1)), swap(own, rep_stages[0])
-
-    def collect(own, other, across):
-        blocks = {0: own, reps: other, rep_stages[0][1]: across}
-        blocks[reps ^ rep_stages[0][1]] = swap(other, rep_stages[0])
-        for stage in rep_stages[1:]:
-            blocks.update({code ^ stage[1]: swap(blocks[code], stage) for code in list(blocks)})
-        return [blocks[code] for code in range(group)]
-
-    begun = begin_collect(gate_up_0, gate_up_1)
-    d_dealt, begun = lax.optimization_barrier((d_dealt, begun))
-    gate, up = place_columns(collect(*begun), ident, shards)
-    down = place_rows(collect(*begin_collect(down_0, down_1)), ident)
-
-    all_grads = spread(d_dealt.astype(BF16)[None], stages)
-    mix_0, all_grads, gate, up, down = lax.optimization_barrier((mix_0, all_grads, gate, up, down))
-    inverse = jnp.argsort(block_order)
-    own_dealt = lax.dynamic_slice_in_dim(inverse, rep * micro, micro, 0)
-    own_holder = (own_dealt % micro) * reps + own_dealt // micro
-    back_rows = all_grads[plane_place[own_holder ^ ident]]
-    second_rows = jnp.stack([one_way(second, 0), second])
-    boundary_out = jnp.where(on_first, back_rows, second_rows).reshape(
-        1, micro * length, model_width
-    )
-
-    small = jnp.stack([small_first, small_second])
-    for stage in stages:
-        small = small + swap(small, stage)
-    small = jnp.where(on_first, small[0], small[1])
-    small = jnp.sum(lax.all_gather(small, "shard", axis=0, tiled=False), axis=0)
-    small = lax.dynamic_slice_in_dim(small, shard * local_rows, local_rows, 1)
-
+    across = rep_stages[0]
+    d_dealt, mix_0, gate_up_diagonal, back_places = lax.optimization_barrier(
+        (d_dealt, mix_0, swap(gate_up_begun[1], across), back_places)
+    )
+    mix_own, mix_other, mix_across = begin_collect(mix_0, mix_1)
+    rows_sent = [d_dealt, small_first, small_second, jnp.zeros((8, model_width), F32)]
+    grads = spread(jnp.concatenate(rows_sent).astype(BF16)[None], rep_stages[:1])
+    gate, up = place_columns(collect(*gate_up_begun, gate_up_diagonal), ident, shards)
+    down_0, mix_other, mix_across, grads, gate, up = lax.optimization_barrier(
+        (down_0, mix_other, mix_across, grads, gate, up)
+    )
+    down_own, down_other, down_across = begin_collect(down_0, down_1)
+    mix_diagonal = swap(mix_other, across)
+    down_other, down_across, mix_diagonal, grads = lax.optimization_barrier(
+        (down_other, down_across, mix_diagonal, spread(grads, stages[:1]))
+    )
+    down_diagonal = swap(down_other, across)
+    all_grads = spread(grads, rep_stages[1:])
     sources = [ident ^ code for code in range(group)]
     columns = jnp.stack(
         [head_number(device, t) * head for device in sources for t in range(per_device)]
@@ -602,8 +618,31 @@
     for device in sources:
         corners += [device // sharing * each * head, device % sharing * (model_width // sharing)]
     query, forget, into, out = place_mixer(
-        collect(*begin_collect(mix_0, mix_1)), columns, jnp.stack(corners), each * head, model_width
-    )
+        collect(mix_own, mix_other, mix_across, mix_diagonal),
+        columns,
+        jnp.stack(corners),
+        each * head,
+        model_width,
+    )
+    small = jnp.sum(all_grads[:, length:].astype(F32), axis=0)[:8].reshape(2, 4, model_width)
+    small = jnp.where(on_first, small[0], small[1])
+    for stage in shard_stages:
+        small = small + swap(small, stage)
+    small = lax.dynamic_slice_in_dim(small, shard * local_rows, local_rows, 1)
+
+    back_rows = [
+        lax.dynamic_slice(all_grads, (back_places[number], 0, 0), (1, length, model_width))
+        for number in range(micro)
+    ]
+    boundary_out = jnp.where(on_first, jnp.concatenate(back_rows), second_rows).reshape(
+        1, micro * length, model_width
+    )
+    mixer_grads = (query, forget, into, out)
+    down_diagonal, mixer_grads, boundary_out, small = lax.optimization_barrier(
+        (down_diagonal, mixer_grads, boundary_out, small)
+    )
+    query, forget, into, out = mixer_grads
+    down = place_rows(collect(down_own, down_other, down_across, down_diagonal), ident)
 
     return (
         boundary_out,

time: 1270 us -> 1140 us (0.90)
  waiting for transfers between devices: 635 us -> 484 us
  blocking collectives: 14 us -> 0 us
  matrix products: 179 us -> 192 us
    ppermute x123 -> x122, waiting for transfers between devices: 463 us -> 364 us  [swap(): lax.ppermute(block, axis, [(i, i ^ distance) for i in range(lax.axis_size...]
    all_gather x5 -> x6, waiting for transfers between devices: 126 us -> 83.4 us  [over_shard(): return lax.all_gather(piece, 'shard', axis=0, tiled=True)]
    reduce_scatter x6, waiting for transfers between devices: 37 us -> 15.1 us  [to_owner(): return lax.psum_scatter(term, 'shard', scatter_dimension=0, tiled=True)]
    all_gather x1 -> x0, blocking collectives: 14 us -> none  [local(): small = jnp.sum(lax.all_gather(small, 'shard', axis=0, tiled=False), axis=0)]
    ppermute x3, waiting for transfers between devices: 8.52 us -> 21.6 us  [one_way(): return lax.ppermute(block, 'section', [(source, 1 - source)])]
    unnamed x269 -> x304, local copies, waits for them, and re-layouts: 36.2 us -> 46.5 us
    ppermute x123 -> x122, starting transfers between devices: 101 us -> 103 us  [swap(): lax.ppermute(block, axis, [(i, i ^ distance) for i in range(lax.axis_size...]
  transfers between devices with their start and end apart: 137 -> 137, of which waited for: 74 -> 75; matrix products, arithmetic and copies ran while one was open for 29% -> 35% of each run, Pallas kernels for 3% -> 3%
where the time goes in v3:
time: 1140 us; the launch traced here: 1130 us
  waiting for transfers between devices  484 us (42%)
  matrix products  192 us (17%)
  local copies, waits for them, and re-layouts  154 us (14%)
  other arithmetic  123 us (11%)
  starting transfers between devices  113 us (10%)
  Pallas kernels  44.2 us (4%)
  between operations  21.8 us (2%)
    ppermute x122, waiting for transfers between devices, swap(): lax.ppermute(block, axis, [(i, i ^ distance) for i in range(lax.axis_size...  364 us
    ppermute x122, starting transfers between devices, swap(): lax.ppermute(block, axis, [(i, i ^ distance) for i in range(lax.axis_size...  103 us
    all_gather x6, waiting for transfers between devices, over_shard(): return lax.all_gather(piece, 'shard', axis=0, tiled=True)  83.4 us
    dot_general x12, matrix products, product_t(): lax.dot_general(left, right, (((1,), (1,)), ((), ())), preferred_element_...  63 us
    dot_general x12, matrix products, product(): return jnp.dot(left, right, preferred_element_type=F32)  56.1 us
    unnamed x304, local copies, waits for them, and re-layouts  46.5 us
    dot_general x8, matrix products, weight_term(): lax.dot_general(act_rows, grad_rows, (((0,), (0,)), ((), ())), preferred_...  46 us
  transfers between devices with their start and end apart: 137, of which 75 were waited for; matrix products, arithmetic and copies ran while one was open for 35% of the time, Pallas kernels for 3%

profile of v3, /device:TPU:0, one launch (start us, length us, event | category | flops | bytes accessed | tf_op | source)
XLA Modules:
  0.0 1131.6 jit_solution(14773839306320154839)
XLA Ops:
  46.8 25.4 %collective-permute-done.9 = bf16[512,1024]{1,0:T(8,128)(2,1)S(1)} collective-permute-done((bf16[512,1024]{1,0:T(8,128)(2,1)}, bf16[512,1024]{1,0:T(8,128)(2,1)S(1)}, u32[]{:S(2)}, u32[]{:S(2)}) %collective-permute-start.9) | collective-permute-done | bytes 1048608 | tf_op jit(solution)/shard_map/ppermute | solution.py:20
  144.2 40.6 %all-gather.9.cloned.1.call-done = bf16[2048,1024]{1,0:T(8,128)(2,1)} async-done(((bf16[512,1024]{1,0:T(8,128)(2,1)}), bf16[2048,1024]{1,0:T(8,128)(2,1)}) %all-gather.9.cloned.1.call-update) | async-done | bytes 4194320 | tf_op jit(solution)/shard_map/all_gather | solution.py:371
  223.4 14.9 %collective-permute-done = bf16[128,2048]{1,0:T(8,128)(2,1)S(1)} collective-permute-done((bf16[128,2048]{1,0:T(8,128)(2,1)S(1)}, bf16[128,2048]{1,0:T(8,128)(2,1)S(1)}, u32[]{:S(2)}, u32[]{:S(2)}) %collective-permute-start) | collective-permute-done | bytes 524320 | tf_op jit(solution)/shard_map/ppermute | solution.py:24
  241.8 11.9 %collective-permute-done.13 = bf16[256,1024]{1,0:T(8,128)(2,1)S(1)} collective-permute-done((bf16[256,1024]{1,0:T(8,128)(2,1)S(1)}, bf16[256,1024]{1,0:T(8,128)(2,1)S(1)}, u32[]{:S(2)}, u32[]{:S(2)}) %collective-permute-start.13) | collective-permute-done | bytes 524320 | tf_op jit(solution)/shard_map/ppermute | solution.py:20
  307.4 10.5 fusion.197
  320.5 31.2 %all-gather.13.cloned.1.call-done = bf16[704,2048]{1,0:T(8,128)(2,1)} async-done(((bf16[176,2048]{1,0:T(8,128)(2,1)}), bf16[704,2048]{1,0:T(8,128)(2,1)}) %all-gather.13.cloned.1.call-update) | async-done | bytes 2883600 | tf_op jit(solution)/shard_map/all_gather | solution.py:371
  369.0 10.8 collective-permute-done.31
  463.1 10.8 collective-permute-done.43
  513.4 8.3 all-gather.17.cloned.1.call-done
  521.7 10.8 fusion.200
  538.0 8.6 convolution_convert_fusion.1
  552.0 7.9 convolution_convert_fusion.13
  586.2 8.5 collective-permute-done.54
  600.0 7.4 collective-permute-done.55
  620.9 9.7 collective-permute-done.61
  676.0 7.5 convolution_convert_fusion.3
  694.2 12.2 %reduce-scatter.9.cloned.1.call-done = bf16[176,2048]{1,0:T(8,128)(2,1)} async-done(((bf16[704,2048]{1,0:T(8,128)(2,1)}), bf16[176,2048]{1,0:T(8,128)(2,1)}) %reduce-scatter.9.cloned.1.call-update) | async-done | bytes 720912 | tf_op jit(solution)/shard_map/reduce_scatter | solution.py:480
  724.3 10.9 collective-permute-done.72
  755.4 9.9 collective-permute-done.79
  777.9 8.7 convolution_convert_fusion
  788.5 7.3 convolution_convert_fusion.12
  800.3 7.7 fusion.195
  810.9 10.9 collective-permute-done.83
  845.3 9.8 collective-permute-done.90
  884.8 7.5 convolution_convert_fusion.2
  925.3 35.9 %collective-permute-done.96 = bf16[256,1024]{1,0:T(8,128)(2,1)S(1)} collective-permute-done((bf16[256,1024]{1,0:T(8,128)(2,1)S(1)}, bf16[256,1024]{1,0:T(8,128)(2,1)S(1)}, u32[]{:S(2)}, u32[]{:S(2)}) %collective-permute-start.96) | collective-permute-done | bytes 524320 | tf_op jit(solution)/shard_map/ppermute | solution.py:20
  983.1 22.7 %collective-permute-done.101.refs_6_ = bf16[512,1408]{1,0:T(8,128)(2,1)} collective-permute-done((bf16[512,1408]{1,0:T(8,128)(2,1)}, bf16[512,1408]{1,0:T(8,128)(2,1)}, u32[]{:S(2)}, u32[]{:S(2)}) %collective-permute-start.101) | collective-permute-done | bytes 1441824 | tf_op jit(solution)/shard_map/ppermute | solution.py:20
  1012.0 7.4 collective-permute-done.104
  1025.0 12.8 %shard_map.371 = (f32[512,5632]{1,0:T(8,128)}, f32[512,5632]{1,0:T(8,128)}) custom-call(s32[1]{0:T(128)} %bitcast.166.ident_ref, bf16[512,1408]{1,0:T(8,128)(2,1)S(1)} %get-tuple-element.168.refs_0_, bf16[512,1408]{1,0:T(8,128)(2,1)} %collective-permute-done.105.refs_1_, bf16[512,1408]{1,0:T(8,128)(2,1)S(1)} %copy-done.14, ...), custom_call_target="tpu_custom_call" | custom-call | tf_op jit(solution)/shard_map/pallas_call | solution.py:211
  1046.5 23.6 %collective-permute-done.112 = bf16[2,144,2048]{2,1,0:T(8,128)(2,1)S(1)} collective-permute-done((bf16[2,144,2048]{2,1,0:T(8,128)(2,1)}, bf16[2,144,2048]{2,1,0:T(8,128)(2,1)S(1)}, u32[]{:S(2)}, u32[]{:S(2)}) %collective-permute-start.112) | collective-permute-done | bytes 1179680 | tf_op jit(solution)/shard_map/ppermute | solution.py:20
  1071.7 10.2 collective-permute-done.109.refs_4_
  1093.9 10.1 shard_map.372
  (935 shorter events, 677.5 us)
Async XLA Ops:
  7.2 137.0 %all-gather.7.cloned.1.call-start = ((), (), s32[]{:S(2)}) async-start(), calls=%async_computation.6 | async-start | bytes 5242880 | tf_op jit(solution)/shard_map/all_gather | solution.py:371
  19.5 165.2 %all-gather.9.cloned.1.call-start = ((), (), s32[]{:S(2)}) async-start(), calls=%async_computation.7 | async-start | bytes 5242880 | tf_op jit(solution)/shard_map/all_gather | solution.py:371
  19.7 58.7 %collective-permute-start.1 = (s32[1,2,5]{2,1,0:T(2,128)S(1)}, s32[1,2,5]{2,1,0:T(2,128)S(1)}, u32[]{:S(2)}, u32[]{:S(2)}) collective-permute-start(s32[1,2,5]{2,1,0:T(2,128)S(1)} %add_bitcast_fusion), channel_id=1, source_target_pairs={{0,2},{1,3},{2,0},{3,1},{4,6},{5,7},{6,4},{7,5},{8,10},{9,11},{10,... | collective-permute-start | bytes 128 | tf_op jit(solution)/shard_map/ppermute | solution.py:20
  22.7 61.5 %collective-permute-start.3 = (bf16[2,128,2048]{2,1,0:T(8,128)(2,1)S(1)}, bf16[2,128,2048]{2,1,0:T(8,128)(2,1)}, u32[]{:S(2)}, u32[]{:S(2)}) collective-permute-start(bf16[2,128,2048]{2,1,0:T(8,128)(2,1)S(1)} %bitcast.608), channel_id=1, source_target_pairs={{0,16},{1,17},{2,18},{3,19},{4,20},{5,21},{6,22},{7,23},{8,24},{9,... | collective-permute-start | bytes 3145736 | tf_op jit(solution)/shard_map/ppermute | solution.py:24
  27.7 62.9 %collective-permute-start.6 = (bf16[1,4,512]{2,1,0:T(4,128)(2,1)}, bf16[1,4,512]{2,1,0:T(4,128)(2,1)}, u32[]{:S(2)}, u32[]{:S(2)}) collective-permute-start(bf16[1,4,512]{2,1,0:T(4,128)(2,1)} %maximum_bitcast_fusion), channel_id=1, source_target_pairs={{0,8},{4,12},{8,0},{12,4},{1,9},{5,13},{9,1},{13,5},{2,10},{6,14},... | collective-permute-start | bytes 12296 | tf_op jit(solution)/shard_map/ppermute | solution.py:20
  31.0 41.3 %collective-permute-start.9 = (bf16[512,1024]{1,0:T(8,128)(2,1)}, bf16[512,1024]{1,0:T(8,128)(2,1)S(1)}, u32[]{:S(2)}, u32[]{:S(2)}) collective-permute-start(bf16[512,1024]{1,0:T(8,128)(2,1)} %maximum_dynamic-update-slice_fusion.1), channel_id=1, source_target_pairs={{0,16},{16,0},{1,17},{17,1},{2,18},{18,2},{3,19},{19,3},{4,20},{20... | collective-permute-start | bytes 3145736 | tf_op jit(solution)/shard_map/ppermute | solution.py:20
  33.1 89.6 %collective-permute-start.10 = (bf16[176,2048]{1,0:T(8,128)(2,1)}, bf16[176,2048]{1,0:T(8,128)(2,1)}, u32[]{:S(2)}, u32[]{:S(2)}) collective-permute-start(bf16[176,2048]{1,0:T(8,128)(2,1)} %dynamic-slice_bitcast_fusion), channel_id=1, source_target_pairs={{0,16},{16,0},{1,17},{17,1},{2,18},{18,2},{3,19},{19,3},{4,20},{20... | collective-permute-start | bytes 2162696 | tf_op jit(solution)/shard_map/ppermute | solution.py:20
  72.3 53.2 %collective-permute-start.23 = (bf16[512,1408]{1,0:T(8,128)(2,1)}, bf16[512,1408]{1,0:T(8,128)(2,1)}, u32[]{:S(2)}, u32[]{:S(2)}) collective-permute-start(bf16[512,1408]{1,0:T(8,128)(2,1)} %concatenate.363), channel_id=1, source_target_pairs={{0,16},{16,0},{1,17},{17,1},{2,18},{18,2},{3,19},{19,3},{4,20},{20... | collective-permute-start | bytes 4325384 | tf_op jit(solution)/shard_map/ppermute | solution.py:20
  74.7 232.8 %all-gather.11.cloned.1.call-start = ((), (), s32[]{:S(2)}) async-start(), calls=%async_computation.8 | async-start | bytes 7208960 | tf_op jit(solution)/shard_map/all_gather | solution.py:371
  128.7 222.9 %all-gather.13.cloned.1.call-start = ((), (), s32[]{:S(2)}) async-start(), calls=%async_computation.9 | async-start | bytes 3604480 | tf_op jit(solution)/shard_map/all_gather | solution.py:371
  279.9 134.9 %all-gather.15.cloned.1.call-start = ((), (), s32[]{:S(2)}) async-start(), calls=%async_computation.10 | async-start | bytes 3604480 | tf_op jit(solution)/shard_map/all_gather | solution.py:371
  356.7 165.0 %all-gather.17.cloned.1.call-start = ((), (), s32[]{:S(2)}) async-start(), calls=%async_computation.11 | async-start | bytes 7208960 | tf_op jit(solution)/shard_map/all_gather | solution.py:371
  416.0 237.1 %reduce-scatter.7.cloned.1.call-start = ((), (), s32[]{:S(2)}) async-start(), calls=%async_computation.12 | async-start | bytes 7208960 | tf_op jit(solution)/shard_map/reduce_scatter | solution.py:480
  546.7 159.8 %reduce-scatter.9.cloned.1.call-start = ((), (), s32[]{:S(2)}) async-start(), calls=%async_computation.13 | async-start | bytes 3604480 | tf_op jit(solution)/shard_map/reduce_scatter | solution.py:480
  571.3 27.0 %collective-permute-start.68 = (bf16[256,1024]{1,0:T(8,128)(2,1)S(1)}, bf16[256,1024]{1,0:T(8,128)(2,1)S(1)}, u32[]{:S(2)}, u32[]{:S(2)}) collective-permute-start(bf16[256,1024]{1,0:T(8,128)(2,1)S(1)} %pad_maximum_fusion.45), channel_id=1, source_target_pairs={{0,16},{16,0},{1,17},{17,1},{2,18},{18,2},{3,19},{19,3},{4,20},{20... | collective-permute-start | bytes 1572872 | tf_op jit(solution)/shard_map/ppermute | solution.py:20
  635.9 152.6 %reduce-scatter.11.cloned.1.call-start = ((), (), s32[]{:S(2)}) async-start(), calls=%async_computation.14 | async-start | bytes 5242880 | tf_op jit(solution)/shard_map/reduce_scatter | solution.py:480
  711.6 191.3 %reduce-scatter.15.cloned.1.call-start = ((), (), s32[]{:S(2)}) async-start(), calls=%async_computation.16 | async-start | bytes 7208960 | tf_op jit(solution)/shard_map/reduce_scatter | solution.py:480
  795.8 210.1 %reduce-scatter.17.cloned.1.call-start = ((), (), s32[]{:S(2)}) async-start(), calls=%async_computation.17 | async-start | bytes 5242880 | tf_op jit(solution)/shard_map/reduce_scatter | solution.py:480
  864.8 27.5 %collective-permute-start.93 = (bf16[1,256,2048]{2,1,0:T(8,128)(2,1)}, bf16[1,256,2048]{2,1,0:T(8,128)(2,1)}, u32[]{:S(2)}, u32[]{:S(2)}) collective-permute-start(bf16[1,256,2048]{2,1,0:T(8,128)(2,1)} %fusion.11), channel_id=1, source_target_pairs={{0,1},{1,0},{2,3},{3,2},{4,5},{5,4},{6,7},{7,6},{8,9},{9,8},{10,11... | collective-permute-start | bytes 3145736 | tf_op jit(solution)/shard_map/ppermute | solution.py:20
  902.9 135.7 %reduce-scatter.13.cloned.1.call-start = ((), (), s32[]{:S(2)}) async-start(), calls=%async_computation.15 | async-start | bytes 3604480 | tf_op jit(solution)/shard_map/reduce_scatter | solution.py:480
  916.3 45.4 %collective-permute-start.97 = (bf16[512,1408]{1,0:T(8,128)(2,1)S(1)}, bf16[512,1408]{1,0:T(8,128)(2,1)S(1)}, u32[]{:S(2)}, u32[]{:S(2)}) collective-permute-start(bf16[512,1408]{1,0:T(8,128)(2,1)S(1)} %get-tuple-element.266), channel_id=1, source_target_pairs={{0,16},{16,0},{1,17},{17,1},{2,18},{18,2},{3,19},{19,3},{4,20},{20... | collective-permute-start | bytes 4325384 | tf_op jit(solution)/shard_map/ppermute | solution.py:20
  917.0 44.7 %collective-permute-start.98 = (bf16[512,1408]{1,0:T(8,128)(2,1)S(1)}, bf16[512,1408]{1,0:T(8,128)(2,1)S(1)}, u32[]{:S(2)}, u32[]{:S(2)}) collective-permute-start(bf16[512,1408]{1,0:T(8,128)(2,1)S(1)} %get-tuple-element.168.refs_0_), channel_id=1, source_target_pairs={{0,2},{1,3},{2,0},{3,1},{4,6},{5,7},{6,4},{7,5},{8,10},{9,11},{10,... | collective-permute-start | bytes 4325384 | tf_op jit(solution)/shard_map/ppermute | solution.py:20
  922.3 38.9 %collective-permute-start.96 = (bf16[256,1024]{1,0:T(8,128)(2,1)S(1)}, bf16[256,1024]{1,0:T(8,128)(2,1)S(1)}, u32[]{:S(2)}, u32[]{:S(2)}) collective-permute-start(bf16[256,1024]{1,0:T(8,128)(2,1)S(1)} %pad_maximum_fusion.52), channel_id=1, source_target_pairs={{0,16},{16,0},{1,17},{17,1},{2,18},{18,2},{3,19},{19,3},{4,20},{20... | collective-permute-start | bytes 1572872 | tf_op jit(solution)/shard_map/ppermute | solution.py:20
  924.0 37.5 %collective-permute-start.95 = (bf16[256,1024]{1,0:T(8,128)(2,1)S(1)}, bf16[256,1024]{1,0:T(8,128)(2,1)S(1)}, u32[]{:S(2)}, u32[]{:S(2)}) collective-permute-start(bf16[256,1024]{1,0:T(8,128)(2,1)S(1)} %slice.1035), channel_id=1, source_target_pairs={{0,2},{1,3},{2,0},{3,1},{4,6},{5,7},{6,4},{7,5},{8,10},{9,11},{10,... | collective-permute-start | bytes 1572872 | tf_op jit(solution)/shard_map/ppermute | solution.py:20
  974.0 31.9 %collective-permute-start.101 = (bf16[512,1408]{1,0:T(8,128)(2,1)}, bf16[512,1408]{1,0:T(8,128)(2,1)}, u32[]{:S(2)}, u32[]{:S(2)}) collective-permute-start(bf16[512,1408]{1,0:T(8,128)(2,1)} %copy-done.98), channel_id=1, source_target_pairs={{0,2},{1,3},{2,0},{3,1},{4,6},{5,7},{6,4},{7,5},{8,10},{9,11},{10,... | collective-permute-start | bytes 4325384 | tf_op jit(solution)/shard_map/ppermute | solution.py:20
  975.5 35.3 %collective-permute-start.105 = (bf16[512,1408]{1,0:T(8,128)(2,1)S(1)}, bf16[512,1408]{1,0:T(8,128)(2,1)}, u32[]{:S(2)}, u32[]{:S(2)}) collective-permute-start(bf16[512,1408]{1,0:T(8,128)(2,1)S(1)} %get-tuple-element.168.refs_0_), channel_id=1, source_target_pairs={{0,1},{1,0},{2,3},{3,2},{4,5},{5,4},{6,7},{7,6},{8,9},{9,8},{10,11... | collective-permute-start | bytes 4325384 | tf_op jit(solution)/shard_map/ppermute | solution.py:20
  1010.8 27.8 %collective-permute-start.102 = (bf16[512,1024]{1,0:T(8,128)(2,1)}, bf16[512,1024]{1,0:T(8,128)(2,1)S(1)}, u32[]{:S(2)}, u32[]{:S(2)}) collective-permute-start(bf16[512,1024]{1,0:T(8,128)(2,1)} %get-tuple-element.271), channel_id=1, source_target_pairs={{0,16},{16,0},{1,17},{17,1},{2,18},{18,2},{3,19},{19,3},{4,20},{20... | collective-permute-start | bytes 3145736 | tf_op jit(solution)/shard_map/ppermute | solution.py:20
  1041.0 29.1 %collective-permute-start.112 = (bf16[2,144,2048]{2,1,0:T(8,128)(2,1)}, bf16[2,144,2048]{2,1,0:T(8,128)(2,1)S(1)}, u32[]{:S(2)}, u32[]{:S(2)}) collective-permute-start(bf16[2,144,2048]{2,1,0:T(8,128)(2,1)} %pad_maximum_fusion.11), channel_id=1, source_target_pairs={{0,16},{16,0},{1,17},{17,1},{2,18},{18,2},{3,19},{19,3},{4,20},{20... | collective-permute-start | bytes 3538952 | tf_op jit(solution)/shard_map/ppermute | solution.py:20
  1042.0 39.9 %collective-permute-start.111 = (bf16[512,1024]{1,0:T(8,128)(2,1)S(1)}, bf16[512,1024]{1,0:T(8,128)(2,1)}, u32[]{:S(2)}, u32[]{:S(2)}) collective-permute-start(bf16[512,1024]{1,0:T(8,128)(2,1)S(1)} %collective-permute-done.102.refs_4_), channel_id=1, source_target_pairs={{0,2},{1,3},{2,0},{3,1},{4,6},{5,7},{6,4},{7,5},{8,10},{9,11},{10,... | collective-permute-start | bytes 3145736 | tf_op jit(solution)/shard_map/ppermute | solution.py:20
  1045.0 36.9 %collective-permute-start.109 = (bf16[176,2048]{1,0:T(8,128)(2,1)S(1)}, bf16[176,2048]{1,0:T(8,128)(2,1)S(1)}, u32[]{:S(2)}, u32[]{:S(2)}) collective-permute-start(bf16[176,2048]{1,0:T(8,128)(2,1)S(1)} %get-tuple-element.303), channel_id=1, source_target_pairs={{0,16},{16,0},{1,17},{17,1},{2,18},{18,2},{3,19},{19,3},{4,20},{20... | collective-permute-start | bytes 2162696 | tf_op jit(solution)/shard_map/ppermute | solution.py:20
  1046.1 35.8 %collective-permute-start.110 = (bf16[176,2048]{1,0:T(8,128)(2,1)S(1)}, bf16[176,2048]{1,0:T(8,128)(2,1)S(1)}, u32[]{:S(2)}, u32[]{:S(2)}) collective-permute-start(bf16[176,2048]{1,0:T(8,128)(2,1)S(1)} %get-tuple-element.302.refs_0_), channel_id=1, source_target_pairs={{0,2},{1,3},{2,0},{3,1},{4,6},{5,7},{6,4},{7,5},{8,10},{9,11},{10,... | collective-permute-start | bytes 2162696 | tf_op jit(solution)/shard_map/ppermute | solution.py:20
  1091.4 26.9 %collective-permute-start.121 = (bf16[176,2048]{1,0:T(8,128)(2,1)S(1)}, bf16[176,2048]{1,0:T(8,128)(2,1)S(1)}, u32[]{:S(2)}, u32[]{:S(2)}) collective-permute-start(bf16[176,2048]{1,0:T(8,128)(2,1)S(1)} %get-tuple-element.302.refs_0_), channel_id=1, source_target_pairs={{0,1},{1,0},{2,3},{3,2},{4,5},{5,4},{6,7},{7,6},{8,9},{9,8},{10,11... | collective-permute-start | bytes 2162696 | tf_op jit(solution)/shard_map/ppermute | solution.py:20
  (251 other events, 2301.3 us)
Sparse Core Ops, SparseCore 0:
  19.6 83.4 all-gather.6
  105.3 79.4 all-gather.8
  186.9 105.2 all-gather.10
  294.2 57.4 all-gather.12
  356.8 58.0 all-gather.14
  416.2 105.3 all-gather.16
  546.8 100.5 reduce-scatter.6
  649.7 56.7 reduce-scatter.8
  711.7 76.7 reduce-scatter.10
  795.9 102.8 reduce-scatter.14
  903.1 76.0 reduce-scatter.16
  981.9 56.6 reduce-scatter.12

commit v4 on v3

--- a/solution.py
+++ b/solution.py
@@ -593,11 +593,14 @@
     )
 
     across = rep_stages[0]
-    d_dealt, mix_0, gate_up_diagonal, back_places = lax.optimization_barrier(
-        (d_dealt, mix_0, swap(gate_up_begun[1], across), back_places)
+    small = jnp.concatenate([small_first, small_second])
+    for stage in shard_stages:
+        small = small + swap(small, stage)
+    d_dealt, mix_0, gate_up_diagonal, back_places, small = lax.optimization_barrier(
+        (d_dealt, mix_0, swap(gate_up_begun[1], across), back_places, small)
     )
     mix_own, mix_other, mix_across = begin_collect(mix_0, mix_1)
-    rows_sent = [d_dealt, small_first, small_second, jnp.zeros((8, model_width), F32)]
+    rows_sent = [d_dealt, small, jnp.zeros((8, model_width), F32)]
     grads = spread(jnp.concatenate(rows_sent).astype(BF16)[None], rep_stages[:1])
     gate, up = place_columns(collect(*gate_up_begun, gate_up_diagonal), ident, shards)
     down_0, mix_other, mix_across, grads, gate, up = lax.optimization_barrier(
@@ -609,7 +612,8 @@
         (down_other, down_across, mix_diagonal, spread(grads, stages[:1]))
     )
     down_diagonal = swap(down_other, across)
-    all_grads = spread(grads, rep_stages[1:])
+    grads = spread(grads, rep_stages[1:-1])
+    far_grads = swap(grads, stages[-1])
     sources = [ident ^ code for code in range(group)]
     columns = jnp.stack(
         [head_number(device, t) * head for device in sources for t in range(per_device)]
@@ -624,16 +628,22 @@
         each * head,
         model_width,
     )
-    small = jnp.sum(all_grads[:, length:].astype(F32), axis=0)[:8].reshape(2, 4, model_width)
-    small = jnp.where(on_first, small[0], small[1])
-    for stage in shard_stages:
-        small = small + swap(small, stage)
-    small = lax.dynamic_slice_in_dim(small, shard * local_rows, local_rows, 1)
-
-    back_rows = [
-        lax.dynamic_slice(all_grads, (back_places[number], 0, 0), (1, length, model_width))
-        for number in range(micro)
-    ]
+    small = jnp.sum(grads[:, length:].astype(F32), axis=0)
+    small = (small + jnp.sum(far_grads[:, length:].astype(F32), axis=0))[:8]
+    small = lax.dynamic_slice(
+        small, (4 * section, shard * local_rows), (4, local_rows)
+    )
+
+    near_count = grads.shape[0]
+    back_rows = []
+    for number in range(micro):
+        place = back_places[number]
+        start = (place % near_count, 0, 0)
+        near, far = [
+            lax.dynamic_slice(value, start, (1, length, model_width))
+            for value in (grads, far_grads)
+        ]
+        back_rows.append(jnp.where(place < near_count, near, far))
     boundary_out = jnp.where(on_first, jnp.concatenate(back_rows), second_rows).reshape(
         1, micro * length, model_width
     )

time: 1140 us -> 1130 us (level)
    unnamed x304 -> x317, local copies, waits for them, and re-layouts: 46.5 us -> 42.1 us
  transfers between devices with their start and end apart: 137 -> 137, of which waited for: 75 -> 76; matrix products, arithmetic and copies ran while one was open for 35% -> 35% of each run, Pallas kernels for 3% -> 3%
where the time goes in v4:
time: 1130 us
  waiting for transfers between devices  479 us (42%)
  matrix products  192 us (17%)
  local copies, waits for them, and re-layouts  146 us (13%)
  other arithmetic  130 us (12%)
  starting transfers between devices  111 us (10%)
  Pallas kernels  44.1 us (4%)
  between operations  23.2 us (2%)
    ppermute x122, waiting for transfers between devices, swap(): lax.ppermute(block, axis, [(i, i ^ distance) for i in range(lax.axis_size...  360 us
    ppermute x122, starting transfers between devices, swap(): lax.ppermute(block, axis, [(i, i ^ distance) for i in range(lax.axis_size...  101 us
    all_gather x6, waiting for transfers between devices, over_shard(): return lax.all_gather(piece, 'shard', axis=0, tiled=True)  83.2 us
    dot_general x12, matrix products, product_t(): lax.dot_general(left, right, (((1,), (1,)), ((), ())), preferred_element_...  63.9 us
    dot_general x12, matrix products, product(): return jnp.dot(left, right, preferred_element_type=F32)  56.1 us
    dot_general x8, matrix products, weight_term(): lax.dot_general(act_rows, grad_rows, (((0,), (0,)), ((), ())), preferred_...  46 us
    unnamed x317, local copies, waits for them, and re-layouts  42.1 us
  transfers between devices with their start and end apart: 137, of which 76 were waited for; matrix products, arithmetic and copies ran while one was open for 35% of the time, Pallas kernels for 3%

profile of v4, /device:TPU:0, one launch (start us, length us, event | category | flops | bytes accessed | tf_op | source)
XLA Modules:
  0.0 1125.7 jit_solution(12123724482139445014)
XLA Ops:
  46.8 25.4 %collective-permute-done.9 = bf16[512,1024]{1,0:T(8,128)(2,1)S(1)} collective-permute-done((bf16[512,1024]{1,0:T(8,128)(2,1)}, bf16[512,1024]{1,0:T(8,128)(2,1)S(1)}, u32[]{:S(2)}, u32[]{:S(2)}) %collective-permute-start.9) | collective-permute-done | bytes 1048608 | tf_op jit(solution)/shard_map/ppermute | solution.py:20
  144.2 40.6 %all-gather.9.cloned.1.call-done = bf16[2048,1024]{1,0:T(8,128)(2,1)} async-done(((bf16[512,1024]{1,0:T(8,128)(2,1)}), bf16[2048,1024]{1,0:T(8,128)(2,1)}) %all-gather.9.cloned.1.call-update) | async-done | bytes 4194320 | tf_op jit(solution)/shard_map/all_gather | solution.py:371
  223.4 14.9 %collective-permute-done = bf16[128,2048]{1,0:T(8,128)(2,1)S(1)} collective-permute-done((bf16[128,2048]{1,0:T(8,128)(2,1)S(1)}, bf16[128,2048]{1,0:T(8,128)(2,1)S(1)}, u32[]{:S(2)}, u32[]{:S(2)}) %collective-permute-start) | collective-permute-done | bytes 524320 | tf_op jit(solution)/shard_map/ppermute | solution.py:24
  241.8 11.9 %collective-permute-done.13 = bf16[256,1024]{1,0:T(8,128)(2,1)S(1)} collective-permute-done((bf16[256,1024]{1,0:T(8,128)(2,1)S(1)}, bf16[256,1024]{1,0:T(8,128)(2,1)S(1)}, u32[]{:S(2)}, u32[]{:S(2)}) %collective-permute-start.13) | collective-permute-done | bytes 524320 | tf_op jit(solution)/shard_map/ppermute | solution.py:20
  307.6 10.5 fusion.197
  320.7 31.0 %all-gather.13.cloned.1.call-done = bf16[704,2048]{1,0:T(8,128)(2,1)} async-done(((bf16[176,2048]{1,0:T(8,128)(2,1)}), bf16[704,2048]{1,0:T(8,128)(2,1)}) %all-gather.13.cloned.1.call-update) | async-done | bytes 2883600 | tf_op jit(solution)/shard_map/all_gather | solution.py:371
  369.1 10.8 collective-permute-done.31
  463.1 10.9 collective-permute-done.43
  513.4 8.3 all-gather.17.cloned.1.call-done
  521.7 10.8 fusion.200
  538.0 8.6 convolution_convert_fusion.1
  552.0 7.9 convolution_convert_fusion.13
  586.3 8.4 collective-permute-done.54
  600.0 7.4 collective-permute-done.55
  620.9 9.7 collective-permute-done.61
  676.5 7.5 convolution_convert_fusion.3
  694.8 11.7 %reduce-scatter.9.cloned.1.call-done = bf16[176,2048]{1,0:T(8,128)(2,1)} async-done(((bf16[704,2048]{1,0:T(8,128)(2,1)}), bf16[176,2048]{1,0:T(8,128)(2,1)}) %reduce-scatter.9.cloned.1.call-update) | async-done | bytes 720912 | tf_op jit(solution)/shard_map/reduce_scatter | solution.py:480
  724.3 10.9 collective-permute-done.72
  755.4 9.9 collective-permute-done.79
  777.9 8.7 convolution_convert_fusion
  788.5 7.3 convolution_convert_fusion.12
  800.3 7.7 fusion.195
  810.9 11.0 collective-permute-done.83
  845.3 9.8 collective-permute-done.90
  884.9 7.5 convolution_convert_fusion.2
  927.6 33.2 %collective-permute-done.96 = bf16[256,1024]{1,0:T(8,128)(2,1)S(1)} collective-permute-done((bf16[256,1024]{1,0:T(8,128)(2,1)S(1)}, bf16[256,1024]{1,0:T(8,128)(2,1)S(1)}, u32[]{:S(2)}, u32[]{:S(2)}) %collective-permute-start.96) | collective-permute-done | bytes 524320 | tf_op jit(solution)/shard_map/ppermute | solution.py:20
  996.6 12.3 %collective-permute-done.101.refs_6_ = bf16[512,1408]{1,0:T(8,128)(2,1)} collective-permute-done((bf16[512,1408]{1,0:T(8,128)(2,1)}, bf16[512,1408]{1,0:T(8,128)(2,1)}, u32[]{:S(2)}, u32[]{:S(2)}) %collective-permute-start.101) | collective-permute-done | bytes 1441824 | tf_op jit(solution)/shard_map/ppermute | solution.py:20
  1014.1 8.3 collective-permute-done.106
  1027.5 12.6 %shard_map.371 = (f32[512,5632]{1,0:T(8,128)}, f32[512,5632]{1,0:T(8,128)}) custom-call(s32[1]{0:T(128)} %bitcast.161.ident_ref, bf16[512,1408]{1,0:T(8,128)(2,1)S(1)} %get-tuple-element.170.refs_0_, bf16[512,1408]{1,0:T(8,128)(2,1)} %collective-permute-done.107.refs_1_, bf16[512,1408]{1,0:T(8,128)(2,1)S(1)} %copy-done.14, ...), custom_call_target="tpu_custom_call" | custom-call | tf_op jit(solution)/shard_map/pallas_call | solution.py:211
  1051.0 23.6 %collective-permute-done.114 = bf16[2,144,2048]{2,1,0:T(8,128)(2,1)S(1)} collective-permute-done((bf16[2,144,2048]{2,1,0:T(8,128)(2,1)}, bf16[2,144,2048]{2,1,0:T(8,128)(2,1)S(1)}, u32[]{:S(2)}, u32[]{:S(2)}) %collective-permute-start.114) | collective-permute-done | bytes 1179680 | tf_op jit(solution)/shard_map/ppermute | solution.py:20
  1076.2 7.9 collective-permute-done.111.refs_4_
  1095.2 10.1 shard_map.372
  (951 shorter events, 685.4 us)
Async XLA Ops:
  7.2 137.0 %all-gather.7.cloned.1.call-start = ((), (), s32[]{:S(2)}) async-start(), calls=%async_computation.6 | async-start | bytes 5242880 | tf_op jit(solution)/shard_map/all_gather | solution.py:371
  19.5 165.2 %all-gather.9.cloned.1.call-start = ((), (), s32[]{:S(2)}) async-start(), calls=%async_computation.7 | async-start | bytes 5242880 | tf_op jit(solution)/shard_map/all_gather | solution.py:371
  19.7 58.7 %collective-permute-start.1 = (s32[1,2,5]{2,1,0:T(2,128)S(1)}, s32[1,2,5]{2,1,0:T(2,128)S(1)}, u32[]{:S(2)}, u32[]{:S(2)}) collective-permute-start(s32[1,2,5]{2,1,0:T(2,128)S(1)} %add_bitcast_fusion), channel_id=1, source_target_pairs={{0,2},{1,3},{2,0},{3,1},{4,6},{5,7},{6,4},{7,5},{8,10},{9,11},{10,... | collective-permute-start | bytes 128 | tf_op jit(solution)/shard_map/ppermute | solution.py:20
  22.7 61.6 %collective-permute-start.3 = (bf16[2,128,2048]{2,1,0:T(8,128)(2,1)S(1)}, bf16[2,128,2048]{2,1,0:T(8,128)(2,1)}, u32[]{:S(2)}, u32[]{:S(2)}) collective-permute-start(bf16[2,128,2048]{2,1,0:T(8,128)(2,1)S(1)} %bitcast.599), channel_id=1, source_target_pairs={{0,16},{1,17},{2,18},{3,19},{4,20},{5,21},{6,22},{7,23},{8,24},{9,... | collective-permute-start | bytes 3145736 | tf_op jit(solution)/shard_map/ppermute | solution.py:24
  27.7 62.9 %collective-permute-start.6 = (bf16[1,4,512]{2,1,0:T(4,128)(2,1)}, bf16[1,4,512]{2,1,0:T(4,128)(2,1)}, u32[]{:S(2)}, u32[]{:S(2)}) collective-permute-start(bf16[1,4,512]{2,1,0:T(4,128)(2,1)} %maximum_bitcast_fusion), channel_id=1, source_target_pairs={{0,8},{4,12},{8,0},{12,4},{1,9},{5,13},{9,1},{13,5},{2,10},{6,14},... | collective-permute-start | bytes 12296 | tf_op jit(solution)/shard_map/ppermute | solution.py:20
  31.0 41.2 %collective-permute-start.9 = (bf16[512,1024]{1,0:T(8,128)(2,1)}, bf16[512,1024]{1,0:T(8,128)(2,1)S(1)}, u32[]{:S(2)}, u32[]{:S(2)}) collective-permute-start(bf16[512,1024]{1,0:T(8,128)(2,1)} %maximum_dynamic-update-slice_fusion.1), channel_id=1, source_target_pairs={{0,16},{16,0},{1,17},{17,1},{2,18},{18,2},{3,19},{19,3},{4,20},{20... | collective-permute-start | bytes 3145736 | tf_op jit(solution)/shard_map/ppermute | solution.py:20
  33.1 89.6 %collective-permute-start.10 = (bf16[176,2048]{1,0:T(8,128)(2,1)}, bf16[176,2048]{1,0:T(8,128)(2,1)}, u32[]{:S(2)}, u32[]{:S(2)}) collective-permute-start(bf16[176,2048]{1,0:T(8,128)(2,1)} %dynamic-slice_bitcast_fusion), channel_id=1, source_target_pairs={{0,16},{16,0},{1,17},{17,1},{2,18},{18,2},{3,19},{19,3},{4,20},{20... | collective-permute-start | bytes 2162696 | tf_op jit(solution)/shard_map/ppermute | solution.py:20
  72.3 53.2 %collective-permute-start.23 = (bf16[512,1408]{1,0:T(8,128)(2,1)}, bf16[512,1408]{1,0:T(8,128)(2,1)}, u32[]{:S(2)}, u32[]{:S(2)}) collective-permute-start(bf16[512,1408]{1,0:T(8,128)(2,1)} %concatenate.341), channel_id=1, source_target_pairs={{0,16},{16,0},{1,17},{17,1},{2,18},{18,2},{3,19},{19,3},{4,20},{20... | collective-permute-start | bytes 4325384 | tf_op jit(solution)/shard_map/ppermute | solution.py:20
  74.7 232.9 %all-gather.11.cloned.1.call-start = ((), (), s32[]{:S(2)}) async-start(), calls=%async_computation.8 | async-start | bytes 7208960 | tf_op jit(solution)/shard_map/all_gather | solution.py:371
  84.4 25.6 %collective-permute-start.4 = (bf16[2,128,2048]{2,1,0:T(8,128)(2,1)S(1)}, bf16[2,128,2048]{2,1,0:T(8,128)(2,1)S(1)}, u32[]{:S(2)}, u32[]{:S(2)}) collective-permute-start(bf16[2,128,2048]{2,1,0:T(8,128)(2,1)S(1)} %broadcast_select_fusion.8), channel_id=1, source_target_pairs={{0,2},{1,3},{2,0},{3,1},{4,6},{5,7},{6,4},{7,5},{8,10},{9,11},{10,... | collective-permute-start | bytes 3145736 | tf_op jit(solution)/shard_map/ppermute | solution.py:20
  128.7 223.0 %all-gather.13.cloned.1.call-start = ((), (), s32[]{:S(2)}) async-start(), calls=%async_computation.9 | async-start | bytes 3604480 | tf_op jit(solution)/shard_map/all_gather | solution.py:371
  279.9 134.9 %all-gather.15.cloned.1.call-start = ((), (), s32[]{:S(2)}) async-start(), calls=%async_computation.10 | async-start | bytes 3604480 | tf_op jit(solution)/shard_map/all_gather | solution.py:371
  356.7 165.0 %all-gather.17.cloned.1.call-start = ((), (), s32[]{:S(2)}) async-start(), calls=%async_computation.11 | async-start | bytes 7208960 | tf_op jit(solution)/shard_map/all_gather | solution.py:371
  416.1 237.1 %reduce-scatter.7.cloned.1.call-start = ((), (), s32[]{:S(2)}) async-start(), calls=%async_computation.12 | async-start | bytes 7208960 | tf_op jit(solution)/shard_map/reduce_scatter | solution.py:480
  546.7 159.8 %reduce-scatter.9.cloned.1.call-start = ((), (), s32[]{:S(2)}) async-start(), calls=%async_computation.13 | async-start | bytes 3604480 | tf_op jit(solution)/shard_map/reduce_scatter | solution.py:480
  571.3 27.0 %collective-permute-start.68 = (bf16[256,1024]{1,0:T(8,128)(2,1)S(1)}, bf16[256,1024]{1,0:T(8,128)(2,1)S(1)}, u32[]{:S(2)}, u32[]{:S(2)}) collective-permute-start(bf16[256,1024]{1,0:T(8,128)(2,1)S(1)} %pad_maximum_fusion.45), channel_id=1, source_target_pairs={{0,16},{16,0},{1,17},{17,1},{2,18},{18,2},{3,19},{19,3},{4,20},{20... | collective-permute-start | bytes 1572872 | tf_op jit(solution)/shard_map/ppermute | solution.py:20
  635.9 152.6 %reduce-scatter.11.cloned.1.call-start = ((), (), s32[]{:S(2)}) async-start(), calls=%async_computation.14 | async-start | bytes 5242880 | tf_op jit(solution)/shard_map/reduce_scatter | solution.py:480
  711.6 191.5 %reduce-scatter.15.cloned.1.call-start = ((), (), s32[]{:S(2)}) async-start(), calls=%async_computation.16 | async-start | bytes 7208960 | tf_op jit(solution)/shard_map/reduce_scatter | solution.py:480
  795.8 213.1 %reduce-scatter.17.cloned.1.call-start = ((), (), s32[]{:S(2)}) async-start(), calls=%async_computation.17 | async-start | bytes 5242880 | tf_op jit(solution)/shard_map/reduce_scatter | solution.py:480
  864.8 27.6 %collective-permute-start.93 = (bf16[1,256,2048]{2,1,0:T(8,128)(2,1)}, bf16[1,256,2048]{2,1,0:T(8,128)(2,1)}, u32[]{:S(2)}, u32[]{:S(2)}) collective-permute-start(bf16[1,256,2048]{2,1,0:T(8,128)(2,1)} %fusion.11), channel_id=1, source_target_pairs={{0,1},{1,0},{2,3},{3,2},{4,5},{5,4},{6,7},{7,6},{8,9},{9,8},{10,11... | collective-permute-start | bytes 3145736 | tf_op jit(solution)/shard_map/ppermute | solution.py:20
  903.1 137.0 %reduce-scatter.13.cloned.1.call-start = ((), (), s32[]{:S(2)}) async-start(), calls=%async_computation.15 | async-start | bytes 3604480 | tf_op jit(solution)/shard_map/reduce_scatter | solution.py:480
  915.9 45.6 %collective-permute-start.97 = (bf16[512,1408]{1,0:T(8,128)(2,1)S(1)}, bf16[512,1408]{1,0:T(8,128)(2,1)}, u32[]{:S(2)}, u32[]{:S(2)}) collective-permute-start(bf16[512,1408]{1,0:T(8,128)(2,1)S(1)} %get-tuple-element.268), channel_id=1, source_target_pairs={{0,16},{16,0},{1,17},{17,1},{2,18},{18,2},{3,19},{19,3},{4,20},{20... | collective-permute-start | bytes 4325384 | tf_op jit(solution)/shard_map/ppermute | solution.py:20
  916.6 44.9 %collective-permute-start.98 = (bf16[512,1408]{1,0:T(8,128)(2,1)S(1)}, bf16[512,1408]{1,0:T(8,128)(2,1)S(1)}, u32[]{:S(2)}, u32[]{:S(2)}) collective-permute-start(bf16[512,1408]{1,0:T(8,128)(2,1)S(1)} %get-tuple-element.170.refs_0_), channel_id=1, source_target_pairs={{0,2},{1,3},{2,0},{3,1},{4,6},{5,7},{6,4},{7,5},{8,10},{9,11},{10,... | collective-permute-start | bytes 4325384 | tf_op jit(solution)/shard_map/ppermute | solution.py:20
  921.3 39.5 %collective-permute-start.96 = (bf16[256,1024]{1,0:T(8,128)(2,1)S(1)}, bf16[256,1024]{1,0:T(8,128)(2,1)S(1)}, u32[]{:S(2)}, u32[]{:S(2)}) collective-permute-start(bf16[256,1024]{1,0:T(8,128)(2,1)S(1)} %pad_maximum_fusion.52), channel_id=1, source_target_pairs={{0,16},{16,0},{1,17},{17,1},{2,18},{18,2},{3,19},{19,3},{4,20},{20... | collective-permute-start | bytes 1572872 | tf_op jit(solution)/shard_map/ppermute | solution.py:20
  926.3 35.0 %collective-permute-start.95 = (bf16[256,1024]{1,0:T(8,128)(2,1)S(1)}, bf16[256,1024]{1,0:T(8,128)(2,1)S(1)}, u32[]{:S(2)}, u32[]{:S(2)}) collective-permute-start(bf16[256,1024]{1,0:T(8,128)(2,1)S(1)} %slice.1042), channel_id=1, source_target_pairs={{0,2},{1,3},{2,0},{3,1},{4,6},{5,7},{6,4},{7,5},{8,10},{9,11},{10,... | collective-permute-start | bytes 1572872 | tf_op jit(solution)/shard_map/ppermute | solution.py:20
  976.4 32.5 %collective-permute-start.101 = (bf16[512,1408]{1,0:T(8,128)(2,1)}, bf16[512,1408]{1,0:T(8,128)(2,1)}, u32[]{:S(2)}, u32[]{:S(2)}) collective-permute-start(bf16[512,1408]{1,0:T(8,128)(2,1)} %collective-permute-done.97.refs_4_), channel_id=1, source_target_pairs={{0,2},{1,3},{2,0},{3,1},{4,6},{5,7},{6,4},{7,5},{8,10},{9,11},{10,... | collective-permute-start | bytes 4325384 | tf_op jit(solution)/shard_map/ppermute | solution.py:20
  986.3 27.1 %collective-permute-start.107 = (bf16[512,1408]{1,0:T(8,128)(2,1)S(1)}, bf16[512,1408]{1,0:T(8,128)(2,1)}, u32[]{:S(2)}, u32[]{:S(2)}) collective-permute-start(bf16[512,1408]{1,0:T(8,128)(2,1)S(1)} %get-tuple-element.170.refs_0_), channel_id=1, source_target_pairs={{0,1},{1,0},{2,3},{3,2},{4,5},{5,4},{6,7},{7,6},{8,9},{9,8},{10,11... | collective-permute-start | bytes 4325384 | tf_op jit(solution)/shard_map/ppermute | solution.py:20
  1013.4 26.7 %collective-permute-start.104 = (bf16[512,1024]{1,0:T(8,128)(2,1)}, bf16[512,1024]{1,0:T(8,128)(2,1)S(1)}, u32[]{:S(2)}, u32[]{:S(2)}) collective-permute-start(bf16[512,1024]{1,0:T(8,128)(2,1)} %get-tuple-element.273), channel_id=1, source_target_pairs={{0,16},{16,0},{1,17},{17,1},{2,18},{18,2},{3,19},{19,3},{4,20},{20... | collective-permute-start | bytes 3145736 | tf_op jit(solution)/shard_map/ppermute | solution.py:20
  1045.4 29.1 %collective-permute-start.114 = (bf16[2,144,2048]{2,1,0:T(8,128)(2,1)}, bf16[2,144,2048]{2,1,0:T(8,128)(2,1)S(1)}, u32[]{:S(2)}, u32[]{:S(2)}) collective-permute-start(bf16[2,144,2048]{2,1,0:T(8,128)(2,1)} %pad_maximum_fusion.11), channel_id=1, source_target_pairs={{0,16},{16,0},{1,17},{17,1},{2,18},{18,2},{3,19},{19,3},{4,20},{20... | collective-permute-start | bytes 3538952 | tf_op jit(solution)/shard_map/ppermute | solution.py:20
  1045.4 38.7 %collective-permute-start.113 = (bf16[512,1024]{1,0:T(8,128)(2,1)S(1)}, bf16[512,1024]{1,0:T(8,128)(2,1)}, u32[]{:S(2)}, u32[]{:S(2)}) collective-permute-start(bf16[512,1024]{1,0:T(8,128)(2,1)S(1)} %collective-permute-done.104.refs_4_), channel_id=1, source_target_pairs={{0,2},{1,3},{2,0},{3,1},{4,6},{5,7},{6,4},{7,5},{8,10},{9,11},{10,... | collective-permute-start | bytes 3145736 | tf_op jit(solution)/shard_map/ppermute | solution.py:20
  1048.1 36.0 %collective-permute-start.111 = (bf16[176,2048]{1,0:T(8,128)(2,1)S(1)}, bf16[176,2048]{1,0:T(8,128)(2,1)S(1)}, u32[]{:S(2)}, u32[]{:S(2)}) collective-permute-start(bf16[176,2048]{1,0:T(8,128)(2,1)S(1)} %get-tuple-element.305), channel_id=1, source_target_pairs={{0,16},{16,0},{1,17},{17,1},{2,18},{18,2},{3,19},{19,3},{4,20},{20... | collective-permute-start | bytes 2162696 | tf_op jit(solution)/shard_map/ppermute | solution.py:20
  1050.0 34.1 %collective-permute-start.112 = (bf16[176,2048]{1,0:T(8,128)(2,1)S(1)}, bf16[176,2048]{1,0:T(8,128)(2,1)S(1)}, u32[]{:S(2)}, u32[]{:S(2)}) collective-permute-start(bf16[176,2048]{1,0:T(8,128)(2,1)S(1)} %get-tuple-element.304.refs_0_), channel_id=1, source_target_pairs={{0,2},{1,3},{2,0},{3,1},{4,6},{5,7},{6,4},{7,5},{8,10},{9,11},{10,... | collective-permute-start | bytes 2162696 | tf_op jit(solution)/shard_map/ppermute | solution.py:20
  (258 other events, 2623.5 us)
Sparse Core Ops, SparseCore 0:
  19.6 83.4 all-gather.6
  105.3 79.4 all-gather.8
  186.9 105.2 all-gather.10
  294.2 57.4 all-gather.12
  356.8 58.0 all-gather.14
  416.3 105.3 all-gather.16
  546.8 100.5 reduce-scatter.6
  649.7 56.7 reduce-scatter.8
  711.7 76.7 reduce-scatter.10
  795.9 102.8 reduce-scatter.14
  903.2 76.1 reduce-scatter.16
  982.1 57.2 reduce-scatter.12

commit v5 on v4

--- a/solution.py
+++ b/solution.py
@@ -621,13 +621,6 @@
     corners = []
     for device in sources:
         corners += [device // sharing * each * head, device % sharing * (model_width // sharing)]
-    query, forget, into, out = place_mixer(
-        collect(mix_own, mix_other, mix_across, mix_diagonal),
-        columns,
-        jnp.stack(corners),
-        each * head,
-        model_width,
-    )
     small = jnp.sum(grads[:, length:].astype(F32), axis=0)
     small = (small + jnp.sum(far_grads[:, length:].astype(F32), axis=0))[:8]
     small = lax.dynamic_slice(
@@ -647,11 +640,16 @@
     boundary_out = jnp.where(on_first, jnp.concatenate(back_rows), second_rows).reshape(
         1, micro * length, model_width
     )
-    mixer_grads = (query, forget, into, out)
-    down_diagonal, mixer_grads, boundary_out, small = lax.optimization_barrier(
-        (down_diagonal, mixer_grads, boundary_out, small)
-    )
-    query, forget, into, out = mixer_grads
+    down_diagonal, boundary_out, small = lax.optimization_barrier(
+        (down_diagonal, boundary_out, small)
+    )
+    query, forget, into, out = place_mixer(
+        collect(mix_own, mix_other, mix_across, mix_diagonal),
+        columns,
+        jnp.stack(corners),
+        each * head,
+        model_width,
+    )
     down = place_rows(collect(down_own, down_other, down_across, down_diagonal), ident)
 
     return (

time: 1130 us -> 1150 us (1.018)
    unnamed x317 -> x321, local copies, waits for them, and re-layouts: 42.1 us -> 45.9 us
  transfers between devices with their start and end apart: 137 -> 137, of which waited for: 76 -> 72; matrix products, arithmetic and copies ran while one was open for 35% -> 34% of each run, Pallas kernels for 3% -> 3%
where the time goes in v5:
time: 1150 us; the launch traced here: 1140 us
  waiting for transfers between devices  487 us (42%)
  matrix products  192 us (17%)
  local copies, waits for them, and re-layouts  150 us (13%)
  other arithmetic  129 us (11%)
  starting transfers between devices  112 us (10%)
  Pallas kernels  45.8 us (4%)
  between operations  23.2 us (2%)
    ppermute x122, waiting for transfers between devices, swap(): lax.ppermute(block, axis, [(i, i ^ distance) for i in range(lax.axis_size...  368 us
    ppermute x122, starting transfers between devices, swap(): lax.ppermute(block, axis, [(i, i ^ distance) for i in range(lax.axis_size...  102 us
    all_gather x6, waiting for transfers between devices, over_shard(): return lax.all_gather(piece, 'shard', axis=0, tiled=True)  83.1 us
    dot_general x12, matrix products, product_t(): lax.dot_general(left, right, (((1,), (1,)), ((), ())), preferred_element_...  64 us
    dot_general x12, matrix products, product(): return jnp.dot(left, right, preferred_element_type=F32)  56.1 us
    dot_general x8, matrix products, weight_term(): lax.dot_general(act_rows, grad_rows, (((0,), (0,)), ((), ())), preferred_...  46 us
    unnamed x321, local copies, waits for them, and re-layouts  45.9 us
  transfers between devices with their start and end apart: 137, of which 72 were waited for; matrix products, arithmetic and copies ran while one was open for 34% of the time, Pallas kernels for 3%

profile of v5, /device:TPU:0, one launch (start us, length us, event | category | flops | bytes accessed | tf_op | source)
XLA Modules:
  0.0 1140.0 jit_solution(3833086789641767900)
XLA Ops:
  46.8 25.4 %collective-permute-done.9 = bf16[512,1024]{1,0:T(8,128)(2,1)S(1)} collective-permute-done((bf16[512,1024]{1,0:T(8,128)(2,1)}, bf16[512,1024]{1,0:T(8,128)(2,1)S(1)}, u32[]{:S(2)}, u32[]{:S(2)}) %collective-permute-start.9) | collective-permute-done | bytes 1048608 | tf_op jit(solution)/shard_map/ppermute | solution.py:20
  144.2 40.6 %all-gather.9.cloned.1.call-done = bf16[2048,1024]{1,0:T(8,128)(2,1)} async-done(((bf16[512,1024]{1,0:T(8,128)(2,1)}), bf16[2048,1024]{1,0:T(8,128)(2,1)}) %all-gather.9.cloned.1.call-update) | async-done | bytes 4194320 | tf_op jit(solution)/shard_map/all_gather | solution.py:371
  223.4 14.9 %collective-permute-done = bf16[128,2048]{1,0:T(8,128)(2,1)S(1)} collective-permute-done((bf16[128,2048]{1,0:T(8,128)(2,1)S(1)}, bf16[128,2048]{1,0:T(8,128)(2,1)S(1)}, u32[]{:S(2)}, u32[]{:S(2)}) %collective-permute-start) | collective-permute-done | bytes 524320 | tf_op jit(solution)/shard_map/ppermute | solution.py:24
  241.8 11.9 %collective-permute-done.13 = bf16[256,1024]{1,0:T(8,128)(2,1)S(1)} collective-permute-done((bf16[256,1024]{1,0:T(8,128)(2,1)S(1)}, bf16[256,1024]{1,0:T(8,128)(2,1)S(1)}, u32[]{:S(2)}, u32[]{:S(2)}) %collective-permute-start.13) | collective-permute-done | bytes 524320 | tf_op jit(solution)/shard_map/ppermute | solution.py:20
  307.5 10.5 fusion.197
  320.6 31.1 %all-gather.13.cloned.1.call-done = bf16[704,2048]{1,0:T(8,128)(2,1)} async-done(((bf16[176,2048]{1,0:T(8,128)(2,1)}), bf16[704,2048]{1,0:T(8,128)(2,1)}) %all-gather.13.cloned.1.call-update) | async-done | bytes 2883600 | tf_op jit(solution)/shard_map/all_gather | solution.py:371
  369.1 10.8 collective-permute-done.31
  463.3 10.8 collective-permute-done.43
  513.6 8.1 all-gather.17.cloned.1.call-done
  521.7 10.8 fusion.200
  538.1 8.6 convolution_convert_fusion.1
  552.0 7.9 convolution_convert_fusion.13
  586.3 8.4 collective-permute-done.54
  600.0 7.4 collective-permute-done.55
  621.0 9.7 collective-permute-done.61
  676.5 7.5 convolution_convert_fusion.3
  694.8 11.7 %reduce-scatter.9.cloned.1.call-done = bf16[176,2048]{1,0:T(8,128)(2,1)} async-done(((bf16[704,2048]{1,0:T(8,128)(2,1)}), bf16[176,2048]{1,0:T(8,128)(2,1)}) %reduce-scatter.9.cloned.1.call-update) | async-done | bytes 720912 | tf_op jit(solution)/shard_map/reduce_scatter | solution.py:480
  724.3 10.9 collective-permute-done.72
  755.4 9.9 collective-permute-done.79
  777.9 8.7 convolution_convert_fusion
  800.3 7.7 fusion.195
  811.0 10.9 collective-permute-done.83
  845.4 9.8 collective-permute-done.90
  884.9 7.5 convolution_convert_fusion.2
  927.5 33.2 %collective-permute-done.96 = bf16[256,1024]{1,0:T(8,128)(2,1)S(1)} collective-permute-done((bf16[256,1024]{1,0:T(8,128)(2,1)S(1)}, bf16[256,1024]{1,0:T(8,128)(2,1)S(1)}, u32[]{:S(2)}, u32[]{:S(2)}) %collective-permute-start.96) | collective-permute-done | bytes 524320 | tf_op jit(solution)/shard_map/ppermute | solution.py:20
  996.7 12.3 %collective-permute-done.101.refs_6_ = bf16[512,1408]{1,0:T(8,128)(2,1)} collective-permute-done((bf16[512,1408]{1,0:T(8,128)(2,1)}, bf16[512,1408]{1,0:T(8,128)(2,1)}, u32[]{:S(2)}, u32[]{:S(2)}) %collective-permute-start.101) | collective-permute-done | bytes 1441824 | tf_op jit(solution)/shard_map/ppermute | solution.py:20
  1014.1 8.3 collective-permute-done.106
  1027.6 12.6 %shard_map.371 = (f32[512,5632]{1,0:T(8,128)}, f32[512,5632]{1,0:T(8,128)}) custom-call(s32[1]{0:T(128)} %bitcast.161.ident_ref, bf16[512,1408]{1,0:T(8,128)(2,1)S(1)} %get-tuple-element.166.refs_0_, bf16[512,1408]{1,0:T(8,128)(2,1)} %collective-permute-done.107.refs_1_, bf16[512,1408]{1,0:T(8,128)(2,1)S(1)} %copy-done.14, ...), custom_call_target="tpu_custom_call" | custom-call | tf_op jit(solution)/shard_map/pallas_call | solution.py:211
  1050.9 23.6 %collective-permute-done.114 = bf16[2,144,2048]{2,1,0:T(8,128)(2,1)S(1)} collective-permute-done((bf16[2,144,2048]{2,1,0:T(8,128)(2,1)}, bf16[2,144,2048]{2,1,0:T(8,128)(2,1)S(1)}, u32[]{:S(2)}, u32[]{:S(2)}) %collective-permute-start.114) | collective-permute-done | bytes 1179680 | tf_op jit(solution)/shard_map/ppermute | solution.py:20
  1076.1 8.0 collective-permute-done.111.refs_4_
  1097.8 13.5 %collective-permute-done.115.refs_6_ = bf16[176,2048]{1,0:T(8,128)(2,1)} collective-permute-done((bf16[176,2048]{1,0:T(8,128)(2,1)S(1)}, bf16[176,2048]{1,0:T(8,128)(2,1)}, u32[]{:S(2)}, u32[]{:S(2)}) %collective-permute-start.115) | collective-permute-done | bytes 720928 | tf_op jit(solution)/shard_map/ppermute | solution.py:20
  1115.7 9.7 shard_map.372
  (955 shorter events, 694.2 us)
Async XLA Ops:
  7.2 137.0 %all-gather.7.cloned.1.call-start = ((), (), s32[]{:S(2)}) async-start(), calls=%async_computation.6 | async-start | bytes 5242880 | tf_op jit(solution)/shard_map/all_gather | solution.py:371
  19.5 165.2 %all-gather.9.cloned.1.call-start = ((), (), s32[]{:S(2)}) async-start(), calls=%async_computation.7 | async-start | bytes 5242880 | tf_op jit(solution)/shard_map/all_gather | solution.py:371
  19.7 58.7 %collective-permute-start.1 = (s32[1,2,5]{2,1,0:T(2,128)S(1)}, s32[1,2,5]{2,1,0:T(2,128)S(1)}, u32[]{:S(2)}, u32[]{:S(2)}) collective-permute-start(s32[1,2,5]{2,1,0:T(2,128)S(1)} %add_bitcast_fusion), channel_id=1, source_target_pairs={{0,2},{1,3},{2,0},{3,1},{4,6},{5,7},{6,4},{7,5},{8,10},{9,11},{10,... | collective-permute-start | bytes 128 | tf_op jit(solution)/shard_map/ppermute | solution.py:20
  22.7 61.5 %collective-permute-start.3 = (bf16[2,128,2048]{2,1,0:T(8,128)(2,1)S(1)}, bf16[2,128,2048]{2,1,0:T(8,128)(2,1)}, u32[]{:S(2)}, u32[]{:S(2)}) collective-permute-start(bf16[2,128,2048]{2,1,0:T(8,128)(2,1)S(1)} %bitcast.599), channel_id=1, source_target_pairs={{0,16},{1,17},{2,18},{3,19},{4,20},{5,21},{6,22},{7,23},{8,24},{9,... | collective-permute-start | bytes 3145736 | tf_op jit(solution)/shard_map/ppermute | solution.py:24
  27.7 62.9 %collective-permute-start.6 = (bf16[1,4,512]{2,1,0:T(4,128)(2,1)}, bf16[1,4,512]{2,1,0:T(4,128)(2,1)}, u32[]{:S(2)}, u32[]{:S(2)}) collective-permute-start(bf16[1,4,512]{2,1,0:T(4,128)(2,1)} %maximum_bitcast_fusion), channel_id=1, source_target_pairs={{0,8},{4,12},{8,0},{12,4},{1,9},{5,13},{9,1},{13,5},{2,10},{6,14},... | collective-permute-start | bytes 12296 | tf_op jit(solution)/shard_map/ppermute | solution.py:20
  31.0 41.3 %collective-permute-start.9 = (bf16[512,1024]{1,0:T(8,128)(2,1)}, bf16[512,1024]{1,0:T(8,128)(2,1)S(1)}, u32[]{:S(2)}, u32[]{:S(2)}) collective-permute-start(bf16[512,1024]{1,0:T(8,128)(2,1)} %maximum_dynamic-update-slice_fusion.1), channel_id=1, source_target_pairs={{0,16},{16,0},{1,17},{17,1},{2,18},{18,2},{3,19},{19,3},{4,20},{20... | collective-permute-start | bytes 3145736 | tf_op jit(solution)/shard_map/ppermute | solution.py:20
  33.1 89.6 %collective-permute-start.10 = (bf16[176,2048]{1,0:T(8,128)(2,1)}, bf16[176,2048]{1,0:T(8,128)(2,1)}, u32[]{:S(2)}, u32[]{:S(2)}) collective-permute-start(bf16[176,2048]{1,0:T(8,128)(2,1)} %dynamic-slice_bitcast_fusion), channel_id=1, source_target_pairs={{0,16},{16,0},{1,17},{17,1},{2,18},{18,2},{3,19},{19,3},{4,20},{20... | collective-permute-start | bytes 2162696 | tf_op jit(solution)/shard_map/ppermute | solution.py:20
  72.3 53.2 %collective-permute-start.23 = (bf16[512,1408]{1,0:T(8,128)(2,1)}, bf16[512,1408]{1,0:T(8,128)(2,1)}, u32[]{:S(2)}, u32[]{:S(2)}) collective-permute-start(bf16[512,1408]{1,0:T(8,128)(2,1)} %concatenate.341), channel_id=1, source_target_pairs={{0,16},{16,0},{1,17},{17,1},{2,18},{18,2},{3,19},{19,3},{4,20},{20... | collective-permute-start | bytes 4325384 | tf_op jit(solution)/shard_map/ppermute | solution.py:20
  74.7 232.9 %all-gather.11.cloned.1.call-start = ((), (), s32[]{:S(2)}) async-start(), calls=%async_computation.8 | async-start | bytes 7208960 | tf_op jit(solution)/shard_map/all_gather | solution.py:371
  84.3 25.6 %collective-permute-start.4 = (bf16[2,128,2048]{2,1,0:T(8,128)(2,1)S(1)}, bf16[2,128,2048]{2,1,0:T(8,128)(2,1)S(1)}, u32[]{:S(2)}, u32[]{:S(2)}) collective-permute-start(bf16[2,128,2048]{2,1,0:T(8,128)(2,1)S(1)} %broadcast_select_fusion.8), channel_id=1, source_target_pairs={{0,2},{1,3},{2,0},{3,1},{4,6},{5,7},{6,4},{7,5},{8,10},{9,11},{10,... | collective-permute-start | bytes 3145736 | tf_op jit(solution)/shard_map/ppermute | solution.py:20
  128.7 223.0 %all-gather.13.cloned.1.call-start = ((), (), s32[]{:S(2)}) async-start(), calls=%async_computation.9 | async-start | bytes 3604480 | tf_op jit(solution)/shard_map/all_gather | solution.py:371
  279.9 134.9 %all-gather.15.cloned.1.call-start = ((), (), s32[]{:S(2)}) async-start(), calls=%async_computation.10 | async-start | bytes 3604480 | tf_op jit(solution)/shard_map/all_gather | solution.py:371
  356.7 165.0 %all-gather.17.cloned.1.call-start = ((), (), s32[]{:S(2)}) async-start(), calls=%async_computation.11 | async-start | bytes 7208960 | tf_op jit(solution)/shard_map/all_gather | solution.py:371
  416.1 237.1 %reduce-scatter.7.cloned.1.call-start = ((), (), s32[]{:S(2)}) async-start(), calls=%async_computation.12 | async-start | bytes 7208960 | tf_op jit(solution)/shard_map/reduce_scatter | solution.py:480
  546.7 159.7 %reduce-scatter.9.cloned.1.call-start = ((), (), s32[]{:S(2)}) async-start(), calls=%async_computation.13 | async-start | bytes 3604480 | tf_op jit(solution)/shard_map/reduce_scatter | solution.py:480
  571.3 27.0 %collective-permute-start.68 = (bf16[256,1024]{1,0:T(8,128)(2,1)S(1)}, bf16[256,1024]{1,0:T(8,128)(2,1)S(1)}, u32[]{:S(2)}, u32[]{:S(2)}) collective-permute-start(bf16[256,1024]{1,0:T(8,128)(2,1)S(1)} %pad_maximum_fusion.45), channel_id=1, source_target_pairs={{0,16},{16,0},{1,17},{17,1},{2,18},{18,2},{3,19},{19,3},{4,20},{20... | collective-permute-start | bytes 1572872 | tf_op jit(solution)/shard_map/ppermute | solution.py:20
  635.9 152.6 %reduce-scatter.11.cloned.1.call-start = ((), (), s32[]{:S(2)}) async-start(), calls=%async_computation.14 | async-start | bytes 5242880 | tf_op jit(solution)/shard_map/reduce_scatter | solution.py:480
  711.6 191.5 %reduce-scatter.15.cloned.1.call-start = ((), (), s32[]{:S(2)}) async-start(), calls=%async_computation.16 | async-start | bytes 7208960 | tf_op jit(solution)/shard_map/reduce_scatter | solution.py:480
  795.8 213.1 %reduce-scatter.17.cloned.1.call-start = ((), (), s32[]{:S(2)}) async-start(), calls=%async_computation.17 | async-start | bytes 5242880 | tf_op jit(solution)/shard_map/reduce_scatter | solution.py:480
  864.8 27.6 %collective-permute-start.93 = (bf16[1,256,2048]{2,1,0:T(8,128)(2,1)}, bf16[1,256,2048]{2,1,0:T(8,128)(2,1)}, u32[]{:S(2)}, u32[]{:S(2)}) collective-permute-start(bf16[1,256,2048]{2,1,0:T(8,128)(2,1)} %fusion.11), channel_id=1, source_target_pairs={{0,1},{1,0},{2,3},{3,2},{4,5},{5,4},{6,7},{7,6},{8,9},{9,8},{10,11... | collective-permute-start | bytes 3145736 | tf_op jit(solution)/shard_map/ppermute | solution.py:20
  903.1 137.0 %reduce-scatter.13.cloned.1.call-start = ((), (), s32[]{:S(2)}) async-start(), calls=%async_computation.15 | async-start | bytes 3604480 | tf_op jit(solution)/shard_map/reduce_scatter | solution.py:480
  915.9 45.5 %collective-permute-start.97 = (bf16[512,1408]{1,0:T(8,128)(2,1)S(1)}, bf16[512,1408]{1,0:T(8,128)(2,1)}, u32[]{:S(2)}, u32[]{:S(2)}) collective-permute-start(bf16[512,1408]{1,0:T(8,128)(2,1)S(1)} %get-tuple-element.260), channel_id=1, source_target_pairs={{0,16},{16,0},{1,17},{17,1},{2,18},{18,2},{3,19},{19,3},{4,20},{20... | collective-permute-start | bytes 4325384 | tf_op jit(solution)/shard_map/ppermute | solution.py:20
  916.5 44.9 %collective-permute-start.98 = (bf16[512,1408]{1,0:T(8,128)(2,1)S(1)}, bf16[512,1408]{1,0:T(8,128)(2,1)S(1)}, u32[]{:S(2)}, u32[]{:S(2)}) collective-permute-start(bf16[512,1408]{1,0:T(8,128)(2,1)S(1)} %get-tuple-element.166.refs_0_), channel_id=1, source_target_pairs={{0,2},{1,3},{2,0},{3,1},{4,6},{5,7},{6,4},{7,5},{8,10},{9,11},{10,... | collective-permute-start | bytes 4325384 | tf_op jit(solution)/shard_map/ppermute | solution.py:20
  921.3 39.5 %collective-permute-start.96 = (bf16[256,1024]{1,0:T(8,128)(2,1)S(1)}, bf16[256,1024]{1,0:T(8,128)(2,1)S(1)}, u32[]{:S(2)}, u32[]{:S(2)}) collective-permute-start(bf16[256,1024]{1,0:T(8,128)(2,1)S(1)} %pad_maximum_fusion.52), channel_id=1, source_target_pairs={{0,16},{16,0},{1,17},{17,1},{2,18},{18,2},{3,19},{19,3},{4,20},{20... | collective-permute-start | bytes 1572872 | tf_op jit(solution)/shard_map/ppermute | solution.py:20
  926.2 35.0 %collective-permute-start.95 = (bf16[256,1024]{1,0:T(8,128)(2,1)S(1)}, bf16[256,1024]{1,0:T(8,128)(2,1)S(1)}, u32[]{:S(2)}, u32[]{:S(2)}) collective-permute-start(bf16[256,1024]{1,0:T(8,128)(2,1)S(1)} %slice.1042), channel_id=1, source_target_pairs={{0,2},{1,3},{2,0},{3,1},{4,6},{5,7},{6,4},{7,5},{8,10},{9,11},{10,... | collective-permute-start | bytes 1572872 | tf_op jit(solution)/shard_map/ppermute | solution.py:20
  976.4 32.5 %collective-permute-start.101 = (bf16[512,1408]{1,0:T(8,128)(2,1)}, bf16[512,1408]{1,0:T(8,128)(2,1)}, u32[]{:S(2)}, u32[]{:S(2)}) collective-permute-start(bf16[512,1408]{1,0:T(8,128)(2,1)} %collective-permute-done.97.refs_4_), channel_id=1, source_target_pairs={{0,2},{1,3},{2,0},{3,1},{4,6},{5,7},{6,4},{7,5},{8,10},{9,11},{10,... | collective-permute-start | bytes 4325384 | tf_op jit(solution)/shard_map/ppermute | solution.py:20
  986.5 27.0 %collective-permute-start.107 = (bf16[512,1408]{1,0:T(8,128)(2,1)S(1)}, bf16[512,1408]{1,0:T(8,128)(2,1)}, u32[]{:S(2)}, u32[]{:S(2)}) collective-permute-start(bf16[512,1408]{1,0:T(8,128)(2,1)S(1)} %get-tuple-element.166.refs_0_), channel_id=1, source_target_pairs={{0,1},{1,0},{2,3},{3,2},{4,5},{5,4},{6,7},{7,6},{8,9},{9,8},{10,11... | collective-permute-start | bytes 4325384 | tf_op jit(solution)/shard_map/ppermute | solution.py:20
  1013.5 26.7 %collective-permute-start.104 = (bf16[512,1024]{1,0:T(8,128)(2,1)}, bf16[512,1024]{1,0:T(8,128)(2,1)S(1)}, u32[]{:S(2)}, u32[]{:S(2)}) collective-permute-start(bf16[512,1024]{1,0:T(8,128)(2,1)} %get-tuple-element.265), channel_id=1, source_target_pairs={{0,16},{16,0},{1,17},{17,1},{2,18},{18,2},{3,19},{19,3},{4,20},{20... | collective-permute-start | bytes 3145736 | tf_op jit(solution)/shard_map/ppermute | solution.py:20
  1045.4 29.1 %collective-permute-start.114 = (bf16[2,144,2048]{2,1,0:T(8,128)(2,1)}, bf16[2,144,2048]{2,1,0:T(8,128)(2,1)S(1)}, u32[]{:S(2)}, u32[]{:S(2)}) collective-permute-start(bf16[2,144,2048]{2,1,0:T(8,128)(2,1)} %pad_maximum_fusion.11), channel_id=1, source_target_pairs={{0,16},{16,0},{1,17},{17,1},{2,18},{18,2},{3,19},{19,3},{4,20},{20... | collective-permute-start | bytes 3538952 | tf_op jit(solution)/shard_map/ppermute | solution.py:20
  1045.4 38.7 %collective-permute-start.113 = (bf16[512,1024]{1,0:T(8,128)(2,1)S(1)}, bf16[512,1024]{1,0:T(8,128)(2,1)S(1)}, u32[]{:S(2)}, u32[]{:S(2)}) collective-permute-start(bf16[512,1024]{1,0:T(8,128)(2,1)S(1)} %collective-permute-done.104.refs_4_), channel_id=1, source_target_pairs={{0,2},{1,3},{2,0},{3,1},{4,6},{5,7},{6,4},{7,5},{8,10},{9,11},{10,... | collective-permute-start | bytes 3145736 | tf_op jit(solution)/shard_map/ppermute | solution.py:20
  1048.0 36.1 %collective-permute-start.111 = (bf16[176,2048]{1,0:T(8,128)(2,1)S(1)}, bf16[176,2048]{1,0:T(8,128)(2,1)S(1)}, u32[]{:S(2)}, u32[]{:S(2)}) collective-permute-start(bf16[176,2048]{1,0:T(8,128)(2,1)S(1)} %get-tuple-element.297), channel_id=1, source_target_pairs={{0,16},{16,0},{1,17},{17,1},{2,18},{18,2},{3,19},{19,3},{4,20},{20... | collective-permute-start | bytes 2162696 | tf_op jit(solution)/shard_map/ppermute | solution.py:20
  1050.1 34.0 %collective-permute-start.112 = (bf16[176,2048]{1,0:T(8,128)(2,1)S(1)}, bf16[176,2048]{1,0:T(8,128)(2,1)}, u32[]{:S(2)}, u32[]{:S(2)}) collective-permute-start(bf16[176,2048]{1,0:T(8,128)(2,1)S(1)} %get-tuple-element.296.refs_0_), channel_id=1, source_target_pairs={{0,2},{1,3},{2,0},{3,1},{4,6},{5,7},{6,4},{7,5},{8,10},{9,11},{10,... | collective-permute-start | bytes 2162696 | tf_op jit(solution)/shard_map/ppermute | solution.py:20
  (260 other events, 2653.7 us)
Sparse Core Ops, SparseCore 0:
  19.6 83.4 all-gather.6
  105.3 79.4 all-gather.8
  186.9 105.2 all-gather.10
  294.2 57.4 all-gather.12
  356.8 58.0 all-gather.14
  416.3 105.3 all-gather.16
  546.9 100.5 reduce-scatter.6
  649.7 56.6 reduce-scatter.8
  711.7 76.7 reduce-scatter.10
  795.9 102.8 reduce-scatter.14
  903.2 76.0 reduce-scatter.16
  982.0 57.4 reduce-scatter.12
